TPU v7x, 256 devices: a whole 4x4x8 slice. The times are simulated.
256 devices in a mesh: slab: 128 (over z, y, x_lo, core), grp: 2 (over x_hi).
Axes of the slice: x: 4 (x_hi: 2, x_lo: 2; x = x_hi * 2 + x_lo), y: 4, z: 8, core: 2. Of those that a mesh axis runs over, the one named last changes fastest.
Arguments:
- base_index: int32 [3, 131072], P(None, ('slab', 'grp')), may hold values from 0 to 511, as said below
- fraction: float32 [3, 131072], P(None, ('slab', 'grp')), may hold values from 0 to 1
- charge: float32 [131072], P(('slab', 'grp')), may hold values from -4 to 4
- atom_count: int32 [256], P(('slab', 'grp')), may hold values from 256 to 512, as said below
- owner_index: int32 [32768], P(('slab', 'grp')), may hold values from 0 to 127, as said below
- neighbour: int32 [32, 32768], P(None, ('slab', 'grp')), may hold values from 0 to 767, as said below
- influence: float32 [256, 512, 512], P('grp', 'slab'), may hold values from 1 to 300
- layer_one: bfloat16 [128, 240], replicated, may hold values from -0.5 to 0.5
- bias_one: float32 [240], replicated, may hold values from -3 to 3
- layer_two: bfloat16 [240, 240], replicated, may hold values from -0.375 to 0.375
- bias_two: float32 [240], replicated, may hold values from -3 to 3
- layer_out: bfloat16 [240, 3], replicated, may hold values from -0.375 to 0.375
- bias_out: float32 [3], replicated, may hold values from -3 to 3
Outputs:
- atom_force: float32 [3, 131072], P(None, ('slab', 'grp'))
- potential: float32 [256, 512, 512], P(('slab', 'grp'))
Inputs may be any that keep to these rules, and one draw needn't show every extreme that they name: `base_index`: row 0 is an x base cell below 512, row 1 a y base cell below 512, row 2 a base plane below 1 within the device. The first 128 atoms of every device fall into 16 groups by position modulo 16; in each group the x and y bases of all devices lie within 4 cells, periodically, of a common point. `atom_count`: slots at or beyond a device's count are padding. One device uses all 512 slots and one uses half of them. `owner_index`: on each device the centroids name each of the atoms 0 .. 127 once. `neighbour`: indices into the device's extended list (first 128 atoms of the device before, its own 512 atoms, first 128 atoms of the device after). Every slot names one of the first 128 atoms of one of the three devices, in the owner's group (same position modulo 16), never the owner itself; slots may repeat.
All inputs are finite; a program needn't handle non-finite values.
Results may differ from a plain program's by a relative error of at most 0.0076.
The roundings to bfloat16 on the way count: a program that leaves them out, or rounds other values in their place, can miss the bound.
Values may be sent and summed in bfloat16 or wider, within the bound.
No kernel may reach another device: no remote copies, remote signals or barrier semaphores. Data moves between devices by JAX's collectives and lax.ppermute only.
A program may use at most 64 MiB of HBM per device.

v0:
```python
import math

import jax
import jax.numpy as jnp
from jax import lax
from jax.sharding import PartitionSpec as P

NX = 512
NY = 512
CZ = 1
NEIGH = 32


DISPLACE_MAX = 1.0
RADIUS = 4.0
CENTROID_CHARGE = -2.0
HIGHEST = lax.Precision.HIGHEST


def padded(cells, sides, width):
    for axis, dim in sides:
        count = lax.axis_size(axis)
        head = lax.slice_in_dim(cells, 0, width, axis=dim)
        tail = lax.slice_in_dim(cells, cells.shape[dim] - width, cells.shape[dim], axis=dim)
        cells = jnp.concatenate(
            [
                lax.ppermute(tail, axis, [(i, (i + 1) % count) for i in range(count)]),
                cells,
                lax.ppermute(head, axis, [((i + 1) % count, i) for i in range(count)]),
            ],
            axis=dim,
        )
    return cells


def shifted_2(value, axis, steps):
    count = lax.axis_size(axis)
    pairs = [(source, (source + steps) % count) for source in range(count)]
    return lax.ppermute(value, axis, pairs)


def spline(offset):
    size = jnp.abs(offset)
    inner = 2.0 / 3.0 - size * size + 0.5 * size * size * size
    outer = (2.0 - size) ** 3 / 6.0
    return jnp.where(size < 1.0, inner, jnp.where(size < 2.0, outer, 0.0 * size))


def spline_slope(offset):
    size = jnp.abs(offset)
    inner = (-2.0 * size + 1.5 * size * size) * jnp.sign(offset)
    outer = -0.5 * (2.0 - size) ** 2 * jnp.sign(offset)
    return jnp.where(size < 1.0, inner, jnp.where(size < 2.0, outer, 0.0 * size))


def wrap_int(values, period):
    return jnp.where(
        values >= period // 2,
        values - period,
        jnp.where(values < -(period // 2), values + period, values),
    )


def features(displace):
    scale = lax.rsqrt(
        1.0 + (displace[0] ** 2 + displace[1] ** 2 + displace[2] ** 2) / (RADIUS * RADIUS)
    )
    return jnp.stack(
        [
            scale,
            scale * displace[0] / RADIUS,
            scale * displace[1] / RADIUS,
            scale * displace[2] / RADIUS,
        ],
        axis=-1,
    )


def fitting(inputs, layer_one, bias_one, layer_two, bias_two, layer_out, bias_out):
    pre_one = (
        jnp.dot(inputs.astype(jnp.bfloat16), layer_one, preferred_element_type=jnp.float32)
        + bias_one
    )
    hidden_one = jnp.tanh(pre_one)
    pre_two = (
        jnp.dot(hidden_one.astype(jnp.bfloat16), layer_two, preferred_element_type=jnp.float32)
        + bias_two
    )
    hidden_two = jnp.tanh(pre_two) + hidden_one
    raw_out = (
        jnp.dot(hidden_two.astype(jnp.bfloat16), layer_out, preferred_element_type=jnp.float32)
        + bias_out
    )
    tanh_out = jnp.tanh(raw_out)
    return (DISPLACE_MAX * tanh_out, (hidden_one, pre_two, tanh_out))


def fitting_back(pull, saved, layer_one, layer_two, layer_out):
    hidden_one, pre_two, tanh_out = saved
    grad_out = pull * (DISPLACE_MAX * (1.0 - tanh_out * tanh_out))
    grad_two = jnp.dot(
        grad_out.astype(jnp.bfloat16), layer_out.T, preferred_element_type=jnp.float32
    )
    tanh_two = jnp.tanh(pre_two)
    grad_pre = grad_two * (1.0 - tanh_two * tanh_two)
    grad_one = (
        jnp.dot(grad_pre.astype(jnp.bfloat16), layer_two.T, preferred_element_type=jnp.float32)
        + grad_two
    )
    grad_first = grad_one * (1.0 - hidden_one * hidden_one)
    return jnp.dot(grad_first.astype(jnp.bfloat16), layer_one.T, preferred_element_type=jnp.float32)


def cas_table(row_ids, column_ids, period):
    angle = (row_ids[:, None] * column_ids[None, :] % period).astype(jnp.float32) * (
        2.0 * math.pi / period
    )
    return jnp.cos(angle) + jnp.sin(angle)


def weight_tables(base_row, frac_row, period):
    offset = (
        wrap_int(jnp.arange(period)[None, :] - base_row[:, None], period).astype(jnp.float32)
        - frac_row[:, None]
    )
    return (spline(offset), spline_slope(offset))


def depth_tables(plane_ids, base_row, frac_row):
    offset = (plane_ids[None, :] - base_row[:, None]).astype(jnp.float32) - frac_row[:, None]
    return (spline(offset), spline_slope(offset))


def spread_plane(weighted, weight_x, weight_y_b):
    scaled = (weighted[:, None] * weight_x).astype(jnp.bfloat16)
    return lax.dot_general(
        scaled, weight_y_b, (((0,), (0,)), ((), ())), preferred_element_type=jnp.float32
    )


def probe_plane(field_b, stacked_b, weight_y, slope_y, particle_rows):
    both = jnp.dot(stacked_b, field_b, preferred_element_type=jnp.float32)
    probed = jnp.sum(both[:particle_rows] * weight_y, axis=1)
    along_x = jnp.sum(both[particle_rows:] * weight_y, axis=1)
    along_y = jnp.sum(both[:particle_rows] * slope_y, axis=1)
    return (probed, along_x, along_y)


def plane_transform(field, table_x, table_y):
    inner = jnp.einsum("cxy,yv->cxv", field, table_y, precision=HIGHEST)
    return jnp.einsum("ux,cxv->cuv", table_x, inner, precision=HIGHEST)


def body(
    base_index,
    fraction,
    charge,
    atom_count,
    owner_index,
    neighbour,
    influence,
    layer_one,
    bias_one,
    layer_two,
    bias_two,
    layer_out,
    bias_out,
):
    atom_rows = base_index.shape[1]
    centroid_rows = owner_index.shape[0]
    rim_size = atom_rows // 4
    slab_size = lax.axis_size("slab")
    group_size = lax.axis_size("grp")
    group_index = lax.axis_index("grp")
    mesh_depth = CZ * slab_size * group_size
    present = (jnp.arange(atom_rows) < atom_count[0]).astype(jnp.float32)
    atom_charge = charge * present
    packed = jnp.concatenate([base_index.astype(jnp.float32), fraction], axis=0)
    rim_rows = packed[:, :rim_size]
    beside_all = padded(
        jnp.concatenate([rim_rows, rim_rows], axis=1), ((("slab", "grp"), 1),), rim_size
    )
    lift = jnp.zeros((6, 1), jnp.float32).at[2, 0].set(float(CZ))
    extended = jnp.concatenate(
        [beside_all[:, :rim_size] - lift, packed, beside_all[:, 3 * rim_size :] + lift], axis=1
    )
    owned = packed[:, owner_index]
    nearby = extended[:, neighbour]
    int_part = nearby[:3] - owned[:3, None, :]
    int_part = jnp.stack([wrap_int(int_part[0], NX), wrap_int(int_part[1], NY), int_part[2]])
    displace = int_part + (nearby[3:] - owned[3:, None, :])
    feature_rows, feature_back = jax.vjp(features, displace)
    inputs = feature_rows.transpose(1, 0, 2).reshape(centroid_rows, 4 * NEIGH)
    shifted, saved = fitting(inputs, layer_one, bias_one, layer_two, bias_two, layer_out, bias_out)
    base_all = jnp.concatenate([base_index, base_index[:, owner_index]], axis=1)
    frac_all = jnp.concatenate([fraction, owned[3:] + shifted.T], axis=1)
    charge_all = jnp.concatenate(
        [atom_charge, jnp.full((centroid_rows,), CENTROID_CHARGE, jnp.float32)]
    )
    particle_rows = atom_rows + centroid_rows
    low_shift = -((CZ + 1) // CZ)
    high_shift = (CZ + 2) // CZ
    table_x = cas_table(jnp.arange(NX), jnp.arange(NX), NX)
    table_y = cas_table(jnp.arange(NY), jnp.arange(NY), NY)
    local_rows = slab_size * CZ
    block_rows = mesh_depth // group_size
    row_ids = jnp.arange(local_rows)
    my_planes = (row_ids // CZ * group_size + group_index) * CZ + row_ids % CZ
    my_waves = group_index * block_rows + jnp.arange(block_rows)
    weight_x, slope_x = weight_tables(base_all[0], frac_all[0], NX)
    weight_y, slope_y = weight_tables(base_all[1], frac_all[1], NY)
    weight_z, slope_z = depth_tables(
        jnp.arange(low_shift * CZ, (high_shift + 1) * CZ), base_all[2], frac_all[2]
    )
    weight_y_b = weight_y.astype(jnp.bfloat16)
    stacked_b = jnp.concatenate([weight_x, slope_x], axis=0).astype(jnp.bfloat16)
    charge_z = charge_all[:, None] * weight_z
    density = jnp.zeros((CZ, NX, NY), jnp.float32)
    for shift_by in range(low_shift, high_shift + 1):
        plane_block = jnp.stack(
            [spread_plane(charge_z[:, (shift_by - low_shift) * CZ], weight_x, weight_y_b)]
        )
        if shift_by != 0:
            plane_block = shifted_2(plane_block, ("slab", "grp"), shift_by)
        density = density + plane_block
    columns = lax.all_to_all(
        plane_transform(density, table_x, table_y), "slab", split_axis=1, concat_axis=0, tiled=True
    )
    cas_rows = cas_table(jnp.arange(block_rows * lax.axis_size("grp")), my_planes, mesh_depth)
    spectrum = lax.psum_scatter(
        jnp.einsum("kz,zxy->kxy", cas_rows, columns, precision=HIGHEST),
        "grp",
        scatter_dimension=0,
        tiled=True,
    )
    weighted = spectrum * influence
    every_row = jnp.arange(mesh_depth)
    every_plane = (
        every_row % local_rows // CZ * group_size + every_row // local_rows
    ) * CZ + every_row % CZ
    cas_rows = cas_table(every_plane, my_waves, mesh_depth)
    returned_rows = lax.psum_scatter(
        jnp.einsum("zk,kxy->zxy", cas_rows, weighted, precision=HIGHEST),
        "grp",
        scatter_dimension=0,
        tiled=True,
    )
    plane_rows = lax.all_to_all(returned_rows, "slab", split_axis=0, concat_axis=1, tiled=True)
    potential = plane_transform(plane_rows, table_x, table_y) / float(NX * NY * mesh_depth)
    potential_b = potential.astype(jnp.bfloat16)
    gradient = jnp.zeros((3, particle_rows), jnp.float32)
    for shift_by in range(low_shift, high_shift + 1):
        if shift_by == 0:
            field_b = potential_b
        else:
            field_b = shifted_2(potential_b, ("slab", "grp"), -shift_by)
        column = (shift_by - low_shift) * CZ
        probed, along_x, along_y = probe_plane(
            field_b[0], stacked_b, weight_y, slope_y, particle_rows
        )
        gradient = gradient + jnp.stack(
            [
                weight_z[:, column] * along_x,
                weight_z[:, column] * along_y,
                slope_z[:, column] * probed,
            ]
        )
    pushed = charge_all[None, :] * gradient
    atom_push = pushed[:, :atom_rows]
    pull = pushed[:, atom_rows:]
    grad_inputs = fitting_back(pull.T, saved, layer_one, layer_two, layer_out)
    (grad_displace,) = feature_back(grad_inputs.reshape(centroid_rows, NEIGH, 4).transpose(1, 0, 2))
    ext_force = (
        jnp.zeros((3, atom_rows + 2 * rim_size), jnp.float32)
        .at[:, neighbour.reshape(-1)]
        .add(grad_displace.reshape(3, -1))
    )
    ext_force = ext_force.at[:, rim_size + owner_index].add(pull - jnp.sum(grad_displace, axis=1))
    returned = padded(
        jnp.concatenate([ext_force[:, :rim_size], ext_force[:, rim_size + atom_rows :]], axis=1),
        ((("slab", "grp"), 1),),
        rim_size,
    )
    local_force = ext_force[:, rim_size : rim_size + atom_rows]
    local_force = local_force.at[:, :rim_size].add(
        returned[:, :rim_size] + returned[:, 3 * rim_size :]
    )
    return (atom_push + local_force, potential)


def solution(mesh):
    return jax.shard_map(
        body,
        mesh=mesh,
        in_specs=(
            P(None, ("slab", "grp")),
            P(None, ("slab", "grp")),
            P(("slab", "grp")),
            P(("slab", "grp")),
            P(("slab", "grp")),
            P(None, ("slab", "grp")),
            P("grp", "slab", None),
            P(),
            P(),
            P(),
            P(),
            P(),
            P(),
        ),
        out_specs=(P(None, ("slab", "grp")), P(("slab", "grp"), None, None)),
        check_vma=False,
    )
```

profile of v0, /device:TPU:1, one launch (start us, length us, event | category | flops | bytes accessed | tf_op | source)
XLA Modules:
  0.0 445.1 jit_solution(9316476362020393142)
XLA Ops:
  7.2 0.7 convert_element_type.77
  7.9 0.7 fusion.169
  8.6 4.1 collective-permute-start.1
  12.7 0.7 pad_maximum_fusion.2
  13.4 0.7 fusion.144
  14.3 0.7 compare_select_fusion.6
  16.4 0.7 fusion.180
  17.1 0.8 copy.107
  17.9 0.6 gather_fusion
  18.6 0.9 add_reduce_fusion
  19.5 0.7 broadcast_add_fusion
  20.2 0.7 broadcast_add_fusion.1
  20.9 0.7 pad_maximum_fusion.1
  21.8 10.8 %gather_fusion.2 = f32[4096,6]{1,0:T(8,128)S(1)} fusion(f32[6,768]{0,1:T(8,128)S(1)} %copy.111, s32[4096]{0:T(1024)S(1)} %fusion.144), kind=kCustom, calls=%fused_computation.2 | custom fusion | bytes 212992 | tf_op jit(solution)/shard_map/gather | solution.py:188
  34.4 2.4 convolution_bitcast_fusion.5
  36.8 4.6 %collective-permute-start.3 = (f32[1,512,512]{2,1,0:T(8,128)S(1)}, f32[1,512,512]{2,1,0:T(8,128)S(1)}, u32[]{:S(2)}, u32[]{:S(2)}) collective-permute-start(f32[1,512,512]{2,1,0:T(8,128)S(1)} %convolution_bitcast_fusion.5), channel_id=1, source_target_pairs={{0,255},{1,0},{2,1},{3,2},{4,3},{5,4},{6,5},{7,6},{8,7},{9,8},{10,... | collective-permute-start | bytes 3145736 | tf_op jit(solution)/shard_map/ppermute | solution.py:39
  41.4 2.4 convolution_bitcast_fusion.6
  43.9 10.2 %collective-permute-start.2 = (f32[1,512,512]{2,1,0:T(8,128)S(1)}, f32[1,512,512]{2,1,0:T(8,128)S(1)}, u32[]{:S(2)}, u32[]{:S(2)}) collective-permute-start(f32[1,512,512]{2,1,0:T(8,128)S(1)} %convolution_bitcast_fusion.6), channel_id=1, source_target_pairs={{0,254},{1,255},{2,0},{3,1},{4,2},{5,3},{6,4},{7,5},{8,6},{9,7},{1... | collective-permute-start | bytes 3145736 | tf_op jit(solution)/shard_map/ppermute | solution.py:39
  54.1 2.4 convolution_bitcast_fusion.3
  56.6 2.4 convolution_bitcast_fusion.2
  59.1 2.4 convolution_bitcast_fusion.1
  62.1 2.4 convolution_bitcast_fusion.4
  64.5 5.5 %collective-permute-done.2 = f32[1,512,512]{2,1,0:T(8,128)S(1)} collective-permute-done((f32[1,512,512]{2,1,0:T(8,128)S(1)}, f32[1,512,512]{2,1,0:T(8,128)S(1)}, u32[]{:S(2)}, u32[]{:S(2)}) %collective-permute-start.2) | collective-permute-done | bytes 1048608 | tf_op jit(solution)/shard_map/ppermute | solution.py:39
  70.0 27.2 %collective-permute-done.4 = f32[1,512,512]{2,1,0:T(8,128)S(1)} collective-permute-done((f32[1,512,512]{2,1,0:T(8,128)S(1)}, f32[1,512,512]{2,1,0:T(8,128)S(1)}, u32[]{:S(2)}, u32[]{:S(2)}) %collective-permute-start.4) | collective-permute-done | bytes 1048608 | tf_op jit(solution)/shard_map/ppermute | solution.py:39
  97.3 14.4 %collective-permute-done.5 = f32[1,512,512]{2,1,0:T(8,128)S(1)} collective-permute-done((f32[1,512,512]{2,1,0:T(8,128)S(1)}, f32[1,512,512]{2,1,0:T(8,128)S(1)}, u32[]{:S(2)}, u32[]{:S(2)}) %collective-permute-start.5) | collective-permute-done | bytes 1048608 | tf_op jit(solution)/shard_map/ppermute | solution.py:39
  111.7 8.8 %collective-permute-done.6 = f32[1,512,512]{2,1,0:T(8,128)S(1)} collective-permute-done((f32[1,512,512]{2,1,0:T(8,128)S(1)}, f32[1,512,512]{2,1,0:T(8,128)S(1)}, u32[]{:S(2)}, u32[]{:S(2)}) %collective-permute-start.6) | collective-permute-done | bytes 1048608 | tf_op jit(solution)/shard_map/ppermute | solution.py:39
  120.5 6.2 %fusion.39 = f32[512,512]{1,0:T(8,128)S(1)} fusion(f32[1,512,512]{2,1,0:T(8,128)S(1)} %collective-permute-done.6, f32[1,512,512]{2,1,0:T(8,128)S(1)} %collective-permute-done.5, f32[1,512,512]{2,1,0:T(8,128)S(1)} %collective-permute-done.4, f32[1,512,512]{2,1,0:T(8,128)S(1)} %convolution_bitcast_fusion.4, f32[1,512,512]{2,1,0:T(8,128)S(1)} %collective-permute-done.2, ...), kind=kOutput, calls=%fused_computation.105 | convolution fusion | flops 1615855616 | bytes 7340032 | tf_op jit(solution)/shard_map/cxy,yv->cxv/dot_general | solution.py:150
  126.8 7.9 %convolution_bitcast_fusion = f32[1,512,512]{1,2,0:T(8,128)S(1)} fusion(f32[512,512]{1,0:T(8,128)S(1)} %fusion.39), kind=kOutput, calls=%fused_computation.18 | convolution fusion | flops 1614544896 | bytes 2097152 | tf_op jit(solution)/shard_map/ux,cxv->cuv/dot_general | solution.py:151
  134.6 1.9 copy.114
  136.6 8.4 %all-to-all-start = ((f32[1,512,512]{2,0,1:T(1,128)}), f32[1,512,512]{2,0,1:T(1,128)S(1)}, u32[]{:S(2)}, u32[]{:S(2)}) async-start(f32[1,512,512]{2,0,1:T(1,128)} %copy.114), calls=%async_computation | async-start | bytes 2097152 | tf_op jit(solution)/shard_map/all_to_all | solution.py:226
  145.3 28.9 %all-to-all-done = f32[1,512,512]{2,0,1:T(1,128)S(1)} async-done(((f32[1,512,512]{2,0,1:T(1,128)}), f32[1,512,512]{2,0,1:T(1,128)S(1)}, u32[]{:S(2)}, u32[]{:S(2)}) %all-to-all-start) | async-done | bytes 1048608 | tf_op jit(solution)/shard_map/all_to_all | solution.py:226
  174.2 2.6 reduce.21
  177.1 2.4 fusion.43
  179.5 2.6 copy.116
  184.1 69.8 %all-reduce.10.cloned.1.call-done = f32[256,4,512]{2,1,0:T(4,128)} async-done(((f32[256,4,512]{2,1,0:T(4,128)}), f32[256,4,512]{2,1,0:T(4,128)}) %all-reduce.10.cloned.1.call-update) | async-done | bytes 2097168
  253.8 1.8 dynamic-slice_multiply_fusion
  255.6 3.9 fusion.41
  259.6 38.0 %reduce-scatter.2.cloned.1.call-done = f32[128,4,512]{2,0,1:T(8,128)} async-done(((f32[256,4,512]{2,0,1:T(8,128)}), f32[128,4,512]{2,0,1:T(8,128)}) %reduce-scatter.2.cloned.1.call-update) | async-done | bytes 1048592 | tf_op jit(solution)/shard_map/reduce_scatter | solution.py:242
  297.6 2.9 copy.118
  300.5 11.6 %all-to-all-start.1 = ((f32[128,4,512]{2,1,0:T(4,128)}), f32[128,4,512]{2,1,0:T(4,128)S(1)}, u32[]{:S(2)}, u32[]{:S(2)}) async-start(f32[128,4,512]{2,1,0:T(4,128)} %copy.118), calls=%async_computation.2 | async-start | bytes 2097152 | tf_op jit(solution)/shard_map/all_to_all | solution.py:248
  312.1 29.1 %all-to-all-done.1 = f32[128,4,512]{2,1,0:T(4,128)S(1)} async-done(((f32[128,4,512]{2,1,0:T(4,128)}), f32[128,4,512]{2,1,0:T(4,128)S(1)}, u32[]{:S(2)}, u32[]{:S(2)}) %all-to-all-start.1) | async-done | bytes 1048608 | tf_op jit(solution)/shard_map/all_to_all | solution.py:248
  341.6 6.6 %fusion.85 = f32[512,512]{1,0:T(8,128)S(1)} fusion(f32[512,512]{1,0:T(8,128)S(1)} %reshape.591), kind=kOutput, calls=%fused_computation.140 | convolution fusion | flops 1614544896 | bytes 2097152 | tf_op jit(solution)/shard_map/cxy,yv->cxv/dot_general | solution.py:150
  348.3 8.4 %fusion.281 = (bf16[1,512,512]{1,2,0:T(8,128)(2,1)S(1)}, f32[1,512,512]{1,2,0:T(8,128)}) fusion(f32[512,512]{1,0:T(8,128)S(1)} %fusion.85), kind=kOutput, calls=%fused_computation.433 | convolution fusion | flops 1615069184 | bytes 2621440 | tf_op jit(solution)/shard_map/ux,cxv->cuv/dot_general | solution.py:151
  356.7 1.3 collective-permute-start.11
  358.0 1.8 fusion.72
  359.8 2.4 collective-permute-start.7
  362.2 1.5 collective-permute-start.8
  363.7 1.9 collective-permute-start.9
  365.6 3.8 collective-permute-start.10
  369.3 0.8 fusion.79
  370.2 10.7 %collective-permute-done.11 = bf16[1,512,512]{1,2,0:T(8,128)(2,1)S(1)} collective-permute-done((bf16[1,512,512]{1,2,0:T(8,128)(2,1)S(1)}, bf16[1,512,512]{1,2,0:T(8,128)(2,1)S(1)}, u32[]{:S(2)}, u32[]{:S(2)}) %collective-permute-start.11) | collective-permute-done | bytes 524320 | tf_op jit(solution)/shard_map/ppermute | solution.py:39
  380.9 0.8 fusion.73
  381.8 0.8 fusion.83
  382.6 1.1 collective-permute-done.8
  383.7 0.8 fusion.81
  384.6 11.6 %collective-permute-done.9 = bf16[1,512,512]{1,2,0:T(8,128)(2,1)S(1)} collective-permute-done((bf16[1,512,512]{1,2,0:T(8,128)(2,1)S(1)}, bf16[1,512,512]{1,2,0:T(8,128)(2,1)S(1)}, u32[]{:S(2)}, u32[]{:S(2)}) %collective-permute-start.9) | collective-permute-done | bytes 524320 | tf_op jit(solution)/shard_map/ppermute | solution.py:39
  396.2 0.8 fusion.77
  397.1 0.8 fusion.75
  397.9 3.7 fusion.23
  403.3 22.5 %scatter_custom_fusion = f32[3,768]{0,1:T(8,128)S(1)} fusion(s32[4096]{0:T(1024)S(1)} %bitcast.231, f32[4096,3]{1,0:T(8,128)S(1)} %bitcast.220, f32[]{:T(128)} %constant.227.clone.1), kind=kCustom, calls=%fused_computation.144 | custom fusion | flops 12288 | bytes 9220 | tf_op jit(solution)/shard_map/scatter-add | solution.py:276
  425.7 1.4 scatter_fusion
  427.2 5.5 %collective-permute-start.12 = (f32[3,128]{1,0:T(4,128)S(1)}, f32[3,128]{1,0:T(4,128)S(1)}, u32[]{:S(2)}, u32[]{:S(2)}) collective-permute-start(f32[3,128]{1,0:T(4,128)S(1)} %copy.132), channel_id=1, source_target_pairs={{0,1},{1,2},{2,3},{3,4},{4,5},{5,6},{6,7},{7,8},{8,9},{9,10},{10,1... | collective-permute-start | bytes 4616 | tf_op jit(solution)/shard_map/ppermute | solution.py:27
  433.5 2.5 copy.126
  436.8 0.7 fusion.178
  (87 shorter events, 9.2 us)
Async XLA Ops:
  7.2 26.5 %copy-start = (bf16[240,240]{1,0:T(8,128)(2,1)S(1)}, bf16[240,240]{1,0:T(8,128)(2,1)}, u32[]{:S(2)}) copy-start(bf16[240,240]{1,0:T(8,128)(2,1)} %param.26) | copy-start | bytes 345604
  8.6 10.9 %collective-permute-start.1 = (f32[6,128]{1,0:T(8,128)S(1)}, f32[6,128]{1,0:T(8,128)S(1)}, u32[]{:S(2)}, u32[]{:S(2)}) collective-permute-start(f32[6,128]{1,0:T(8,128)S(1)} %fusion.169), channel_id=1, source_target_pairs={{1,0},{2,1},{3,2},{4,3},{5,4},{6,5},{7,6},{8,7},{9,8},{10,9},{11,1... | collective-permute-start | bytes 9224 | tf_op jit(solution)/shard_map/ppermute | solution.py:29
  12.7 7.5 %collective-permute-start = (f32[6,128]{1,0:T(8,128)S(1)}, f32[6,128]{1,0:T(8,128)S(1)}, u32[]{:S(2)}, u32[]{:S(2)}) collective-permute-start(f32[6,128]{1,0:T(8,128)S(1)} %fusion.169), channel_id=1, source_target_pairs={{0,1},{1,2},{2,3},{3,4},{4,5},{5,6},{6,7},{7,8},{8,9},{9,10},{10,1... | collective-permute-start | bytes 9224 | tf_op jit(solution)/shard_map/ppermute | solution.py:27
  32.6 0.9 copy-start.2
  32.7 0.9 copy-start.6
  32.7 1.0 copy-start.7
  32.7 1.3 copy-start.5
  32.7 1.3 copy-start.8
  32.7 1.4 copy-start.3
  36.8 27.7 %collective-permute-start.3 = (f32[1,512,512]{2,1,0:T(8,128)S(1)}, f32[1,512,512]{2,1,0:T(8,128)S(1)}, u32[]{:S(2)}, u32[]{:S(2)}) collective-permute-start(f32[1,512,512]{2,1,0:T(8,128)S(1)} %convolution_bitcast_fusion.5), channel_id=1, source_target_pairs={{0,255},{1,0},{2,1},{3,2},{4,3},{5,4},{6,5},{7,6},{8,7},{9,8},{10,... | collective-permute-start | bytes 3145736 | tf_op jit(solution)/shard_map/ppermute | solution.py:39
  43.9 26.2 %collective-permute-start.2 = (f32[1,512,512]{2,1,0:T(8,128)S(1)}, f32[1,512,512]{2,1,0:T(8,128)S(1)}, u32[]{:S(2)}, u32[]{:S(2)}) collective-permute-start(f32[1,512,512]{2,1,0:T(8,128)S(1)} %convolution_bitcast_fusion.6), channel_id=1, source_target_pairs={{0,254},{1,255},{2,0},{3,1},{4,2},{5,3},{6,4},{7,5},{8,6},{9,7},{1... | collective-permute-start | bytes 3145736 | tf_op jit(solution)/shard_map/ppermute | solution.py:39
  56.5 40.8 %collective-permute-start.4 = (f32[1,512,512]{2,1,0:T(8,128)S(1)}, f32[1,512,512]{2,1,0:T(8,128)S(1)}, u32[]{:S(2)}, u32[]{:S(2)}) collective-permute-start(f32[1,512,512]{2,1,0:T(8,128)S(1)} %convolution_bitcast_fusion.3), channel_id=1, source_target_pairs={{0,1},{1,2},{2,3},{3,4},{4,5},{5,6},{6,7},{7,8},{8,9},{9,10},{10,1... | collective-permute-start | bytes 3145736 | tf_op jit(solution)/shard_map/ppermute | solution.py:39
  59.0 52.7 %collective-permute-start.5 = (f32[1,512,512]{2,1,0:T(8,128)S(1)}, f32[1,512,512]{2,1,0:T(8,128)S(1)}, u32[]{:S(2)}, u32[]{:S(2)}) collective-permute-start(f32[1,512,512]{2,1,0:T(8,128)S(1)} %convolution_bitcast_fusion.2), channel_id=1, source_target_pairs={{0,2},{1,3},{2,4},{3,5},{4,6},{5,7},{6,8},{7,9},{8,10},{9,11},{10,... | collective-permute-start | bytes 3145736 | tf_op jit(solution)/shard_map/ppermute | solution.py:39
  61.6 59.0 %collective-permute-start.6 = (f32[1,512,512]{2,1,0:T(8,128)S(1)}, f32[1,512,512]{2,1,0:T(8,128)S(1)}, u32[]{:S(2)}, u32[]{:S(2)}) collective-permute-start(f32[1,512,512]{2,1,0:T(8,128)S(1)} %convolution_bitcast_fusion.1), channel_id=1, source_target_pairs={{0,3},{1,4},{2,5},{3,6},{4,7},{5,8},{6,9},{7,10},{8,11},{9,12},{10... | collective-permute-start | bytes 3145736 | tf_op jit(solution)/shard_map/ppermute | solution.py:39
  136.6 37.6 %all-to-all-start = ((f32[1,512,512]{2,0,1:T(1,128)}), f32[1,512,512]{2,0,1:T(1,128)S(1)}, u32[]{:S(2)}, u32[]{:S(2)}) async-start(f32[1,512,512]{2,0,1:T(1,128)} %copy.114), calls=%async_computation | async-start | bytes 2097152 | tf_op jit(solution)/shard_map/all_to_all | solution.py:226
  145.0 108.8 %all-reduce.10.cloned.1.call-start = ((), (), s32[]{:S(2)}) async-start(), calls=%async_computation.4 | async-start | bytes 4194304
  182.1 0.7 copy-start.9
  182.1 71.7 %copy-start.1 = (f32[128,4,512]{2,1,0:T(4,128)S(1)}, f32[128,4,512]{2,1,0:T(4,128)}, u32[]{:S(2)}) copy-start(f32[128,4,512]{2,1,0:T(4,128)} %param.23) | copy-start | bytes 3145732
  182.2 115.5 %reduce-scatter.2.cloned.1.call-start = ((), (), s32[]{:S(2)}) async-start(), calls=%async_computation.3 | async-start | bytes 3145728 | tf_op jit(solution)/shard_map/reduce_scatter | solution.py:242
  300.5 11.6 %copy-start.4 = (s32[32,128]{1,0:T(8,128)S(1)}, s32[32,128]{1,0:T(8,128)}, u32[]{:S(2)}) copy-start(s32[32,128]{1,0:T(8,128)} %param.22) | copy-start | bytes 49156
  300.5 40.8 %all-to-all-start.1 = ((f32[128,4,512]{2,1,0:T(4,128)}), f32[128,4,512]{2,1,0:T(4,128)S(1)}, u32[]{:S(2)}, u32[]{:S(2)}) async-start(f32[128,4,512]{2,1,0:T(4,128)} %copy.118), calls=%async_computation.2 | async-start | bytes 2097152 | tf_op jit(solution)/shard_map/all_to_all | solution.py:248
  356.7 24.2 %collective-permute-start.11 = (bf16[1,512,512]{1,2,0:T(8,128)(2,1)S(1)}, bf16[1,512,512]{1,2,0:T(8,128)(2,1)S(1)}, u32[]{:S(2)}, u32[]{:S(2)}) collective-permute-start(bf16[1,512,512]{1,2,0:T(8,128)(2,1)S(1)} %get-tuple-element.145), channel_id=1, source_target_pairs={{0,253},{1,254},{2,255},{3,0},{4,1},{5,2},{6,3},{7,4},{8,5},{9,6},... | collective-permute-start | bytes 1572872 | tf_op jit(solution)/shard_map/ppermute | solution.py:39
  359.8 22.0 %collective-permute-start.7 = (bf16[1,512,512]{1,2,0:T(8,128)(2,1)S(1)}, bf16[1,512,512]{1,2,0:T(8,128)(2,1)S(1)}, u32[]{:S(2)}, u32[]{:S(2)}) collective-permute-start(bf16[1,512,512]{1,2,0:T(8,128)(2,1)S(1)} %get-tuple-element.145), channel_id=1, source_target_pairs={{0,2},{1,3},{2,4},{3,5},{4,6},{5,7},{6,8},{7,9},{8,10},{9,11},{10,... | collective-permute-start | bytes 1572872 | tf_op jit(solution)/shard_map/ppermute | solution.py:39
  362.2 21.6 %collective-permute-start.8 = (bf16[1,512,512]{1,2,0:T(8,128)(2,1)S(1)}, bf16[1,512,512]{1,2,0:T(8,128)(2,1)S(1)}, u32[]{:S(2)}, u32[]{:S(2)}) collective-permute-start(bf16[1,512,512]{1,2,0:T(8,128)(2,1)S(1)} %get-tuple-element.145), channel_id=1, source_target_pairs={{0,1},{1,2},{2,3},{3,4},{4,5},{5,6},{6,7},{7,8},{8,9},{9,10},{10,1... | collective-permute-start | bytes 1572872 | tf_op jit(solution)/shard_map/ppermute | solution.py:39
  363.7 32.6 %collective-permute-start.9 = (bf16[1,512,512]{1,2,0:T(8,128)(2,1)S(1)}, bf16[1,512,512]{1,2,0:T(8,128)(2,1)S(1)}, u32[]{:S(2)}, u32[]{:S(2)}) collective-permute-start(bf16[1,512,512]{1,2,0:T(8,128)(2,1)S(1)} %get-tuple-element.145), channel_id=1, source_target_pairs={{0,255},{1,0},{2,1},{3,2},{4,3},{5,4},{6,5},{7,6},{8,7},{9,8},{10,... | collective-permute-start | bytes 1572872 | tf_op jit(solution)/shard_map/ppermute | solution.py:39
  365.6 31.5 %collective-permute-start.10 = (bf16[1,512,512]{1,2,0:T(8,128)(2,1)S(1)}, bf16[1,512,512]{1,2,0:T(8,128)(2,1)S(1)}, u32[]{:S(2)}, u32[]{:S(2)}) collective-permute-start(bf16[1,512,512]{1,2,0:T(8,128)(2,1)S(1)} %get-tuple-element.145), channel_id=1, source_target_pairs={{0,254},{1,255},{2,0},{3,1},{4,2},{5,3},{6,4},{7,5},{8,6},{9,7},{1... | collective-permute-start | bytes 1572872 | tf_op jit(solution)/shard_map/ppermute | solution.py:39
  427.2 9.0 %collective-permute-start.12 = (f32[3,128]{1,0:T(4,128)S(1)}, f32[3,128]{1,0:T(4,128)S(1)}, u32[]{:S(2)}, u32[]{:S(2)}) collective-permute-start(f32[3,128]{1,0:T(4,128)S(1)} %copy.132), channel_id=1, source_target_pairs={{0,1},{1,2},{2,3},{3,4},{4,5},{5,6},{6,7},{7,8},{8,9},{9,10},{10,1... | collective-permute-start | bytes 4616 | tf_op jit(solution)/shard_map/ppermute | solution.py:27
  432.8 4.0 collective-permute-start.13
Sparse Core Ops, SparseCore 0:
  182.3 71.5 all-reduce.9
  259.7 37.8 reduce-scatter.1
where the time goes:
time: 453 us; the launch traced here: 445 us
  waiting for transfers between devices  246 us (54%)
  matrix products  56.4 us (12%)
  starting transfers between devices  56.3 us (12%)
  other arithmetic  43.3 us (10%)
  local copies, waits for them, and re-layouts  27 us (6%)
  between operations  16.1 us (4%)
    ppermute x10, waiting for transfers between devices, shifted_2(): return lax.ppermute(value, axis, pairs)  79.5 us
    unnamed x3, waiting for transfers between devices  69.8 us
    reduce_scatter x1, waiting for transfers between devices, body(): lax.psum_scatter(jnp.einsum('zk,kxy->zxy', cas_rows, weighted, precision=...  38 us
    all_to_all x1, waiting for transfers between devices, body(): lax.all_to_all(returned_rows, 'slab', split_axis=0, concat_axis=1, tiled=...  29.1 us
    all_to_all x1, waiting for transfers between devices, body(): lax.all_to_all(plane_transform(density, table_x, table_y), 'slab', split_...  28.9 us
    ppermute x10, starting transfers between devices, shifted_2(): return lax.ppermute(value, axis, pairs)  26.3 us
    scatter-add x1, other arithmetic, body(): ext_force = jnp.zeros((3, atom_rows + 2 * rim_size), jnp.float32).at[:, n...  22.5 us
    dot_general x2, matrix products, plane_transform(): return jnp.einsum('ux,cxv->cuv', table_x, inner, precision=HIGHEST)  16.3 us
  transfers between devices with their start and end apart: 18, of which 12 were waited for; matrix products, arithmetic and copies ran while one was open for 7% of the time, Pallas kernels for 0%

commit v1 on v0

v1 whole, which is shorter than its diff:
```python
import functools

import jax
import jax.numpy as jnp
import ml_dtypes
import numpy as np
from jax import lax
from jax.experimental import pallas as pl
from jax.experimental.pallas import tpu as pltpu
from jax.sharding import PartitionSpec as P

NX = 512
NY = 512
NZ = 256
NEIGH = 32
HID = 256
CENTROID_CHARGE = -2.0
BF = jnp.bfloat16
F32 = jnp.float32
NEAR = tuple(range(-4, 4))
ROWS = 24
MIB = 1024 * 1024


def cas_pair(row_ids, column_ids, period):
    angle = 2.0 * np.pi / period * (np.outer(row_ids, column_ids) % period)
    table = np.cos(angle) + np.sin(angle)
    high = table.astype(ml_dtypes.bfloat16)
    low = (table - high.astype(np.float64)).astype(ml_dtypes.bfloat16)
    return high, low


def spline(offset):
    size = jnp.abs(offset)
    inner = 2.0 / 3.0 - size * size + 0.5 * size * size * size
    rest = 2.0 - size
    outer = rest * rest * rest * (1.0 / 6.0)
    return jnp.where(size < 1.0, inner, jnp.where(size < 2.0, outer, 0.0))


def spline_slope(offset):
    size = jnp.abs(offset)
    sign = jnp.where(offset > 0.0, 1.0, jnp.where(offset < 0.0, -1.0, 0.0))
    inner = (-2.0 * size + 1.5 * size * size) * sign
    rest = 2.0 - size
    outer = -0.5 * rest * rest * sign
    return jnp.where(size < 1.0, inner, jnp.where(size < 2.0, outer, 0.0))


def wrapped(values):
    return jnp.where(
        values >= 256.0, values - 512.0, jnp.where(values < -256.0, values + 512.0, values)
    )


def dot(left, right):
    return jnp.dot(left, right, preferred_element_type=F32)


def split(values):
    high = values.astype(BF)
    low = (values - high.astype(F32)).astype(BF)
    return high, low


def pack_kernel(count_ref, base_ref, frac_ref, charge_ref, owner_ref, near_ref, out_ref):
    for k in range(4):
        lanes = slice(128 * k, 128 * (k + 1))
        out_ref[k : k + 1, :] = base_ref[0:1, lanes].astype(F32)
        out_ref[4 + k : 5 + k, :] = base_ref[1:2, lanes].astype(F32)
        for c in range(3):
            out_ref[8 + 4 * c + k : 9 + 4 * c + k, :] = frac_ref[c : c + 1, lanes]
        slot = lax.broadcasted_iota(jnp.int32, (1, 128), 1) + 128 * k
        out_ref[20 + k : 21 + k, :] = jnp.where(
            slot < count_ref[0], charge_ref[k : k + 1, :], 0.0
        )
    owner = owner_ref[...]
    near = near_ref[...]
    side = jnp.where(near < 128, 0, jnp.where(near < 256, 8, 16))
    code = side + (((owner >> 4) - ((near & 127) >> 4)) & 7)
    atom = lax.broadcasted_iota(jnp.int32, (128, 128), 0)
    chosen = jnp.where(atom == owner, 1.0, 0.0).astype(BF)
    out_ref[24:56, :] = lax.dot_general(
        code.astype(F32).astype(BF), chosen, (((1,), (1,)), ((), ())), preferred_element_type=F32
    )


def spread_kernel(
    p0, p1, p2, p3, p4, p5, p6, p7,
    w1_ref, b1_ref, w2_ref, b2_ref, wo_ref, bo_ref, hh_ref, hl_ref,
    out_ref, part_ref, h1_ref, t2_ref, to_ref,
    code_s, feat_s, in_s, xin_s, cell_s, wgt_s, sx_s, wy_s,
):
    pays = (p0, p1, p2, p3, p4, p5, p6, p7)
    rim = [jnp.concatenate([ref[r : r + 1, :] for ref in pays], axis=0) for r in (0, 4, 8, 12, 16)]
    for i in range(8):
        code_s[:, i, :] = pays[i][24:56, :]
    for j in range(8):
        turned = [pltpu.roll(v, 16 * j, 1) if j else v for v in rim]
        for s in (-1, 0, 1):
            cand = [pltpu.roll(v, (-s) % 8, 0) if s else v for v in turned]
            dx = wrapped(cand[0] - rim[0]) + (cand[2] - rim[2])
            dy = wrapped(cand[1] - rim[1]) + (cand[3] - rim[3])
            dz = float(s) + (cand[4] - rim[4])
            scale = lax.rsqrt(1.0 + (dx * dx + dy * dy + dz * dz) * (1.0 / 16.0))
            c = (s + 1) * 8 + j
            feat_s[c, 0] = scale
            feat_s[c, 1] = scale * dx * 0.25
            feat_s[c, 2] = scale * dy * 0.25
            feat_s[c, 3] = scale * dz * 0.25

    def choose(block, carry):
        codes = [code_s[block * 4 + m] for m in range(4)]
        held = [[jnp.zeros((8, 128), F32) for _ in range(4)] for _ in range(4)]
        for c in range(24):
            feats = [feat_s[c, f] for f in range(4)]
            for m in range(4):
                mask = codes[m] == float(c)
                for f in range(4):
                    held[m][f] = jnp.where(mask, feats[f], held[m][f])
        for m in range(4):
            for f in range(4):
                in_s[(block * 4 + m) * 4 + f] = held[m][f]
        return carry

    lax.fori_loop(0, 8, choose, 0)
    for i in range(1, 7):
        xin_s[:, (i - 1) * 128 : i * 128] = in_s[:, i, :].astype(BF)
    h1 = jnp.tanh(dot(w1_ref[...], xin_s[...]) + b1_ref[...])
    t2 = jnp.tanh(dot(w2_ref[...], h1.astype(BF)) + b2_ref[...])
    to = jnp.tanh(dot(wo_ref[...], (t2 + h1).astype(BF)) + bo_ref[...])
    h1_ref[...] = h1[:, 256:640]
    t2_ref[...] = t2[:, 256:640]
    to_ref[...] = to[:, 256:640]
    for n, i in enumerate((2, 3, 4, 5)):
        rows = slice(4 * n, 4 * n + 4)
        for c in range(4):
            part_ref[c, rows, :] = pays[i][4 * c : 4 * c + 4, :]
        part_ref[4, rows, :] = float(4 - i) - pays[i][16:20, :]
        part_ref[5, rows, :] = pays[i][20:24, :]
    for i in range(1, 7):
        row = slice(15 + i, 16 + i)
        lanes = slice((i - 1) * 128, i * 128)
        part_ref[0, row, :] = pays[i][0:1, :]
        part_ref[1, row, :] = pays[i][4:5, :]
        part_ref[2, row, :] = pays[i][8:9, :] + to[0:1, lanes]
        part_ref[3, row, :] = pays[i][12:13, :] + to[1:2, lanes]
        part_ref[4, row, :] = float(4 - i) - (pays[i][16:17, :] + to[2:3, lanes])
        part_ref[5, row, :] = jnp.full((1, 128), CENTROID_CHARGE, F32)
    part_ref[:, 22:24, :] = jnp.zeros((6, 2, 128), F32)

    charge_z = part_ref[5] * spline(part_ref[4])
    for axis in range(2):
        cells, offsets = stencil(part_ref[axis], part_ref[2 + axis])
        for k in range(4):
            value = spline(offsets[k])
            cell_s[axis * 4 + k] = cells[k]
            wgt_s[axis * 4 + k] = charge_z * value if axis == 0 else value

    def tables(row, carry):
        lanes = pl.ds(pl.multiple_of(row * 128, 128), 128)
        for axis, table in ((0, sx_s), (1, wy_s)):
            cells = [cell_s[axis * 4 + k, pl.ds(row, 1), :] for k in range(4)]
            values = [wgt_s[axis * 4 + k, pl.ds(row, 1), :] for k in range(4)]
            for part in range(16):
                here = lax.broadcasted_iota(jnp.int32, (32, 128), 0).astype(F32) + 32.0 * part
                found = jnp.zeros((32, 128), F32)
                for k in range(4):
                    found = jnp.where(here == cells[k], values[k], found)
                table[32 * part : 32 * part + 32, lanes] = found.astype(BF)
        return carry

    lax.fori_loop(0, 22, tables, 0)
    density = lax.dot_general(
        sx_s[...], wy_s[...], (((1,), (1,)), ((), ())), preferred_element_type=F32
    )
    hh, hl = hh_ref[...], hl_ref[...]
    high, low = split(density)
    inner = dot(high, hh) + dot(low, hh) + dot(high, hl)
    high, low = split(inner)
    spectrum = dot(hh, high) + dot(hh, low) + dot(hl, high)
    lower = lax.broadcasted_iota(jnp.int32, (64, 8, 128), 1) < 4
    for g in range(2):
        tile0 = spectrum[:, 256 * g : 256 * g + 128].reshape(64, 8, 128)
        tile1 = spectrum[:, 256 * g + 128 : 256 * g + 256].reshape(64, 8, 128)
        even = jnp.where(lower, tile0, pltpu.roll(tile1, 4, 1))
        odd = jnp.where(lower, pltpu.roll(tile0, 4, 1), tile1)
        out_ref[:, 0, 8 * g : 8 * g + 8, :] = even.astype(BF)
        out_ref[:, 1, 8 * g : 8 * g + 8, :] = odd.astype(BF)


def stencil(base, frac):
    whole = jnp.floor(frac)
    cells, offsets = [], []
    for k in range(4):
        step = whole + float(k - 1)
        cell = base + step
        cell = jnp.where(cell < 0.0, cell + 512.0, jnp.where(cell >= 512.0, cell - 512.0, cell))
        cells.append(cell)
        offsets.append(step - frac)
    return cells, offsets


def depth_kernel(x_ref, infl_ref, fh_ref, fl_ref, ih_ref, il_ref, out_ref, wide_s, xb_s, back_s):
    wide_s[...] = x_ref[...].astype(F32)
    for r in range(8):
        lanes = slice(128 * r, 128 * r + 128)
        xb_s[0:128, lanes] = wide_s[:, r, :].astype(BF)
        xb_s[128:256, lanes] = wide_s[:, 8 + r, :].astype(BF)
    for r in range(0, 8, 2):
        lanes = slice(128 * r, 128 * r + 256)
        xb = xb_s[:, lanes]
        spectrum = dot(fh_ref[...], xb) + dot(fl_ref[...], xb)
        weight = jnp.concatenate([infl_ref[r], infl_ref[r + 1]], axis=1)
        high, low = split(spectrum * weight)
        back = dot(ih_ref[...], high) + dot(il_ref[...], high) + dot(ih_ref[...], low)
        for t in range(2):
            column = back[:, 128 * t : 128 * t + 128]
            back_s[:, r + t, :] = column[0:128]
            back_s[:, 8 + r + t, :] = column[128:256]
    out_ref[...] = back_s[...].astype(BF)


def probe_kernel(
    y_ref, part_ref, hh_ref, hl_ref,
    pot_ref, o0, o1, o2, o3, o4, o5, o6, o7,
    r_s, field_s, cell_s, wgt_s, wx_s, vs_s, push_s,
):
    outs = (o0, o1, o2, o3, o4, o5, o6, o7)
    lower = lax.broadcasted_iota(jnp.int32, (64, 8, 128), 1) < 4
    for g in range(2):
        even = y_ref[:, 0, 8 * g : 8 * g + 8, :].astype(F32)
        odd = y_ref[:, 1, 8 * g : 8 * g + 8, :].astype(F32)
        tile0 = jnp.where(lower, even, pltpu.roll(odd, 4, 1))
        tile1 = jnp.where(lower, pltpu.roll(even, 4, 1), odd)
        r_s[:, 256 * g : 256 * g + 128] = tile0.reshape(512, 128).astype(BF)
        r_s[:, 256 * g + 128 : 256 * g + 256] = tile1.reshape(512, 128).astype(BF)
    hh, hl = hh_ref[...], hl_ref[...]
    inner = dot(hh, r_s[...]) + dot(hl, r_s[...])
    high, low = split(inner)
    potential = (dot(high, hh) + dot(low, hh) + dot(high, hl)) * (1.0 / 67108864.0)
    pot_ref[0] = potential
    field_s[...] = potential.T.astype(BF)

    for axis in range(2):
        cells, offsets = stencil(part_ref[axis], part_ref[2 + axis])
        for k in range(4):
            cell_s[axis * 4 + k] = cells[k]
            wgt_s[axis * 4 + k] = spline(offsets[k])
            wgt_s[8 + axis * 4 + k] = spline_slope(offsets[k])

    def probe(row, carry):
        row_at = pl.ds(row, 1)
        cells = [cell_s[k, row_at, :] for k in range(4)]
        values = [wgt_s[k, row_at, :] for k in range(4)]
        slopes = [wgt_s[8 + k, row_at, :] for k in range(4)]
        for part in range(16):
            here = lax.broadcasted_iota(jnp.int32, (32, 128), 0).astype(F32) + 32.0 * part
            found = jnp.zeros((32, 128), F32)
            sloped = jnp.zeros((32, 128), F32)
            for k in range(4):
                mask = here == cells[k]
                found = jnp.where(mask, values[k], found)
                sloped = jnp.where(mask, slopes[k], sloped)
            wx_s[32 * part : 32 * part + 32, 0:128] = found.astype(BF)
            wx_s[32 * part : 32 * part + 32, 128:256] = sloped.astype(BF)
        vs_s[...] = dot(field_s[...], wx_s[...])
        cells = [cell_s[4 + k, row_at, :] for k in range(4)]
        values = [wgt_s[4 + k, row_at, :] for k in range(4)]
        slopes = [wgt_s[12 + k, row_at, :] for k in range(4)]
        probed = jnp.zeros((8, 128), F32)
        along_x = jnp.zeros((8, 128), F32)
        along_y = jnp.zeros((8, 128), F32)
        for part in range(64):
            rows = slice(8 * part, 8 * part + 8)
            here = lax.broadcasted_iota(jnp.int32, (8, 128), 0).astype(F32) + 8.0 * part
            found = jnp.zeros((8, 128), F32)
            sloped = jnp.zeros((8, 128), F32)
            for k in range(4):
                mask = here == cells[k]
                found = jnp.where(mask, values[k], found)
                sloped = jnp.where(mask, slopes[k], sloped)
            value = vs_s[rows, 0:128]
            slope = vs_s[rows, 128:256]
            probed = probed + value * found
            along_x = along_x + slope * found
            along_y = along_y + value * sloped
        push_s[0, row_at, :] = jnp.sum(along_x, axis=0, keepdims=True)
        push_s[1, row_at, :] = jnp.sum(along_y, axis=0, keepdims=True)
        push_s[2, row_at, :] = jnp.sum(probed, axis=0, keepdims=True)
        return carry

    lax.fori_loop(0, 22, probe, 0)
    charge = part_ref[5]
    charge_z = charge * spline(part_ref[4])
    charge_slope = charge * spline_slope(part_ref[4])
    push = [
        push_s[0] * charge_z,
        push_s[1] * charge_z,
        push_s[2] * charge_slope,
    ]
    for i in range(8):
        outs[i][...] = jnp.zeros((ROWS, 128), F32)
        for c in range(3):
            if 2 <= i <= 5:
                outs[i][4 * c : 4 * c + 4, :] = push[c][4 * (i - 2) : 4 * (i - 2) + 4]
            for n in range(3):
                source = i - 1 + n
                if 1 <= source <= 6:
                    outs[i][12 + 3 * c + n : 13 + 3 * c + n, :] = push[c][15 + source : 16 + source]


def force_kernel(
    s0, s1, s2, s3, s4, s5, s6, s7, before_ref, own_ref, after_ref,
    h1_ref, t2_ref, to_ref, w1_ref, w2_ref, wo_ref, out_ref, gin_s,
):
    total = s0[...] + s1[...] + s2[...] + s3[...] + s4[...] + s5[...] + s6[...] + s7[...]
    pull = [
        jnp.concatenate([total[12 + 3 * c + n : 13 + 3 * c + n] for n in range(3)], axis=1)
        for c in range(3)
    ]
    to = to_ref[...]
    pulls = jnp.concatenate(pull + [jnp.zeros((5, 384), F32)], axis=0)
    g_out = pulls * (1.0 - to * to)
    g_two = dot(wo_ref[...], g_out.astype(BF))
    t2, h1 = t2_ref[...], h1_ref[...]
    g_pre = g_two * (1.0 - t2 * t2)
    g_one = dot(w2_ref[...], g_pre.astype(BF)) + g_two
    gin_s[...] = dot(w1_ref[...], (g_one * (1.0 - h1 * h1)).astype(BF))
    pays = (before_ref, own_ref, after_ref)
    turn = lax.broadcasted_iota(jnp.int32, (8, 128), 0).astype(F32)

    def rims(ref):
        return [ref[r : r + 1, :] for r in (0, 4, 8, 12, 16)]

    def rolled(row):
        return jnp.concatenate([pltpu.roll(row, 16 * j, 1) if j else row for j in range(8)], axis=0)

    own_rim = rims(own_ref)
    turned = [[rolled(row) for row in rims(ref)] for ref in pays]
    force = [total[4 * c : 4 * c + 1] for c in range(3)]
    owner_sum = [jnp.zeros((8, 128), F32) for _ in range(3)]
    for n, s in ((0, 1), (1, -1), (1, 0), (1, 1), (2, -1)):
        owner = rims(pays[n])
        cand = turned[n + s]
        dx = wrapped(cand[0] - owner[0]) + (cand[2] - owner[2])
        dy = wrapped(cand[1] - owner[1]) + (cand[3] - owner[3])
        dz = float(s) + (cand[4] - owner[4])
        scale = lax.rsqrt(1.0 + (dx * dx + dy * dy + dz * dz) * (1.0 / 16.0))
        lanes = slice(128 * n, 128 * n + 128)
        mine = turn + float(8 * (s + 1))
        cots = [jnp.zeros((8, 128), F32) for _ in range(4)]
        for m in range(NEIGH):
            mask = pays[n][24 + m : 25 + m, :] == mine
            for f in range(4):
                cots[f] = cots[f] + jnp.where(mask, gin_s[4 * m + f : 4 * m + f + 1, lanes], 0.0)
        along = cots[0] + (cots[1] * dx + cots[2] * dy + cots[3] * dz) * 0.25
        common = along * (scale * scale * scale) * (-1.0 / 16.0)
        moved = [
            common * dx + cots[1] * scale * 0.25,
            common * dy + cots[2] * scale * 0.25,
            common * dz + cots[3] * scale * 0.25,
        ]
        if n == 1:
            owner_sum = [owner_sum[c] + moved[c] for c in range(3)]
        if n + s == 1:
            for c in range(3):
                for j in range(8):
                    row = moved[c][j : j + 1]
                    force[c] = force[c] + (pltpu.roll(row, (-16 * j) % 128, 1) if j else row)
    for c in range(3):
        own = force[c] + pull[c][:, 128:256] - jnp.sum(owner_sum[c], axis=0, keepdims=True)
        out_ref[c : c + 1, 0:128] = own
        for k in range(1, 4):
            out_ref[c : c + 1, 128 * k : 128 * k + 128] = total[4 * c + k : 4 * c + k + 1]


VM = pl.BlockSpec(memory_space=pltpu.VMEM)


def call(kernel, inputs, outs, scratch=(), limit=40, first=VM, flops=0):
    return pl.pallas_call(
        kernel,
        out_shape=outs,
        in_specs=[first] + [VM] * (len(inputs) - 1),
        out_specs=jax.tree.map(lambda _: VM, outs),
        scratch_shapes=list(scratch),
        compiler_params=pltpu.CompilerParams(vmem_limit_bytes=limit * MIB),
        cost_estimate=pl.CostEstimate(flops=flops, bytes_accessed=4 * MIB, transcendentals=0),
    )(*inputs)


def shape(*dims, dtype=F32):
    return jax.ShapeDtypeStruct(dims, dtype)


def body(
    base_index,
    fraction,
    charge,
    atom_count,
    owner_index,
    neighbour,
    influence,
    layer_one,
    bias_one,
    layer_two,
    bias_two,
    layer_out,
    bias_out,
):
    both = ("slab", "grp")
    devices = 256
    group = lax.axis_index("grp")

    def from_device(value, step):
        pairs = [(source, (source - step) % devices) for source in range(devices)]
        return lax.ppermute(value, both, pairs)

    plane_high, plane_low = cas_pair(np.arange(NX), np.arange(NX), NX)
    split_z = np.concatenate([np.arange(0, NZ, 2), np.arange(1, NZ, 2)])
    fore_high, fore_low = cas_pair(np.arange(NZ), split_z, NZ)
    back_high, back_low = cas_pair(split_z, np.arange(NZ), NZ)
    hh, hl = jnp.asarray(plane_high), jnp.asarray(plane_low)

    with jax.named_scope("pack"):
        payload = call(
            pack_kernel,
            (
                atom_count,
                base_index,
                fraction,
                charge.reshape(4, 128),
                owner_index.reshape(1, 128),
                neighbour,
            ),
            shape(56, 128),
            first=pl.BlockSpec(memory_space=pltpu.SMEM),
            limit=8,
        )
    with jax.named_scope("particles_in"):
        pays = [payload if step == 0 else from_device(payload, step) for step in NEAR]

    with jax.named_scope("influence_swap"):
        kept = lax.dynamic_slice_in_dim(influence, group * 256, 256, axis=2)
        given = lax.dynamic_slice_in_dim(influence, (1 - group) * 256, 256, axis=2)
        taken = lax.ppermute(given, "grp", [(0, 1), (1, 0)])
        infl = jnp.concatenate(
            [jnp.where(group == 0, kept, taken), jnp.where(group == 0, taken, kept)], axis=0
        )
        infl = infl.reshape(NZ, 4, 2, 128).transpose(2, 1, 0, 3).reshape(8, NZ, 128)

    pad = HID - layer_one.shape[1]
    one = jnp.pad(layer_one, ((0, 0), (0, pad)))
    two = jnp.pad(layer_two, ((0, pad), (0, pad)))
    out = jnp.pad(layer_out, ((0, pad), (0, 5)))
    b1 = jnp.pad(bias_one, (0, pad)).reshape(HID, 1)
    b2 = jnp.pad(bias_two, (0, pad)).reshape(HID, 1)
    bo = jnp.pad(bias_out, (0, 5)).reshape(8, 1)

    with jax.named_scope("spread"):
        columns, part, h1, t2, to = call(
            spread_kernel,
            (*pays, one.T, b1, two.T, b2, out.T, bo, hh, hl),
            (
                shape(64, 2, 16, 128, dtype=BF),
                shape(6, ROWS, 128),
                shape(HID, 384),
                shape(HID, 384),
                shape(8, 384),
            ),
            (
                pltpu.VMEM((NEIGH, 8, 128), F32),
                pltpu.VMEM((24, 4, 8, 128), F32),
                pltpu.VMEM((128, 8, 128), F32),
                pltpu.VMEM((128, 768), BF),
                pltpu.VMEM((8, ROWS, 128), F32),
                pltpu.VMEM((8, ROWS, 128), F32),
                pltpu.VMEM((NX, 22 * 128), BF),
                pltpu.VMEM((NY, 22 * 128), BF),
            ),
            flops=4_000_000_000,
        )
    with jax.named_scope("to_columns"):
        columns = lax.all_to_all(columns.reshape(256, 8, 128), both, 0, 0, tiled=True)
    with jax.named_scope("depth"):
        rows = call(
            depth_kernel,
            (
                columns.reshape(128, 16, 128),
                infl,
                jnp.asarray(fore_high),
                jnp.asarray(fore_low),
                jnp.asarray(back_high),
                jnp.asarray(back_low),
            ),
            shape(128, 16, 128, dtype=BF),
            (
                pltpu.VMEM((128, 16, 128), F32),
                pltpu.VMEM((NZ, 1024), BF),
                pltpu.VMEM((128, 16, 128), F32),
            ),
            flops=800_000_000,
        )
    with jax.named_scope("to_planes"):
        rows = lax.all_to_all(rows.reshape(256, 8, 128), both, 0, 0, tiled=True)
    with jax.named_scope("probe"):
        potential, *pushes = call(
            probe_kernel,
            (rows.reshape(64, 2, 16, 128), part, hh, hl),
            (shape(1, NX, NY),) + (shape(ROWS, 128),) * 8,
            (
                pltpu.VMEM((NX, NY), BF),
                pltpu.VMEM((NY, NX), BF),
                pltpu.VMEM((8, ROWS, 128), F32),
                pltpu.VMEM((16, ROWS, 128), F32),
                pltpu.VMEM((NX, 256), BF),
                pltpu.VMEM((NY, 256), F32),
                pltpu.VMEM((3, ROWS, 128), F32),
            ),
            flops=5_000_000_000,
        )
    with jax.named_scope("pushes_out"):
        sums = [
            push if step == 0 else from_device(push, -step) for step, push in zip(NEAR, pushes)
        ]
    with jax.named_scope("force"):
        force = call(
            force_kernel,
            (*sums, pays[3], pays[4], pays[5], h1, t2, to, one, two, out),
            shape(3, 512),
            (pltpu.VMEM((128, 384), F32),),
            limit=16,
        )
    return force, potential


def solution(mesh):
    return jax.shard_map(
        body,
        mesh=mesh,
        in_specs=(
            P(None, ("slab", "grp")),
            P(None, ("slab", "grp")),
            P(("slab", "grp")),
            P(("slab", "grp")),
            P(("slab", "grp")),
            P(None, ("slab", "grp")),
            P("grp", "slab", None),
            P(),
            P(),
            P(),
            P(),
            P(),
            P(),
        ),
        out_specs=(P(None, ("slab", "grp")), P(("slab", "grp"), None, None)),
        check_vma=False,
    )
```

time: 453 us -> 140 us (0.31); the launches traced: 445 us -> 140 us
  waiting for transfers between devices: 246 us -> 30.2 us
  matrix products: 56.4 us -> 0 us
  other arithmetic: 43.3 us -> 1.45 us
  blocking collectives: 0 us -> 33.3 us
  Pallas kernels: 0 us -> 26.8 us
  starting transfers between devices: 56.3 us -> 33.9 us
  between operations: 16.1 us -> 1.55 us
  local copies, waits for them, and re-layouts: 27 us -> 12.7 us
    unnamed x3 -> x0, waiting for transfers between devices: 69.8 us -> none
    all_to_all x2 -> x1, waiting for transfers between devices: 58.1 us -> 0.01 us  [body(): lax.all_to_all(columns.reshape(256, 8, 128), both, 0, 0, tiled=True)]
    dot_general x23 -> x0, matrix products: 56.4 us -> none  [the longest x2 16.3 us: plane_transform(): return jnp.einsum('ux,cxv->cuv', table_x, inner, precision=HIGHEST)]
    ppermute x14 -> x15, waiting for transfers between devices: 80.1 us -> 30.2 us  [the longest x1 15.5 us: body(): taken = lax.ppermute(given, 'grp', [(0, 1), (1, 0)])]
    reduce_scatter x1 -> x0, waiting for transfers between devices: 38 us -> none  [body(): lax.psum_scatter(jnp.einsum('zk,kxy->zxy', cas_rows, weighted, precision=...]
    all_to_all x0 -> x1, blocking collectives: none -> 33.3 us  [body(): rows = lax.all_to_all(rows.reshape(256, 8, 128), both, 0, 0, tiled=True)]
    pallas_call x0 -> x5, Pallas kernels: none -> 26.8 us  [call(): pl.pallas_call(kernel, out_shape=outs, in_specs=[first] + [VM] * (len(inp...]
    scatter-add x3 -> x0, other arithmetic: 24.5 us -> none  [the longest x1 22.5 us: body(): ext_force = jnp.zeros((3, atom_rows + 2 * rim_size), jnp.float32).at[:, n...]
  transfers between devices with their start and end apart: 18 -> 16, of which waited for: 12 -> 5; matrix products, arithmetic and copies ran while one was open for 7% -> 5% of each run, Pallas kernels for 0% -> 0%
where the time goes in v1:
time: 140 us
  starting transfers between devices  33.9 us (24%)
  blocking collectives  33.3 us (24%)
  waiting for transfers between devices  30.2 us (22%)
  Pallas kernels  26.8 us (19%)
  local copies, waits for them, and re-layouts  12.7 us (9%)
  between operations  1.55 us (1%)
  other arithmetic  1.45 us (1%)
    all_to_all x1, blocking collectives, body(): rows = lax.all_to_all(rows.reshape(256, 8, 128), both, 0, 0, tiled=True)  33.3 us
    pallas_call x5, Pallas kernels, call(): pl.pallas_call(kernel, out_shape=outs, in_specs=[first] + [VM] * (len(inp...  26.8 us
    ppermute x14, starting transfers between devices, from_device(): return lax.ppermute(value, both, pairs)  25.3 us
    ppermute x1, waiting for transfers between devices, body(): taken = lax.ppermute(given, 'grp', [(0, 1), (1, 0)])  15.5 us
    ppermute x14, waiting for transfers between devices, from_device(): return lax.ppermute(value, both, pairs)  14.7 us
    unnamed x44, local copies, waits for them, and re-layouts  6.81 us
    all_to_all x1, starting transfers between devices, body(): lax.all_to_all(columns.reshape(256, 8, 128), both, 0, 0, tiled=True)  5.65 us
    reshape x2, local copies, waits for them, and re-layouts, body(): infl = infl.reshape(NZ, 4, 2, 128).transpose(2, 1, 0, 3).reshape(8, NZ, 128)  3.22 us
  transfers between devices with their start and end apart: 16, of which 5 were waited for; matrix products, arithmetic and copies ran while one was open for 5% of the time, Pallas kernels for 0%

profile of v1, /device:TPU:1, one launch (start us, length us, event | category | flops | bytes accessed | tf_op | source)
XLA Modules:
  0.0 139.9 jit_solution(8111700285502570229)
XLA Ops:
  1.3 0.7 copy-done.3
  2.0 0.7 copy-done
  2.7 0.7 copy-done.1
  3.4 0.7 copy-done.2
  4.1 0.1 pack.1.p4.own_ref
  4.2 11.1 %collective-permute-start.6 = (f32[56,128]{1,0:T(8,128)S(1)}, f32[56,128]{1,0:T(8,128)S(1)}, u32[]{:S(2)}, u32[]{:S(2)}) collective-permute-start(f32[56,128]{1,0:T(8,128)S(1)} %pack.1.p4.own_ref), channel_id=1, source_target_pairs={{0,253},{1,254},{2,255},{3,0},{4,1},{5,2},{6,3},{7,4},{8,5},{9,6},... | collective-permute-start | bytes 86024 | tf_op jit(solution)/shard_map/particles_in/ppermute | solution.py:418
  15.3 1.0 collective-permute-start.5
  16.2 2.2 %collective-permute-start.4 = (f32[56,128]{1,0:T(8,128)S(1)}, f32[56,128]{1,0:T(8,128)S(1)}, u32[]{:S(2)}, u32[]{:S(2)}) collective-permute-start(f32[56,128]{1,0:T(8,128)S(1)} %pack.1.p4.own_ref), channel_id=1, source_target_pairs={{0,255},{1,0},{2,1},{3,2},{4,3},{5,4},{6,5},{7,6},{8,7},{9,8},{10,... | collective-permute-start | bytes 86024 | tf_op jit(solution)/shard_map/particles_in/ppermute | solution.py:418
  18.4 0.8 collective-permute-start.3
  19.2 1.4 collective-permute-start.2
  20.6 0.2 copy.29
  20.8 0.1 copy.28
  20.9 0.0 copy-start.15
  20.9 0.9 copy-done.15
  21.8 0.0 copy-start.5
  21.9 0.0 collective-permute-done.6.p7
  21.9 0.1 collective-permute-start.1
  22.0 0.0 collective-permute-done.5.p6
  22.0 0.1 collective-permute-start
  22.1 0.4 copy-done.20
  22.4 0.0 copy-done.18
  22.5 0.0 copy-done.19
  22.5 0.1 copy.35.bo_ref
  22.6 0.1 copy.30.w1_ref
  22.7 0.1 copy.34.wo_ref
  22.7 0.2 copy.33.b2_ref
  22.9 0.1 copy.31.b1_ref
  23.1 0.1 copy.32.w2_ref
  23.2 0.0 collective-permute-done.4.p5.after_ref
  23.2 0.1 collective-permute-done.3.p3.before_ref
  23.2 0.0 collective-permute-done.2.p2
  23.2 7.2 %collective-permute-done.1.p1 = f32[56,128]{1,0:T(8,128)S(1)} collective-permute-done((f32[56,128]{1,0:T(8,128)S(1)}, f32[56,128]{1,0:T(8,128)S(1)}, u32[]{:S(2)}, u32[]{:S(2)}) %collective-permute-start.1) | collective-permute-done | bytes 28704 | tf_op jit(solution)/shard_map/particles_in/ppermute | solution.py:418
  30.4 0.0 collective-permute-done.p0
  30.4 10.0 %spread.1 = (bf16[64,2,16,128]{3,2,1,0:T(8,128)(2,1)}, f32[6,24,128]{2,1,0:T(8,128)S(1)}, f32[256,384]{1,0:T(8,128)S(1)}, f32[256,384]{1,0:T(8,128)S(1)}, f32[8,384]{1,0:T(8,128)S(1)}) custom-call(f32[56,128]{1,0:T(8,128)S(1)} %collective-permute-done.p0, f32[56,128]{1,0:T(8,128)S(1)} %collective-permute-done.1.p1, f32[56,128]{1,0:T(8,128)S(1)} %collective-permute-done.2.p2, ...), custom_call_target="tpu_custom_call" | custom-call | flops 4000000000 | bytes 4194304 | tf_op jit(solution)/shard_map/spread/pallas_call | solution.py:382
  40.4 0.6 copy-done.12
  41.1 5.6 %all-to-all-start = ((bf16[256,8,128]{2,1,0:T(8,128)(2,1)}), bf16[256,8,128]{2,1,0:T(8,128)(2,1)S(1)}, u32[]{:S(2)}, u32[]{:S(2)}) async-start(bf16[256,8,128]{2,1,0:T(8,128)(2,1)} %bitcast.8), calls=%async_computation | async-start | bytes 1048576 | tf_op jit(solution)/shard_map/to_columns/all_to_all | solution.py:485
  46.7 0.0 copy-start.14
  46.7 2.0 %constant_dynamic-slice_fusion = f32[128,4,256]{2,1,0:T(4,128)} fusion(f32[128,4,512]{2,1,0:T(4,128)} %param.25, s32[]{:T(128)S(6)} %select_n.20), kind=kLoop, calls=%fused_computation.3 | loop fusion | bytes 1048580 | tf_op jit(solution)/shard_map/influence_swap/dynamic_slice | solution.py:446
  48.7 2.9 %collective-permute-start.7 = (f32[128,4,256]{2,1,0:T(4,128)}, f32[128,4,256]{2,1,0:T(4,128)}, u32[]{:S(2)}, u32[]{:S(2)}) collective-permute-start(f32[128,4,256]{2,1,0:T(4,128)} %constant_dynamic-slice_fusion), channel_id=1, source_target_pairs={{0,1},{1,0},{2,3},{3,2},{4,5},{5,4},{6,7},{7,6},{8,9},{9,8},{10,11... | collective-permute-start | bytes 1572872 | tf_op jit(solution)/shard_map/influence_swap/ppermute | solution.py:447
  51.6 15.5 %collective-permute-done.7 = f32[128,4,256]{2,1,0:T(4,128)} collective-permute-done((f32[128,4,256]{2,1,0:T(4,128)}, f32[128,4,256]{2,1,0:T(4,128)}, u32[]{:S(2)}, u32[]{:S(2)}) %collective-permute-start.7) | collective-permute-done | bytes 524320 | tf_op jit(solution)/shard_map/influence_swap/ppermute | solution.py:447
  67.1 1.2 dynamic-slice_select_fusion.1
  68.3 0.2 pad_maximum_fusion
  68.6 1.7 %reshape.44 = f32[256,4,2,128]{3,2,1,0:T(2,128)} reshape(f32[256,4,256]{2,1,0:T(4,128)S(1)} %pad_maximum_fusion) | data formatting | bytes 2097152 | tf_op jit(solution)/shard_map/influence_swap/reshape | solution.py:451
  70.3 1.5 %copy.36 = f32[256,4,2,128]{3,0,1,2:T(8,128)S(1)} copy(f32[256,4,2,128]{3,2,1,0:T(2,128)} %reshape.44) | data formatting | bytes 2097152 | tf_op jit(solution)/shard_map/influence_swap/reshape | solution.py:451
  71.8 0.0 all-to-all-done
  71.8 0.0 copy-start.10
  71.8 0.9 copy-done.10
  72.7 0.9 copy-done.11
  73.6 2.6 %depth.1 = bf16[128,16,128]{2,1,0:T(8,128)(2,1)S(1)} custom-call(bf16[128,16,128]{2,1,0:T(8,128)(2,1)S(1)} %bitcast.20, f32[8,256,128]{2,1,0:T(8,128)S(1)} %bitcast.19, bf16[256,256]{1,0:T(8,128)(2,1)S(1)} %copy-done.11, bf16[256,256]{1,0:T(8,128)(2,1)S(1)} %copy-done.10, bf16[256,256]{1,0:T(8,128)(2,1)S(1)} %copy-done.9, bf16[256,256]{1,0:T(8,128)(2,1)S(1)} %copy-done.8), custom_call_target="tpu_custom_call" | custom-call | flops 800000000 | bytes 4194304 | tf_op jit(solution)/shard_map/depth/pallas_call | solution.py:382
  76.2 0.0 copy-start.7
  76.3 33.3 %all_to_all.10 = bf16[256,8,128]{2,1,0:T(8,128)(2,1)S(1)} all-to-all(bf16[256,8,128]{2,1,0:T(8,128)(2,1)S(1)} %bitcast.22), channel_id=1, replica_groups=mesh['slab'=128,'grp'=2] {'slab','grp'}, dimensions={0} | all-to-all | bytes 1048576 | tf_op jit(solution)/shard_map/to_planes/all_to_all | solution.py:506
  109.6 12.5 %probe.1 = (f32[1,512,512]{2,1,0:T(8,128)}, f32[24,128]{1,0:T(8,128)S(1)}, f32[24,128]{1,0:T(8,128)S(1)}, f32[24,128]{1,0:T(8,128)S(1)}, f32[24,128]{1,0:T(8,128...) custom-call(bf16[64,2,16,128]{3,2,1,0:T(8,128)(2,1)S(1)} %bitcast.21, ...), custom_call_target="tpu_custom_call" | custom-call | flops 5000000000 | bytes 4194304 | tf_op jit(solution)/shard_map/probe/pallas_call | solution.py:382
  122.1 0.9 collective-permute-start.8
  123.0 1.0 collective-permute-start.9
  124.0 1.4 %collective-permute-start.10 = (f32[24,128]{1,0:T(8,128)S(1)}, f32[24,128]{1,0:T(8,128)S(1)}, u32[]{:S(2)}, u32[]{:S(2)}) collective-permute-start(f32[24,128]{1,0:T(8,128)S(1)} %get-tuple-element.20), channel_id=1, source_target_pairs={{0,254},{1,255},{2,0},{3,1},{4,2},{5,3},{6,4},{7,5},{8,6},{9,7},{1... | collective-permute-start | bytes 36872 | tf_op jit(solution)/shard_map/pushes_out/ppermute | solution.py:418
  125.4 3.7 %collective-permute-start.11 = (f32[24,128]{1,0:T(8,128)S(1)}, f32[24,128]{1,0:T(8,128)S(1)}, u32[]{:S(2)}, u32[]{:S(2)}) collective-permute-start(f32[24,128]{1,0:T(8,128)S(1)} %get-tuple-element.21), channel_id=1, source_target_pairs={{0,255},{1,0},{2,1},{3,2},{4,3},{5,4},{6,5},{7,6},{8,7},{9,8},{10,... | collective-permute-start | bytes 36872 | tf_op jit(solution)/shard_map/pushes_out/ppermute | solution.py:418
  129.1 0.0 collective-permute-start.12
  129.1 0.0 collective-permute-done.8.s0
  129.1 0.7 collective-permute-start.13
  129.8 1.2 collective-permute-start.14
  130.9 2.7 %collective-permute-done.12.s5 = f32[24,128]{1,0:T(8,128)S(1)} collective-permute-done((f32[24,128]{1,0:T(8,128)S(1)}, f32[24,128]{1,0:T(8,128)S(1)}, u32[]{:S(2)}, u32[]{:S(2)}) %collective-permute-start.12) | collective-permute-done | bytes 12320 | tf_op jit(solution)/shard_map/pushes_out/ppermute | solution.py:418
  133.7 0.0 collective-permute-done.13.s6
  133.7 4.8 %collective-permute-done.14.s7 = f32[24,128]{1,0:T(8,128)S(1)} collective-permute-done((f32[24,128]{1,0:T(8,128)S(1)}, f32[24,128]{1,0:T(8,128)S(1)}, u32[]{:S(2)}, u32[]{:S(2)}) %collective-permute-start.14) | collective-permute-done | bytes 12320 | tf_op jit(solution)/shard_map/pushes_out/ppermute | solution.py:418
  138.5 1.5 %force.1 = f32[3,512]{1,0:T(4,128)} custom-call(f32[24,128]{1,0:T(8,128)S(1)} %collective-permute-done.8.s0, f32[24,128]{1,0:T(8,128)S(1)} %collective-permute-done.9.s1, f32[24,128]{1,0:T(8,128)S(1)} %collective-permute-done.10.s2, f32[24,128]{1,0:T(8,128)S(1)} %collective-permute-done.11.s3, f32[24,128]{1,0:T(8,128)S(1)} %get-tuple-element.22.s4, ...), custom_call_target="tpu_custom_call" | custom-call | bytes 4194304 | tf_op jit(solution)/shard_map/force/pallas_call | solution.py:382
  (35 shorter events, 0.1 us)
Async XLA Ops:
  1.3 0.7 copy-start.3
  1.3 0.7 copy-start.4
  2.0 0.7 copy-start
  2.7 0.7 copy-start.1
  3.4 0.7 copy-start.2
  4.1 16.5 %copy-start.17 = (bf16[240,3]{0,1:T(4,128)(2,1)S(1)}, bf16[240,3]{0,1:T(4,128)(2,1)}, u32[]{:S(2)}) copy-start(bf16[240,3]{0,1:T(4,128)(2,1)} %param.30) | copy-start | bytes 4324
  4.1 16.7 %copy-start.16 = (bf16[128,240]{0,1:T(8,128)(2,1)S(1)}, bf16[128,240]{0,1:T(8,128)(2,1)}, u32[]{:S(2)}) copy-start(bf16[128,240]{0,1:T(8,128)(2,1)} %param.26) | copy-start | bytes 184324
  4.2 17.6 %collective-permute-start.6 = (f32[56,128]{1,0:T(8,128)S(1)}, f32[56,128]{1,0:T(8,128)S(1)}, u32[]{:S(2)}, u32[]{:S(2)}) collective-permute-start(f32[56,128]{1,0:T(8,128)S(1)} %pack.1.p4.own_ref), channel_id=1, source_target_pairs={{0,253},{1,254},{2,255},{3,0},{4,1},{5,2},{6,3},{7,4},{8,5},{9,6},... | collective-permute-start | bytes 86024 | tf_op jit(solution)/shard_map/particles_in/ppermute | solution.py:418
  15.3 6.7 %collective-permute-start.5 = (f32[56,128]{1,0:T(8,128)S(1)}, f32[56,128]{1,0:T(8,128)S(1)}, u32[]{:S(2)}, u32[]{:S(2)}) collective-permute-start(f32[56,128]{1,0:T(8,128)S(1)} %pack.1.p4.own_ref), channel_id=1, source_target_pairs={{0,254},{1,255},{2,0},{3,1},{4,2},{5,3},{6,4},{7,5},{8,6},{9,7},{1... | collective-permute-start | bytes 86024 | tf_op jit(solution)/shard_map/particles_in/ppermute | solution.py:418
  16.2 6.9 %collective-permute-start.4 = (f32[56,128]{1,0:T(8,128)S(1)}, f32[56,128]{1,0:T(8,128)S(1)}, u32[]{:S(2)}, u32[]{:S(2)}) collective-permute-start(f32[56,128]{1,0:T(8,128)S(1)} %pack.1.p4.own_ref), channel_id=1, source_target_pairs={{0,255},{1,0},{2,1},{3,2},{4,3},{5,4},{6,5},{7,6},{8,7},{9,8},{10,... | collective-permute-start | bytes 86024 | tf_op jit(solution)/shard_map/particles_in/ppermute | solution.py:418
  18.4 4.8 %collective-permute-start.3 = (f32[56,128]{1,0:T(8,128)S(1)}, f32[56,128]{1,0:T(8,128)S(1)}, u32[]{:S(2)}, u32[]{:S(2)}) collective-permute-start(f32[56,128]{1,0:T(8,128)S(1)} %pack.1.p4.own_ref), channel_id=1, source_target_pairs={{0,1},{1,2},{2,3},{3,4},{4,5},{5,6},{6,7},{7,8},{8,9},{9,10},{10,1... | collective-permute-start | bytes 86024 | tf_op jit(solution)/shard_map/particles_in/ppermute | solution.py:418
  19.2 4.0 %collective-permute-start.2 = (f32[56,128]{1,0:T(8,128)S(1)}, f32[56,128]{1,0:T(8,128)S(1)}, u32[]{:S(2)}, u32[]{:S(2)}) collective-permute-start(f32[56,128]{1,0:T(8,128)S(1)} %pack.1.p4.own_ref), channel_id=1, source_target_pairs={{0,2},{1,3},{2,4},{3,5},{4,6},{5,7},{6,8},{7,9},{8,10},{9,11},{10,... | collective-permute-start | bytes 86024 | tf_op jit(solution)/shard_map/particles_in/ppermute | solution.py:418
  20.9 0.9 copy-start.15
  21.8 0.7 copy-start.20
  21.8 0.7 copy-start.18
  21.8 0.7 copy-start.19
  21.8 8.6 %copy-start.6 = (bf16[512,512]{1,0:T(8,128)(2,1)S(1)}, bf16[512,512]{1,0:T(8,128)(2,1)}, u32[]{:S(2)}) copy-start(bf16[512,512]{1,0:T(8,128)(2,1)} %constant.28.clone.hh_ref) | copy-start | bytes 1572868
  21.8 8.6 %copy-start.5 = (bf16[512,512]{1,0:T(8,128)(2,1)S(1)}, bf16[512,512]{1,0:T(8,128)(2,1)}, u32[]{:S(2)}) copy-start(bf16[512,512]{1,0:T(8,128)(2,1)} %constant.29.clone.hl_ref) | copy-start | bytes 1572868
  21.9 8.5 %collective-permute-start.1 = (f32[56,128]{1,0:T(8,128)S(1)}, f32[56,128]{1,0:T(8,128)S(1)}, u32[]{:S(2)}, u32[]{:S(2)}) collective-permute-start(f32[56,128]{1,0:T(8,128)S(1)} %pack.1.p4.own_ref), channel_id=1, source_target_pairs={{0,3},{1,4},{2,5},{3,6},{4,7},{5,8},{6,9},{7,10},{8,11},{9,12},{10... | collective-permute-start | bytes 86024 | tf_op jit(solution)/shard_map/particles_in/ppermute | solution.py:418
  22.0 8.4 %collective-permute-start = (f32[56,128]{1,0:T(8,128)S(1)}, f32[56,128]{1,0:T(8,128)S(1)}, u32[]{:S(2)}, u32[]{:S(2)}) collective-permute-start(f32[56,128]{1,0:T(8,128)S(1)} %pack.1.p4.own_ref), channel_id=1, source_target_pairs={{0,4},{1,5},{2,6},{3,7},{4,8},{5,9},{6,10},{7,11},{8,12},{9,13},{1... | collective-permute-start | bytes 86024 | tf_op jit(solution)/shard_map/particles_in/ppermute | solution.py:418
  40.4 0.6 copy-start.12
  41.1 30.7 %all-to-all-start = ((bf16[256,8,128]{2,1,0:T(8,128)(2,1)}), bf16[256,8,128]{2,1,0:T(8,128)(2,1)S(1)}, u32[]{:S(2)}, u32[]{:S(2)}) async-start(bf16[256,8,128]{2,1,0:T(8,128)(2,1)} %bitcast.8), calls=%async_computation | async-start | bytes 1048576 | tf_op jit(solution)/shard_map/to_columns/all_to_all | solution.py:485
  46.7 20.4 %copy-start.14 = (f32[128,4,512]{2,1,0:T(4,128)S(1)}, f32[128,4,512]{2,1,0:T(4,128)}, u32[]{:S(2)}) copy-start(f32[128,4,512]{2,1,0:T(4,128)} %param.25) | copy-start | bytes 3145732
  48.7 18.4 %collective-permute-start.7 = (f32[128,4,256]{2,1,0:T(4,128)}, f32[128,4,256]{2,1,0:T(4,128)}, u32[]{:S(2)}, u32[]{:S(2)}) collective-permute-start(f32[128,4,256]{2,1,0:T(4,128)} %constant_dynamic-slice_fusion), channel_id=1, source_target_pairs={{0,1},{1,0},{2,3},{3,2},{4,5},{5,4},{6,7},{7,6},{8,9},{9,8},{10,11... | collective-permute-start | bytes 1572872 | tf_op jit(solution)/shard_map/influence_swap/ppermute | solution.py:447
  70.3 1.5 %copy-start.8 = (bf16[256,256]{1,0:T(8,128)(2,1)S(1)}, bf16[256,256]{1,0:T(8,128)(2,1)}, u32[]{:S(2)}) copy-start(bf16[256,256]{1,0:T(8,128)(2,1)} %constant.33.clone.il_ref) | copy-start | bytes 393220
  70.3 1.5 %copy-start.9 = (bf16[256,256]{1,0:T(8,128)(2,1)S(1)}, bf16[256,256]{1,0:T(8,128)(2,1)}, u32[]{:S(2)}) copy-start(bf16[256,256]{1,0:T(8,128)(2,1)} %constant.32.clone.ih_ref) | copy-start | bytes 393220
  71.8 0.9 copy-start.10
  72.7 0.9 copy-start.11
  76.2 33.3 %copy-start.7 = (bf16[512,512]{1,0:T(8,128)(2,1)S(1)}, bf16[512,512]{1,0:T(8,128)(2,1)}, u32[]{:S(2)}) copy-start(bf16[512,512]{1,0:T(8,128)(2,1)} %constant.28.clone.hh_ref) | copy-start | bytes 1572868
  76.3 33.3 %copy-start.13 = (f32[6,24,128]{2,1,0:T(8,128)S(1)}, f32[6,24,128]{2,1,0:T(8,128)}, u32[]{:S(2)}) copy-start(f32[6,24,128]{2,1,0:T(8,128)} %copy-done.12) | copy-start | bytes 221188
  122.1 7.0 %collective-permute-start.8 = (f32[24,128]{1,0:T(8,128)S(1)}, f32[24,128]{1,0:T(8,128)S(1)}, u32[]{:S(2)}, u32[]{:S(2)}) collective-permute-start(f32[24,128]{1,0:T(8,128)S(1)} %get-tuple-element.18), channel_id=1, source_target_pairs={{0,252},{1,253},{2,254},{3,255},{4,0},{5,1},{6,2},{7,3},{8,4},{9,5... | collective-permute-start | bytes 36872 | tf_op jit(solution)/shard_map/pushes_out/ppermute | solution.py:418
  123.0 6.8 %collective-permute-start.9 = (f32[24,128]{1,0:T(8,128)S(1)}, f32[24,128]{1,0:T(8,128)S(1)}, u32[]{:S(2)}, u32[]{:S(2)}) collective-permute-start(f32[24,128]{1,0:T(8,128)S(1)} %get-tuple-element.19), channel_id=1, source_target_pairs={{0,253},{1,254},{2,255},{3,0},{4,1},{5,2},{6,3},{7,4},{8,5},{9,6},... | collective-permute-start | bytes 36872 | tf_op jit(solution)/shard_map/pushes_out/ppermute | solution.py:418
  124.0 6.9 %collective-permute-start.10 = (f32[24,128]{1,0:T(8,128)S(1)}, f32[24,128]{1,0:T(8,128)S(1)}, u32[]{:S(2)}, u32[]{:S(2)}) collective-permute-start(f32[24,128]{1,0:T(8,128)S(1)} %get-tuple-element.20), channel_id=1, source_target_pairs={{0,254},{1,255},{2,0},{3,1},{4,2},{5,3},{6,4},{7,5},{8,6},{9,7},{1... | collective-permute-start | bytes 36872 | tf_op jit(solution)/shard_map/pushes_out/ppermute | solution.py:418
  125.4 5.5 %collective-permute-start.11 = (f32[24,128]{1,0:T(8,128)S(1)}, f32[24,128]{1,0:T(8,128)S(1)}, u32[]{:S(2)}, u32[]{:S(2)}) collective-permute-start(f32[24,128]{1,0:T(8,128)S(1)} %get-tuple-element.21), channel_id=1, source_target_pairs={{0,255},{1,0},{2,1},{3,2},{4,3},{5,4},{6,5},{7,6},{8,7},{9,8},{10,... | collective-permute-start | bytes 36872 | tf_op jit(solution)/shard_map/pushes_out/ppermute | solution.py:418
  129.1 4.6 %collective-permute-start.12 = (f32[24,128]{1,0:T(8,128)S(1)}, f32[24,128]{1,0:T(8,128)S(1)}, u32[]{:S(2)}, u32[]{:S(2)}) collective-permute-start(f32[24,128]{1,0:T(8,128)S(1)} %get-tuple-element.23), channel_id=1, source_target_pairs={{0,1},{1,2},{2,3},{3,4},{4,5},{5,6},{6,7},{7,8},{8,9},{9,10},{10,1... | collective-permute-start | bytes 36872 | tf_op jit(solution)/shard_map/pushes_out/ppermute | solution.py:418
  129.1 4.6 %collective-permute-start.13 = (f32[24,128]{1,0:T(8,128)S(1)}, f32[24,128]{1,0:T(8,128)S(1)}, u32[]{:S(2)}, u32[]{:S(2)}) collective-permute-start(f32[24,128]{1,0:T(8,128)S(1)} %get-tuple-element.24), channel_id=1, source_target_pairs={{0,2},{1,3},{2,4},{3,5},{4,6},{5,7},{6,8},{7,9},{8,10},{9,11},{10,... | collective-permute-start | bytes 36872 | tf_op jit(solution)/shard_map/pushes_out/ppermute | solution.py:418
  129.8 8.7 %collective-permute-start.14 = (f32[24,128]{1,0:T(8,128)S(1)}, f32[24,128]{1,0:T(8,128)S(1)}, u32[]{:S(2)}, u32[]{:S(2)}) collective-permute-start(f32[24,128]{1,0:T(8,128)S(1)} %get-tuple-element.25), channel_id=1, source_target_pairs={{0,3},{1,4},{2,5},{3,6},{4,7},{5,8},{6,9},{7,10},{8,11},{9,12},{10... | collective-permute-start | bytes 36872 | tf_op jit(solution)/shard_map/pushes_out/ppermute | solution.py:418

commit v2 on v1

v2 whole, which is shorter than its diff:
```python
import functools

import jax
import jax.numpy as jnp
import ml_dtypes
import numpy as np
from jax import lax
from jax.experimental import pallas as pl
from jax.experimental.pallas import tpu as pltpu
from jax.sharding import PartitionSpec as P

NX = 512
NY = 512
NZ = 256
NEIGH = 32
HID = 240
CENTROID_CHARGE = -2.0
BF = jnp.bfloat16
F32 = jnp.float32
ROWS = 24
NEAR = tuple(range(-4, 4))
MIB = 1024 * 1024


def cas_pair(row_ids, column_ids, period):
    angle = 2.0 * np.pi / period * (np.outer(row_ids, column_ids) % period)
    table = np.cos(angle) + np.sin(angle)
    high = table.astype(ml_dtypes.bfloat16)
    low = (table - high.astype(np.float64)).astype(ml_dtypes.bfloat16)
    return high, low


def spline(offset):
    size = jnp.abs(offset)
    inner = 2.0 / 3.0 - size * size + 0.5 * size * size * size
    rest = 2.0 - size
    outer = rest * rest * rest * (1.0 / 6.0)
    return jnp.where(size < 1.0, inner, jnp.where(size < 2.0, outer, 0.0))


def spline_slope(offset):
    size = jnp.abs(offset)
    sign = jnp.where(offset > 0.0, 1.0, jnp.where(offset < 0.0, -1.0, 0.0))
    inner = (-2.0 * size + 1.5 * size * size) * sign
    rest = 2.0 - size
    outer = -0.5 * rest * rest * sign
    return jnp.where(size < 1.0, inner, jnp.where(size < 2.0, outer, 0.0))


def wrapped(values):
    return jnp.where(
        values >= 256.0, values - 512.0, jnp.where(values < -256.0, values + 512.0, values)
    )


def dot(left, right):
    return jnp.dot(left, right, preferred_element_type=F32)


def dot_first(left, right):
    return lax.dot_general(left, right, (((0,), (0,)), ((), ())), preferred_element_type=F32)


def split(values):
    high = values.astype(BF)
    low = (values - high.astype(F32)).astype(BF)
    return high, low


def fetch(pairs, sems, first=0):
    copies = [
        pltpu.make_async_copy(source, target, sems.at[first + n])
        for n, (source, target) in enumerate(pairs)
    ]
    for copy in copies:
        copy.start()
    return copies


def pack_kernel(
    count_ref, base_at, frac_at, charge_at, owner_at, near_at,
    out_ref, base_ref, frac_ref, charge_ref, owner_ref, near_ref, sems,
):
    arrays = (
        (base_at, base_ref), (frac_at, frac_ref), (charge_at, charge_ref),
        (owner_at, owner_ref), (near_at, near_ref),
    )
    copies = [pltpu.make_async_copy(a, b, sems.at[n]) for n, (a, b) in enumerate(arrays)]
    for copy in copies:
        copy.start()
    for copy in copies:
        copy.wait()
    for k in range(4):
        lanes = slice(128 * k, 128 * (k + 1))
        out_ref[k : k + 1, :] = base_ref[0:1, lanes].astype(F32)
        out_ref[4 + k : 5 + k, :] = base_ref[1:2, lanes].astype(F32)
        for c in range(3):
            out_ref[8 + 4 * c + k : 9 + 4 * c + k, :] = frac_ref[c : c + 1, lanes]
        slot = lax.broadcasted_iota(jnp.int32, (1, 128), 1) + 128 * k
        out_ref[20 + k : 21 + k, :] = jnp.where(
            slot < count_ref[0], charge_ref[k : k + 1, :], 0.0
        )
    owner = owner_ref[...]
    near = near_ref[...]
    side = jnp.where(near < 128, 0, jnp.where(near < 256, 8, 16))
    code = side + (((owner >> 4) - ((near & 127) >> 4)) & 7)
    atom = lax.broadcasted_iota(jnp.int32, (128, 128), 0)
    chosen = jnp.where(atom == owner, 1.0, 0.0).astype(BF)
    out_ref[24:56, :] = lax.dot_general(
        code.astype(F32).astype(BF), chosen, (((1,), (1,)), ((), ())), preferred_element_type=F32
    )


def atom_rows(part_ref, first, pay, plane):
    rows = slice(first, first + 4)
    for c in range(4):
        part_ref[c, rows, :] = pay(4 * c, 4 * c + 4)
    part_ref[4, rows, :] = plane - pay(16, 20)
    part_ref[5, rows, :] = pay(20, 24)


def stencil(base, frac):
    whole = jnp.floor(frac)
    cells, offsets = [], []
    for k in range(4):
        step = whole + float(k - 1)
        cell = base + step
        cell = jnp.where(cell < 0.0, cell + 512.0, jnp.where(cell >= 512.0, cell - 512.0, cell))
        cells.append(cell)
        offsets.append(step - frac)
    return cells, offsets


def densities(part_ref, cell_s, wgt_s, tables, total_s):
    charge_z = part_ref[5] * spline(part_ref[4])
    for axis in range(2):
        cells, offsets = stencil(part_ref[axis], part_ref[2 + axis])
        for k in range(4):
            value = spline(offsets[k])
            cell_s[axis * 4 + k] = cells[k]
            wgt_s[axis * 4 + k] = charge_z * value if axis == 0 else value
    place = lax.broadcasted_iota(jnp.int32, (16, 128), 0).astype(F32)
    zero = jnp.zeros((16, 128), BF)

    def fill(row, axis, table, lane):
        cells = [cell_s[axis * 4 + k, row : row + 1, :] for k in range(4)]
        blocks = [jnp.floor(cell * (1.0 / 16.0)) for cell in cells]
        here, there = jnp.zeros((16, 128), F32), jnp.zeros((16, 128), F32)
        for k in range(4):
            value = wgt_s[axis * 4 + k, row : row + 1, :]
            at = jnp.where(blocks[k] == blocks[0], cells[k] - 16.0 * blocks[k], -1.0)
            past = jnp.where(blocks[k] == blocks[0], -1.0, cells[k] - 16.0 * blocks[k])
            here = jnp.where(place == at, value, here)
            there = jnp.where(place == past, value, there)
        here, there = here.astype(BF), there.astype(BF)
        following = blocks[0] + 1.0
        following = jnp.where(following >= 32.0, 0.0, following)
        first = jnp.broadcast_to(blocks[0], (16, 128)).astype(BF)
        second = jnp.broadcast_to(following, (16, 128)).astype(BF)
        for part in range(32):
            label = jnp.full((16, 128), part, BF)
            table[16 * part : 16 * part + 16, lane : lane + 128] = jnp.where(
                first == label, here, jnp.where(second == label, there, zero)
            )

    def chunk(n):
        sx_s, wy_s = tables[n % 2]
        for m in range(4):
            fill(4 * n + m, 0, sx_s, 128 * m)
            fill(4 * n + m, 1, wy_s, 128 * m)

    def product(n):
        sx_s, wy_s = tables[n % 2]
        return lax.dot_general(
            sx_s[...], wy_s[...], (((1,), (1,)), ((), ())), preferred_element_type=F32
        )

    chunk(0)
    for n in range(6):
        if n < 5:
            chunk(n + 1)
        if n == 0:
            total_s[...] = product(n)
        elif n < 5:
            total_s[...] += product(n)
    return total_s[...] + product(5)


def spread_kernel(
    p0, p1, p2, p3, p4, p5, p6, p7,
    w1_at, b1_at, w2_at, b2_at, wo_at, bo_at, table_at,
    out_ref, part_ref, h1_ref, t2_ref, to_ref,
    code_s, feat_s, in_s, xin_s, cell_s, wgt_s, sxa_s, wya_s, sxb_s, wyb_s, total_s,
    table_ref, w1_ref, b1_ref, w2_ref, b2_ref, wo_ref, bo_ref, sems,
):
    copies = fetch(
        (
            (w1_at, w1_ref), (b1_at, b1_ref), (w2_at, w2_ref),
            (b2_at, b2_ref), (wo_at, wo_ref), (bo_at, bo_ref),
        ),
        sems,
    )
    (table_copy,) = fetch(((table_at, table_ref),), sems, 6)
    pays = (p0, p1, p2, p3, p4, p5, p6, p7)

    def pay(i, start, stop):
        return pays[i][start:stop, :]

    rim = [
        jnp.concatenate([pay(i, r, r + 1) for i in range(8)], axis=0) for r in (0, 4, 8, 12, 16)
    ]
    for i in range(8):
        code_s[:, i, :] = pay(i, 24, 56)
    for j in range(8):
        turned = [pltpu.roll(v, 16 * j, 1) if j else v for v in rim]
        for s in (-1, 0, 1):
            cand = [pltpu.roll(v, (-s) % 8, 0) if s else v for v in turned]
            dx = wrapped(cand[0] - rim[0]) + (cand[2] - rim[2])
            dy = wrapped(cand[1] - rim[1]) + (cand[3] - rim[3])
            dz = float(s) + (cand[4] - rim[4])
            scale = lax.rsqrt(1.0 + (dx * dx + dy * dy + dz * dz) * (1.0 / 16.0))
            c = (s + 1) * 8 + j
            feat_s[c, 0] = scale
            feat_s[c, 1] = scale * dx * 0.25
            feat_s[c, 2] = scale * dy * 0.25
            feat_s[c, 3] = scale * dz * 0.25

    def choose(block, carry):
        codes = [code_s[block * 4 + m] for m in range(4)]
        held = [[jnp.zeros((8, 128), F32) for _ in range(4)] for _ in range(4)]
        for c in range(24):
            feats = [feat_s[c, f] for f in range(4)]
            for m in range(4):
                mask = codes[m] == float(c)
                for f in range(4):
                    held[m][f] = jnp.where(mask, feats[f], held[m][f])
        for m in range(4):
            for f in range(4):
                in_s[(block * 4 + m) * 4 + f] = held[m][f]
        return carry

    lax.fori_loop(0, 8, choose, 0)
    for i in range(1, 7):
        xin_s[:, (i - 1) * 128 : i * 128] = in_s[:, i, :].astype(BF)
    for copy in copies:
        copy.wait()

    def column(row):
        wide = jnp.concatenate([row, jnp.zeros((1, 256 - row.shape[1]), F32)], axis=1)
        tall = jnp.broadcast_to(wide, (128, 256)).T[0 : row.shape[1]]
        return jnp.concatenate([tall] * 6, axis=1)

    h1 = jnp.tanh(dot(w1_ref[...], xin_s[...]) + column(b1_ref[...]))
    t2 = jnp.tanh(dot_first(w2_ref[...], h1.astype(BF)) + column(b2_ref[...]))
    to = jnp.tanh(dot(wo_ref[...], (t2 + h1).astype(BF)) + column(bo_ref[...]))
    h1_ref[...] = h1[:, 256:640]
    t2_ref[...] = t2[:, 256:640]
    to_ref[...] = to[:, 256:640]
    for n, i in enumerate((3, 4, 5, 2)):
        atom_rows(part_ref, 4 * n, lambda a, b, i=i: pay(i, a, b), float(4 - i))
    for i in range(1, 7):
        row = slice(15 + i, 16 + i)
        lanes = slice((i - 1) * 128, i * 128)
        part_ref[0, row, :] = pay(i, 0, 1)
        part_ref[1, row, :] = pay(i, 4, 5)
        part_ref[2, row, :] = pay(i, 8, 9) + to[0:1, lanes]
        part_ref[3, row, :] = pay(i, 12, 13) + to[1:2, lanes]
        part_ref[4, row, :] = float(4 - i) - (pay(i, 16, 17) + to[2:3, lanes])
        part_ref[5, row, :] = jnp.full((1, 128), CENTROID_CHARGE, F32)
    part_ref[:, 22:24, :] = jnp.zeros((6, 2, 128), F32)
    tables = ((sxa_s, wya_s), (sxb_s, wyb_s))
    density = densities(part_ref, cell_s, wgt_s, tables, total_s)
    table_copy.wait()
    hh, hl = table_ref[0], table_ref[1]
    high, low = split(density)
    inner = dot(high, hh) + dot(low, hh) + dot(high, hl)
    inner = inner.astype(BF)
    spectrum = dot(hh, inner) + dot(hl, inner)
    lower = lax.broadcasted_iota(jnp.int32, (64, 8, 128), 1) < 4
    for g in range(2):
        tile0 = spectrum[:, 256 * g : 256 * g + 128].reshape(64, 8, 128)
        tile1 = spectrum[:, 256 * g + 128 : 256 * g + 256].reshape(64, 8, 128)
        even = jnp.where(lower, tile0, pltpu.roll(tile1, 4, 1))
        odd = jnp.where(lower, pltpu.roll(tile0, 4, 1), tile1)
        out_ref[:, 0, 8 * g : 8 * g + 8, :] = even.astype(BF)
        out_ref[:, 1, 8 * g : 8 * g + 8, :] = odd.astype(BF)


def influence_kernel(group_ref, kept_ref, taken_ref, out_ref):
    mine = pl.multiple_of(group_ref[0] * 128, 128)
    other = pl.multiple_of(128 - mine, 128)
    for r in range(8):
        lanes = slice(128 * r, 128 * r + 128)
        at = pl.multiple_of(2 * mine + 128 * (r // 4), 128)
        out_ref[pl.ds(mine, 128), lanes] = kept_ref[:, r % 4, pl.ds(at, 128)]
        out_ref[pl.ds(other, 128), lanes] = taken_ref[:, r % 4, 128 * (r // 4) : 128 * (r // 4) + 128]


def depth_kernel(
    x_ref, infl_ref, table_at, out_ref, wide_s, xb_s, back_s, table_ref, sems
):
    (table_copy,) = fetch(((table_at, table_ref),), sems)
    wide_s[...] = x_ref[...].astype(F32)
    for r in range(8):
        lanes = slice(128 * r, 128 * r + 128)
        xb_s[0:128, lanes] = wide_s[:, r, :].astype(BF)
        xb_s[128:256, lanes] = wide_s[:, 8 + r, :].astype(BF)
    table_copy.wait()
    fh, fl, ih, il = (table_ref[n] for n in range(4))
    for r in range(0, 8, 2):
        lanes = slice(128 * r, 128 * r + 256)
        xb = xb_s[:, lanes]
        spectrum = dot(fh, xb) + dot(fl, xb)
        high, low = split(spectrum * infl_ref[:, lanes])
        back = dot(ih, high) + dot(il, high) + dot(ih, low)
        for t in range(2):
            column = back[:, 128 * t : 128 * t + 128]
            back_s[:, r + t, :] = column[0:128]
            back_s[:, 8 + r + t, :] = column[128:256]
    out_ref[...] = back_s[...].astype(BF)


def cells_of(part_ref, cell_s, wgt_s, axes):
    for n, axis in enumerate(axes):
        cells, offsets = stencil(part_ref[axis], part_ref[2 + axis])
        for k in range(4):
            cell_s[n * 4 + k] = cells[k]
            wgt_s[n * 8 + k] = spline(offsets[k])
            wgt_s[n * 8 + 4 + k] = spline_slope(offsets[k])


def lookup_kernel(axis, kind, part_ref, out_ref, cell_s, wgt_s):
    cells_of(part_ref, cell_s, wgt_s, (axis,))

    def fill(row, carry):
        row_at = pl.ds(row, 1)
        cells = [cell_s[k, row_at, :] for k in range(4)]
        values = [wgt_s[k, row_at, :] for k in range(4)]
        slopes = [wgt_s[4 + k, row_at, :] for k in range(4)]
        for part in range(16):
            here = lax.broadcasted_iota(jnp.int32, (32, 128), 0).astype(F32) + 32.0 * part
            found = jnp.zeros((32, 128), F32)
            sloped = jnp.zeros((32, 128), F32)
            for k in range(4):
                mask = here == cells[k]
                found = jnp.where(mask, values[k], found)
                sloped = jnp.where(mask, slopes[k], sloped)
            out_ref[row, 32 * part : 32 * part + 32, 0:128] = found.astype(kind)
            out_ref[row, 32 * part : 32 * part + 32, 128:256] = sloped.astype(kind)
        return carry

    lax.fori_loop(0, 22, fill, 0)


def probe_kernel(
    y_ref, part_ref, wx_at, wy_at, table_at,
    pot_at, o0, o1, o2, o3, o4, o5, o6, o7,
    r_s, field_s, va_s, vb_s, push_s, pot_s, wx_ref, wy_ref, table_ref, sems,
):
    outs = (o0, o1, o2, o3, o4, o5, o6, o7)
    half = pl.ds(0, 10), pl.ds(10, 12)
    (table_copy,) = fetch(((table_at, table_ref),), sems, 4)
    copies = fetch(
        (
            (wx_at, wx_ref),
            (wy_at.at[half[0]], wy_ref.at[half[0]]),
            (wy_at.at[half[1]], wy_ref.at[half[1]]),
        ),
        sems,
    )
    lower = lax.broadcasted_iota(jnp.int32, (64, 8, 128), 1) < 4
    for g in range(2):
        even = y_ref[:, 0, 8 * g : 8 * g + 8, :].astype(F32)
        odd = y_ref[:, 1, 8 * g : 8 * g + 8, :].astype(F32)
        tile0 = jnp.where(lower, even, pltpu.roll(odd, 4, 1))
        tile1 = jnp.where(lower, pltpu.roll(even, 4, 1), odd)
        r_s[:, 256 * g : 256 * g + 128] = tile0.reshape(512, 128).astype(BF)
        r_s[:, 256 * g + 128 : 256 * g + 256] = tile1.reshape(512, 128).astype(BF)
    table_copy.wait()
    hh, hl = table_ref[0], table_ref[1]
    inner = dot(hh, r_s[...]) + dot(hl, r_s[...])
    inner = inner.astype(BF)
    potential = (dot(inner, hh) + dot(inner, hl)) * (1.0 / 67108864.0)
    pot_s[...] = potential
    pot_copy = pltpu.make_async_copy(pot_s, pot_at.at[0], sems.at[3])
    pot_copy.start()
    field_s[...] = potential.T.astype(BF)


    def gather(row, vs_s):
        row_at = pl.ds(row, 1)
        probed = jnp.zeros((8, 128), F32)
        along_x = jnp.zeros((8, 128), F32)
        along_y = jnp.zeros((8, 128), F32)
        for part in range(64):
            rows = slice(8 * part, 8 * part + 8)
            found = wy_ref[row, rows, 0:128]
            value = vs_s[rows, 0:128]
            probed = probed + value * found
            along_x = along_x + vs_s[rows, 128:256] * found
            along_y = along_y + value * wy_ref[row, rows, 128:256]
        push_s[0, row_at, :] = jnp.sum(along_x, axis=0, keepdims=True)
        push_s[1, row_at, :] = jnp.sum(along_y, axis=0, keepdims=True)
        push_s[2, row_at, :] = jnp.sum(probed, axis=0, keepdims=True)

    def probe(pair, carry):
        row = 2 * pair
        vb_s[...] = dot(field_s[...], wx_ref[row + 1])
        gather(row, va_s)
        va_s[...] = dot(field_s[...], wx_ref[jnp.minimum(row + 2, 21)])
        gather(row + 1, vb_s)
        return carry

    copies[0].wait()
    va_s[...] = dot(field_s[...], wx_ref[0])
    copies[1].wait()
    lax.fori_loop(0, 5, probe, 0)
    copies[2].wait()
    lax.fori_loop(5, 11, probe, 0)
    pot_copy.wait()
    charge = part_ref[5]
    charge_z = charge * spline(part_ref[4])
    charge_slope = charge * spline_slope(part_ref[4])
    push = [
        push_s[0] * charge_z,
        push_s[1] * charge_z,
        push_s[2] * charge_slope,
    ]
    for i, ref in enumerate(outs):
        ref[...] = jnp.zeros((ROWS, 128), F32)
        for c in range(3):
            if 2 <= i <= 5:
                first = (12, 0, 4, 8)[i - 2]
                ref[4 * c : 4 * c + 4, :] = push[c][first : first + 4]
            for m in range(3):
                source = i - 1 + m
                if 1 <= source <= 6:
                    to = 12 + 3 * c + m
                    ref[to : to + 1, :] = push[c][15 + source : 16 + source]


def force_kernel(
    s0, s1, s2, s3, s4, s5, s6, s7, before_ref, own_ref, after_ref,
    h1_ref, t2_ref, to_ref, w1_ref, w2_ref, wo_ref, out_ref, gin_s,
):
    total = s0[...] + s1[...] + s2[...] + s3[...] + s4[...] + s5[...] + s6[...] + s7[...]
    pull = [
        jnp.concatenate([total[12 + 3 * c + n : 13 + 3 * c + n] for n in range(3)], axis=1)
        for c in range(3)
    ]
    to = to_ref[...]
    g_out = jnp.concatenate(pull, axis=0) * (1.0 - to * to)
    g_two = dot_first(wo_ref[...], g_out.astype(BF))
    t2, h1 = t2_ref[...], h1_ref[...]
    g_pre = g_two * (1.0 - t2 * t2)
    g_one = dot(w2_ref[...], g_pre.astype(BF)) + g_two
    gin_s[...] = dot_first(w1_ref[...], (g_one * (1.0 - h1 * h1)).astype(BF))
    pays = (before_ref, own_ref, after_ref)
    turn = lax.broadcasted_iota(jnp.int32, (8, 128), 0).astype(F32)

    def rims(ref):
        return [ref[r : r + 1, :] for r in (0, 4, 8, 12, 16)]

    def rolled(row):
        return jnp.concatenate([pltpu.roll(row, 16 * j, 1) if j else row for j in range(8)], axis=0)

    own_rim = rims(own_ref)
    turned = [[rolled(row) for row in rims(ref)] for ref in pays]
    force = [total[4 * c : 4 * c + 1] for c in range(3)]
    owner_sum = [jnp.zeros((8, 128), F32) for _ in range(3)]
    for n, s in ((0, 1), (1, -1), (1, 0), (1, 1), (2, -1)):
        owner = rims(pays[n])
        cand = turned[n + s]
        dx = wrapped(cand[0] - owner[0]) + (cand[2] - owner[2])
        dy = wrapped(cand[1] - owner[1]) + (cand[3] - owner[3])
        dz = float(s) + (cand[4] - owner[4])
        scale = lax.rsqrt(1.0 + (dx * dx + dy * dy + dz * dz) * (1.0 / 16.0))
        lanes = slice(128 * n, 128 * n + 128)
        mine = turn + float(8 * (s + 1))
        cots = [jnp.zeros((8, 128), F32) for _ in range(4)]
        for m in range(NEIGH):
            mask = pays[n][24 + m : 25 + m, :] == mine
            for f in range(4):
                cots[f] = cots[f] + jnp.where(mask, gin_s[4 * m + f : 4 * m + f + 1, lanes], 0.0)
        along = cots[0] + (cots[1] * dx + cots[2] * dy + cots[3] * dz) * 0.25
        common = along * (scale * scale * scale) * (-1.0 / 16.0)
        moved = [
            common * dx + cots[1] * scale * 0.25,
            common * dy + cots[2] * scale * 0.25,
            common * dz + cots[3] * scale * 0.25,
        ]
        if n == 1:
            owner_sum = [owner_sum[c] + moved[c] for c in range(3)]
        if n + s == 1:
            for c in range(3):
                for j in range(8):
                    row = moved[c][j : j + 1]
                    force[c] = force[c] + (pltpu.roll(row, (-16 * j) % 128, 1) if j else row)
    for c in range(3):
        own = force[c] + pull[c][:, 128:256] - jnp.sum(owner_sum[c], axis=0, keepdims=True)
        out_ref[c : c + 1, 0:128] = own
        for k in range(1, 4):
            out_ref[c : c + 1, 128 * k : 128 * k + 128] = total[4 * c + k : 4 * c + k + 1]


VM = pl.BlockSpec(memory_space=pltpu.VMEM)


SM = pl.BlockSpec(memory_space=pltpu.SMEM)
HB = pl.BlockSpec(memory_space=pltpu.HBM)


def call(kernel, inputs, outs, scratch=(), limit=16, spaces=None, first=None, flops=0):
    spaces = spaces or {}
    out_specs = jax.tree.map(lambda _: VM, outs)
    if first is not None:
        out_specs = (first,) + tuple(out_specs)[1:]
    return pl.pallas_call(
        kernel,
        out_shape=outs,
        in_specs=[spaces.get(n, VM) for n in range(len(inputs))],
        out_specs=out_specs,
        scratch_shapes=list(scratch),
        compiler_params=pltpu.CompilerParams(vmem_limit_bytes=limit * MIB),
        cost_estimate=pl.CostEstimate(flops=flops, bytes_accessed=4 * MIB, transcendentals=0),
    )(*inputs)


def shape(*dims, dtype=F32):
    return jax.ShapeDtypeStruct(dims, dtype)


def body(
    base_index,
    fraction,
    charge,
    atom_count,
    owner_index,
    neighbour,
    influence,
    layer_one,
    bias_one,
    layer_two,
    bias_two,
    layer_out,
    bias_out,
):
    both = ("slab", "grp")
    devices = 256
    group = lax.axis_index("grp")

    def from_device(value, step):
        pairs = [(source, (source - step) % devices) for source in range(devices)]
        return lax.ppermute(value, both, pairs)

    planes = jnp.asarray(np.stack(cas_pair(np.arange(NX), np.arange(NX), NX)))
    split_z = np.concatenate([np.arange(0, NZ, 2), np.arange(1, NZ, 2)])
    fore = cas_pair(np.arange(NZ), split_z, NZ)
    back = cas_pair(split_z, np.arange(NZ), NZ)

    with jax.named_scope("pack"):
        payload = call(
            pack_kernel,
            (
                atom_count,
                base_index,
                fraction,
                charge.reshape(4, 128),
                owner_index.reshape(1, 128),
                neighbour,
            ),
            shape(56, 128),
            (
                pltpu.VMEM((3, 512), jnp.int32),
                pltpu.VMEM((3, 512), F32),
                pltpu.VMEM((4, 128), F32),
                pltpu.VMEM((1, 128), jnp.int32),
                pltpu.VMEM((NEIGH, 128), jnp.int32),
                pltpu.SemaphoreType.DMA((5,)),
            ),
            spaces={0: SM, 1: HB, 2: HB, 3: HB, 4: HB, 5: HB},
            limit=59,
        )
    with jax.named_scope("particles_in"):
        pays = [payload if step == 0 else from_device(payload, step) for step in NEAR]
    where = group.astype(jnp.int32).reshape(1)
    with jax.named_scope("influence_swap"):
        given = lax.dynamic_slice_in_dim(influence, (1 - group) * 256, 256, axis=2).astype(BF)
        given, *pays = lax.optimization_barrier((given, *pays))
        taken = lax.ppermute(given, "grp", [(0, 1), (1, 0)])
    with jax.named_scope("spread"):
        columns, part, h1, t2, to = call(
            spread_kernel,
            (
                *pays,
                layer_one.T,
                bias_one.reshape(1, -1),
                layer_two,
                bias_two.reshape(1, -1),
                layer_out.T,
                bias_out.reshape(1, -1),
                planes,
            ),
            (
                shape(64, 2, 16, 128, dtype=BF),
                shape(6, ROWS, 128),
                shape(HID, 384),
                shape(HID, 384),
                shape(3, 384),
            ),
            (
                pltpu.VMEM((NEIGH, 8, 128), F32),
                pltpu.VMEM((24, 4, 8, 128), F32),
                pltpu.VMEM((128, 8, 128), F32),
                pltpu.VMEM((128, 768), BF),
                pltpu.VMEM((8, ROWS, 128), F32),
                pltpu.VMEM((8, ROWS, 128), F32),
                pltpu.VMEM((NX, 512), BF),
                pltpu.VMEM((NY, 512), BF),
                pltpu.VMEM((NX, 512), BF),
                pltpu.VMEM((NY, 512), BF),
                pltpu.VMEM((NX, NY), F32),
                pltpu.VMEM((2, NX, NX), BF),
                pltpu.VMEM((HID, 128), BF),
                pltpu.VMEM((1, HID), F32),
                pltpu.VMEM((HID, HID), BF),
                pltpu.VMEM((1, HID), F32),
                pltpu.VMEM((3, HID), BF),
                pltpu.VMEM((1, 3), F32),
                pltpu.SemaphoreType.DMA((7,)),
            ),
            limit=58,
            spaces={n: HB for n in range(8, 15)},
            flops=4_000_000_000,
        )
    columns, taken = lax.optimization_barrier((columns, taken))
    with jax.named_scope("to_columns"):
        columns = lax.all_to_all(columns.reshape(256, 8, 128), both, 0, 0, tiled=True)
    def lookup(axis, kind):
        return call(
            lambda *refs: lookup_kernel(axis, kind, *refs),
            (part,),
            shape(22, NX, 256, dtype=kind),
            (pltpu.VMEM((4, ROWS, 128), F32), pltpu.VMEM((8, ROWS, 128), F32)),
            limit=58,
            flops=4_000_000_000,
        )

    with jax.named_scope("lookup_x"):
        weights_x = lookup(0, BF)
    with jax.named_scope("influence"):
        infl = call(
            influence_kernel,
            (where, influence, taken.astype(F32)),
            shape(NZ, 1024),
            spaces={0: SM},
        )
    with jax.named_scope("depth"):
        rows = call(
            depth_kernel,
            (
                columns.reshape(128, 16, 128),
                infl,
                jnp.asarray(np.stack(fore + back)),
            ),
            shape(128, 16, 128, dtype=BF),
            (
                pltpu.VMEM((128, 16, 128), F32),
                pltpu.VMEM((NZ, 1024), BF),
                pltpu.VMEM((128, 16, 128), F32),
                pltpu.VMEM((4, NZ, NZ), BF),
                pltpu.SemaphoreType.DMA((1,)),
            ),
            spaces={2: HB},
            limit=50,
            flops=800_000_000,
        )
    with jax.named_scope("to_planes"):
        rows = lax.all_to_all(rows.reshape(256, 8, 128), both, 0, 0, tiled=True)
    with jax.named_scope("lookup_y"):
        weights_y = lookup(1, F32)
    with jax.named_scope("probe"):
        potential, *pushes = call(
            probe_kernel,
            (rows.reshape(64, 2, 16, 128), part, weights_x, weights_y, planes),
            (shape(1, NX, NY),) + (shape(ROWS, 128),) * 8,
            (
                pltpu.VMEM((NX, NY), BF),
                pltpu.VMEM((NY, NX), BF),
                pltpu.VMEM((NY, 256), F32),
                pltpu.VMEM((NY, 256), F32),
                pltpu.VMEM((3, ROWS, 128), F32),
                pltpu.VMEM((NX, NY), F32),
                pltpu.VMEM((22, NX, 256), BF),
                pltpu.VMEM((22, NY, 256), F32),
                pltpu.VMEM((2, NX, NX), BF),
                pltpu.SemaphoreType.DMA((5,)),
            ),
            first=HB,
            limit=52,
            spaces={2: HB, 3: HB, 4: HB},
            flops=5_000_000_000,
        )
    with jax.named_scope("pushes_out"):
        sums = [
            push if step == 0 else from_device(push, -step) for step, push in zip(NEAR, pushes)
        ]
    with jax.named_scope("force"):
        force = call(
            force_kernel,
            (*sums, pays[3], payload, pays[5], h1, t2, to, layer_one.T, layer_two, layer_out.T),
            shape(3, 512),
            (pltpu.VMEM((128, 384), F32),),
            limit=16,
        )
    return force, potential


def solution(mesh):
    return jax.shard_map(
        body,
        mesh=mesh,
        in_specs=(
            P(None, ("slab", "grp")),
            P(None, ("slab", "grp")),
            P(("slab", "grp")),
            P(("slab", "grp")),
            P(("slab", "grp")),
            P(None, ("slab", "grp")),
            P("grp", "slab", None),
            P(),
            P(),
            P(),
            P(),
            P(),
            P(),
        ),
        out_specs=(P(None, ("slab", "grp")), P(("slab", "grp"), None, None)),
        check_vma=False,
    )
```

time: 140 us -> 124 us (0.89)
  blocking collectives: 33.3 us -> 0 us
  Pallas kernels: 26.8 us -> 40 us
  local copies, waits for them, and re-layouts: 12.7 us -> 1.23 us
  waiting for transfers between devices: 30.2 us -> 41.1 us
  starting transfers between devices: 33.9 us -> 39.2 us
    all_to_all x1 -> x0, blocking collectives: 33.3 us -> none  [body(): rows = lax.all_to_all(rows.reshape(256, 8, 128), both, 0, 0, tiled=True)]
    all_to_all x1, waiting for transfers between devices: 0.01 us -> 19.6 us  [body(): lax.all_to_all(columns.reshape(256, 8, 128), both, 0, 0, tiled=True)]
    ppermute x1, waiting for transfers between devices: 15.5 us -> 0.01 us  [body(): taken = lax.ppermute(given, 'grp', [(0, 1), (1, 0)])]
    pallas_call x5 -> x8, Pallas kernels: 26.8 us -> 40 us  [call(): pl.pallas_call(kernel, out_shape=outs, in_specs=[spaces.get(n, VM) for n...]
    unnamed x44 -> x40, local copies, waits for them, and re-layouts: 6.81 us -> 0.09 us
    all_to_all x0 -> x1, starting transfers between devices: none -> 6.17 us  [body(): rows = lax.all_to_all(rows.reshape(256, 8, 128), both, 0, 0, tiled=True)]
    all_to_all x0 -> x1, waiting for transfers between devices: none -> 6.01 us  [body(): rows = lax.all_to_all(rows.reshape(256, 8, 128), both, 0, 0, tiled=True)]
    reshape x6 -> x0, local copies, waits for them, and re-layouts: 3.6 us -> none  [the longest x2 3.22 us: body(): infl = infl.reshape(NZ, 4, 2, 128).transpose(2, 1, 0, 3).reshape(8, NZ, 128)]
  transfers between devices with their start and end apart: 16 -> 17, of which waited for: 5 -> 6; matrix products, arithmetic and copies ran while one was open for 5% -> 1% of each run, Pallas kernels for 0% -> 19%
where the time goes in v2:
time: 124 us; the launch traced here: 123 us
  waiting for transfers between devices  41.1 us (33%)
  Pallas kernels  40 us (32%)
  starting transfers between devices  39.2 us (32%)
  between operations  1.69 us (1%)
    pallas_call x8, Pallas kernels, call(): pl.pallas_call(kernel, out_shape=outs, in_specs=[spaces.get(n, VM) for n...  40 us
    ppermute x14, starting transfers between devices, from_device(): return lax.ppermute(value, both, pairs)  25.6 us
    all_to_all x1, waiting for transfers between devices, body(): lax.all_to_all(columns.reshape(256, 8, 128), both, 0, 0, tiled=True)  19.6 us
    ppermute x14, waiting for transfers between devices, from_device(): return lax.ppermute(value, both, pairs)  15.5 us
    all_to_all x1, starting transfers between devices, body(): rows = lax.all_to_all(rows.reshape(256, 8, 128), both, 0, 0, tiled=True)  6.17 us
    all_to_all x1, starting transfers between devices, body(): lax.all_to_all(columns.reshape(256, 8, 128), both, 0, 0, tiled=True)  6.01 us
    all_to_all x1, waiting for transfers between devices, body(): rows = lax.all_to_all(rows.reshape(256, 8, 128), both, 0, 0, tiled=True)  6.01 us
  transfers between devices with their start and end apart: 17, of which 6 were waited for; matrix products, arithmetic and copies ran while one was open for 1% of the time, Pallas kernels for 19%

profile of v2, /device:TPU:1, one launch (start us, length us, event | category | flops | bytes accessed | tf_op | source)
XLA Modules:
  0.0 123.3 jit_solution(2855045806839990964)
XLA Ops:
  0.6 0.0 copy-start.14
  0.6 0.0 copy-start
  1.4 1.6 %pack.1.p4.own_ref = f32[56,128]{1,0:T(8,128)} custom-call(s32[1]{0:T(128)S(6)} %copy.17.count_ref, s32[3,512]{1,0:T(4,128)} %base_at.1, f32[3,512]{1,0:T(4,128)} %frac_at.1, f32[4,128]{1,0:T(4,128)} %bitcast.19, s32[1,128]{1,0:T(1,128)} %bitcast.20, s32[32,128]{1,0:T(8,128)} %near_at.1), custom_call_target="tpu_custom_call" | custom-call | bytes 4194304 | tf_op jit(solution)/shard_map/pack/pallas_call | solution.py:518
  3.0 11.1 %collective-permute-start.6 = (f32[56,128]{1,0:T(8,128)}, f32[56,128]{1,0:T(8,128)S(1)}, u32[]{:S(2)}, u32[]{:S(2)}) collective-permute-start(f32[56,128]{1,0:T(8,128)} %pack.1.p4.own_ref), channel_id=1, source_target_pairs={{0,253},{1,254},{2,255},{3,0},{4,1},{5,2},{6,3},{7,4},{8,5},{9,6},... | collective-permute-start | bytes 86024 | tf_op jit(solution)/shard_map/particles_in/ppermute | solution.py:554
  14.1 1.0 collective-permute-start.5
  15.1 2.2 %collective-permute-start.4 = (f32[56,128]{1,0:T(8,128)}, f32[56,128]{1,0:T(8,128)S(1)}, u32[]{:S(2)}, u32[]{:S(2)}) collective-permute-start(f32[56,128]{1,0:T(8,128)} %pack.1.p4.own_ref), channel_id=1, source_target_pairs={{0,255},{1,0},{2,1},{3,2},{4,3},{5,4},{6,5},{7,6},{8,7},{9,8},{10,... | collective-permute-start | bytes 86024 | tf_op jit(solution)/shard_map/particles_in/ppermute | solution.py:554
  17.3 0.8 collective-permute-start.3
  18.1 1.4 %collective-permute-start.2 = (f32[56,128]{1,0:T(8,128)}, f32[56,128]{1,0:T(8,128)S(1)}, u32[]{:S(2)}, u32[]{:S(2)}) collective-permute-start(f32[56,128]{1,0:T(8,128)} %pack.1.p4.own_ref), channel_id=1, source_target_pairs={{0,2},{1,3},{2,4},{3,5},{4,6},{5,7},{6,8},{7,9},{8,10},{9,11},{10,... | collective-permute-start | bytes 86024 | tf_op jit(solution)/shard_map/particles_in/ppermute | solution.py:554
  19.4 0.0 collective-permute-done.6.p7
  19.4 0.0 collective-permute-start.1
  19.4 0.0 collective-permute-done.5.p6
  19.4 0.0 copy-start.16
  19.5 0.1 collective-permute-start
  19.5 1.1 dynamic-slice_convert_fusion
  20.7 0.0 collective-permute-done.4.p5.after_ref
  20.7 0.0 copy-start.8
  20.7 1.6 %collective-permute-done.3.p3.before_ref = f32[56,128]{1,0:T(8,128)S(1)} collective-permute-done((f32[56,128]{1,0:T(8,128)}, f32[56,128]{1,0:T(8,128)S(1)}, u32[]{:S(2)}, u32[]{:S(2)}) %collective-permute-start.3) | collective-permute-done | bytes 28704 | tf_op jit(solution)/shard_map/particles_in/ppermute | solution.py:554
  22.3 0.0 collective-permute-done.2.p2
  22.3 6.2 %collective-permute-done.1.p1 = f32[56,128]{1,0:T(8,128)S(1)} collective-permute-done((f32[56,128]{1,0:T(8,128)}, f32[56,128]{1,0:T(8,128)S(1)}, u32[]{:S(2)}, u32[]{:S(2)}) %collective-permute-start.1) | collective-permute-done | bytes 28704 | tf_op jit(solution)/shard_map/particles_in/ppermute | solution.py:554
  28.5 0.0 collective-permute-done.p0
  28.5 1.4 %collective-permute-start.7 = (bf16[128,4,256]{2,1,0:T(4,128)(2,1)S(1)}, bf16[128,4,256]{2,1,0:T(4,128)(2,1)S(1)}, u32[]{:S(2)}, u32[]{:S(2)}) collective-permute-start(bf16[128,4,256]{2,1,0:T(4,128)(2,1)S(1)} %dynamic-slice_convert_fusion), channel_id=1, source_target_pairs={{0,1},{1,0},{2,3},{3,2},{4,5},{5,4},{6,7},{7,6},{8,9},{9,8},{10,11... | collective-permute-start | bytes 786440 | tf_op jit(solution)/shard_map/influence_swap/ppermute | solution.py:590
  29.9 0.0 copy-done.15
  29.9 0.0 copy-done.16
  29.9 0.0 copy-done.8
  29.9 0.0 copy-done.10
  29.9 0.0 copy-done.17
  29.9 0.0 copy-done.18
  30.0 0.0 copy-done.19
  30.0 8.4 %spread.1 = (bf16[64,2,16,128]{3,2,1,0:T(8,128)(2,1)}, f32[6,24,128]{2,1,0:T(8,128)}, f32[240,384]{1,0:T(8,128)}, f32[240,384]{1,0:T(8,128)}, f32[3,384]{1,0:T(4,128)}) custom-call(f32[56,128]{1,0:T(8,128)} %copy-done.19, f32[56,128]{1,0:T(8,128)} %copy-done.18, f32[56,128]{1,0:T(8,128)} %copy-done.17, f32[56,128]{1,0:T(8,128)} %copy-done.10, ...), custom_call_target="tpu_custom_call" | custom-call | flops 4000000000 | bytes 4194304 | tf_op jit(solution)/shard_map/spread/pallas_call | solution.py:518
  38.3 0.0 collective-permute-done.7
  38.4 6.0 %all-to-all-start = ((bf16[256,8,128]{2,1,0:T(8,128)(2,1)}), bf16[256,8,128]{2,1,0:T(8,128)(2,1)S(1)}, u32[]{:S(2)}, u32[]{:S(2)}) async-start(bf16[256,8,128]{2,1,0:T(8,128)(2,1)} %bitcast.18), calls=%async_computation | async-start | bytes 1048576 | tf_op jit(solution)/shard_map/to_columns/all_to_all | solution.py:638
  44.4 0.1 convert_element_type.7.taken_ref
  44.5 0.0 copy-done
  44.5 0.7 influence.1.infl_ref
  45.1 19.6 %all-to-all-done = bf16[256,8,128]{2,1,0:T(8,128)(2,1)S(1)} async-done(((bf16[256,8,128]{2,1,0:T(8,128)(2,1)}), bf16[256,8,128]{2,1,0:T(8,128)(2,1)S(1)}, u32[]{:S(2)}, u32[]{:S(2)}) %all-to-all-start) | async-done | bytes 524320 | tf_op jit(solution)/shard_map/to_columns/all_to_all | solution.py:638
  64.8 0.0 copy-done.14
  64.8 3.9 %depth.1 = bf16[128,16,128]{2,1,0:T(8,128)(2,1)} custom-call(bf16[128,16,128]{2,1,0:T(8,128)(2,1)S(1)} %bitcast.13, f32[256,1024]{1,0:T(8,128)S(1)} %influence.1.infl_ref, bf16[4,256,256]{2,1,0:T(8,128)(2,1)S(1)} %copy-done.14), custom_call_target="tpu_custom_call" | custom-call | flops 800000000 | bytes 4194304 | tf_op jit(solution)/shard_map/depth/pallas_call | solution.py:518
  68.7 6.2 %all-to-all-start.1 = ((bf16[256,8,128]{2,1,0:T(8,128)(2,1)}), bf16[256,8,128]{2,1,0:T(8,128)(2,1)S(1)}, u32[]{:S(2)}, u32[]{:S(2)}) async-start(bf16[256,8,128]{2,1,0:T(8,128)(2,1)} %bitcast.10), calls=%async_computation.1 | async-start | bytes 1048576 | tf_op jit(solution)/shard_map/to_planes/all_to_all | solution.py:679
  74.8 0.0 copy-start.1
  74.9 0.0 copy-start.6
  74.9 6.4 %lookup_x.1.wx_at = bf16[22,512,256]{2,1,0:T(8,128)(2,1)} custom-call(f32[6,24,128]{2,1,0:T(8,128)} %get-tuple-element.39.refs_0_.part_ref), custom_call_target="tpu_custom_call" | custom-call | flops 4000000000 | bytes 4194304 | tf_op jit(solution)/shard_map/lookup_x/pallas_call | solution.py:518
  81.3 7.7 %lookup_y.1.wy_at = f32[22,512,256]{2,1,0:T(8,128)} custom-call(f32[6,24,128]{2,1,0:T(8,128)} %get-tuple-element.39.refs_0_.part_ref), custom_call_target="tpu_custom_call" | custom-call | flops 4000000000 | bytes 4194304 | tf_op jit(solution)/shard_map/lookup_y/pallas_call | solution.py:518
  89.0 0.0 copy-start.7
  89.0 0.0 copy-start.9
  89.0 0.0 copy-start.12
  89.1 0.0 copy-start.13
  89.1 6.0 %all-to-all-done.1 = bf16[256,8,128]{2,1,0:T(8,128)(2,1)S(1)} async-done(((bf16[256,8,128]{2,1,0:T(8,128)(2,1)}), bf16[256,8,128]{2,1,0:T(8,128)(2,1)S(1)}, u32[]{:S(2)}, u32[]{:S(2)}) %all-to-all-start.1) | async-done | bytes 524320 | tf_op jit(solution)/shard_map/to_planes/all_to_all | solution.py:679
  95.1 9.8 %probe.1 = (f32[1,512,512]{2,1,0:T(8,128)}, f32[24,128]{1,0:T(8,128)S(1)}, f32[24,128]{1,0:T(8,128)S(1)}, f32[24,128]{1,0:T(8,128)S(1)}, f32[24,128]{1,0:T(8,128...) custom-call(bf16[64,2,16,128]{3,2,1,0:T(8,128)(2,1)S(1)} %bitcast.12, ...), custom_call_target="tpu_custom_call" | custom-call | flops 5000000000 | bytes 4194304 | tf_op jit(solution)/shard_map/probe/pallas_call | solution.py:518
  104.9 1.7 %collective-permute-start.8 = (f32[24,128]{1,0:T(8,128)S(1)}, f32[24,128]{1,0:T(8,128)S(1)}, u32[]{:S(2)}, u32[]{:S(2)}) collective-permute-start(f32[24,128]{1,0:T(8,128)S(1)} %get-tuple-element.40), channel_id=1, source_target_pairs={{0,252},{1,253},{2,254},{3,255},{4,0},{5,1},{6,2},{7,3},{8,4},{9,5... | collective-permute-start | bytes 36872 | tf_op jit(solution)/shard_map/pushes_out/ppermute | solution.py:554
  106.6 1.8 %collective-permute-start.9 = (f32[24,128]{1,0:T(8,128)S(1)}, f32[24,128]{1,0:T(8,128)S(1)}, u32[]{:S(2)}, u32[]{:S(2)}) collective-permute-start(f32[24,128]{1,0:T(8,128)S(1)} %get-tuple-element.41), channel_id=1, source_target_pairs={{0,253},{1,254},{2,255},{3,0},{4,1},{5,2},{6,3},{7,4},{8,5},{9,6},... | collective-permute-start | bytes 36872 | tf_op jit(solution)/shard_map/pushes_out/ppermute | solution.py:554
  108.4 0.9 collective-permute-start.10
  109.3 2.6 %collective-permute-start.11 = (f32[24,128]{1,0:T(8,128)S(1)}, f32[24,128]{1,0:T(8,128)S(1)}, u32[]{:S(2)}, u32[]{:S(2)}) collective-permute-start(f32[24,128]{1,0:T(8,128)S(1)} %get-tuple-element.43), channel_id=1, source_target_pairs={{0,255},{1,0},{2,1},{3,2},{4,3},{5,4},{6,5},{7,6},{8,7},{9,8},{10,... | collective-permute-start | bytes 36872 | tf_op jit(solution)/shard_map/pushes_out/ppermute | solution.py:554
  111.9 0.4 collective-permute-start.12
  112.3 0.0 collective-permute-done.8.s0
  112.3 1.4 %collective-permute-start.13 = (f32[24,128]{1,0:T(8,128)S(1)}, f32[24,128]{1,0:T(8,128)S(1)}, u32[]{:S(2)}, u32[]{:S(2)}) collective-permute-start(f32[24,128]{1,0:T(8,128)S(1)} %get-tuple-element.46), channel_id=1, source_target_pairs={{0,2},{1,3},{2,4},{3,5},{4,6},{5,7},{6,8},{7,9},{8,10},{9,11},{10,... | collective-permute-start | bytes 36872 | tf_op jit(solution)/shard_map/pushes_out/ppermute | solution.py:554
  113.7 0.0 collective-permute-done.9.s1
  113.7 0.3 collective-permute-start.14
  114.0 0.0 collective-permute-done.10.s2
  114.0 0.0 collective-permute-done.11.s3
  114.0 2.5 %collective-permute-done.12.s5 = f32[24,128]{1,0:T(8,128)S(1)} collective-permute-done((f32[24,128]{1,0:T(8,128)S(1)}, f32[24,128]{1,0:T(8,128)S(1)}, u32[]{:S(2)}, u32[]{:S(2)}) %collective-permute-start.12) | collective-permute-done | bytes 12320 | tf_op jit(solution)/shard_map/pushes_out/ppermute | solution.py:554
  116.6 0.0 collective-permute-done.13.s6
  116.6 5.1 %collective-permute-done.14.s7 = f32[24,128]{1,0:T(8,128)S(1)} collective-permute-done((f32[24,128]{1,0:T(8,128)S(1)}, f32[24,128]{1,0:T(8,128)S(1)}, u32[]{:S(2)}, u32[]{:S(2)}) %collective-permute-start.14) | collective-permute-done | bytes 12320 | tf_op jit(solution)/shard_map/pushes_out/ppermute | solution.py:554
  121.7 0.0 copy-done.3
  121.8 1.5 %force.1 = f32[3,512]{1,0:T(4,128)} custom-call(f32[24,128]{1,0:T(8,128)S(1)} %collective-permute-done.8.s0, f32[24,128]{1,0:T(8,128)S(1)} %collective-permute-done.9.s1, f32[24,128]{1,0:T(8,128)S(1)} %collective-permute-done.10.s2, f32[24,128]{1,0:T(8,128)S(1)} %collective-permute-done.11.s3, f32[24,128]{1,0:T(8,128)S(1)} %get-tuple-element.44.s4, ...), custom_call_target="tpu_custom_call" | custom-call | bytes 4194304 | tf_op jit(solution)/shard_map/force/pallas_call | solution.py:518
  (20 shorter events, 0.0 us)
Async XLA Ops:
  0.6 64.1 %copy-start.14 = (bf16[4,256,256]{2,1,0:T(8,128)(2,1)S(1)}, bf16[4,256,256]{2,1,0:T(8,128)(2,1)}, u32[]{:S(2)}) copy-start(bf16[4,256,256]{2,1,0:T(8,128)(2,1)} %constant.17.clone.table_at) | copy-start | bytes 1572868
  0.6 43.8 %copy-start = (f32[128,4,512]{2,1,0:T(4,128)S(1)}, f32[128,4,512]{2,1,0:T(4,128)}, u32[]{:S(2)}) copy-start(f32[128,4,512]{2,1,0:T(4,128)} %kept_ref.1) | copy-start | bytes 3145732
  3.0 16.4 %collective-permute-start.6 = (f32[56,128]{1,0:T(8,128)}, f32[56,128]{1,0:T(8,128)S(1)}, u32[]{:S(2)}, u32[]{:S(2)}) collective-permute-start(f32[56,128]{1,0:T(8,128)} %pack.1.p4.own_ref), channel_id=1, source_target_pairs={{0,253},{1,254},{2,255},{3,0},{4,1},{5,2},{6,3},{7,4},{8,5},{9,6},... | collective-permute-start | bytes 86024 | tf_op jit(solution)/shard_map/particles_in/ppermute | solution.py:554
  14.1 5.3 %collective-permute-start.5 = (f32[56,128]{1,0:T(8,128)}, f32[56,128]{1,0:T(8,128)S(1)}, u32[]{:S(2)}, u32[]{:S(2)}) collective-permute-start(f32[56,128]{1,0:T(8,128)} %pack.1.p4.own_ref), channel_id=1, source_target_pairs={{0,254},{1,255},{2,0},{3,1},{4,2},{5,3},{6,4},{7,5},{8,6},{9,7},{1... | collective-permute-start | bytes 86024 | tf_op jit(solution)/shard_map/particles_in/ppermute | solution.py:554
  15.1 5.6 %collective-permute-start.4 = (f32[56,128]{1,0:T(8,128)}, f32[56,128]{1,0:T(8,128)S(1)}, u32[]{:S(2)}, u32[]{:S(2)}) collective-permute-start(f32[56,128]{1,0:T(8,128)} %pack.1.p4.own_ref), channel_id=1, source_target_pairs={{0,255},{1,0},{2,1},{3,2},{4,3},{5,4},{6,5},{7,6},{8,7},{9,8},{10,... | collective-permute-start | bytes 86024 | tf_op jit(solution)/shard_map/particles_in/ppermute | solution.py:554
  17.3 5.0 %collective-permute-start.3 = (f32[56,128]{1,0:T(8,128)}, f32[56,128]{1,0:T(8,128)S(1)}, u32[]{:S(2)}, u32[]{:S(2)}) collective-permute-start(f32[56,128]{1,0:T(8,128)} %pack.1.p4.own_ref), channel_id=1, source_target_pairs={{0,1},{1,2},{2,3},{3,4},{4,5},{5,6},{6,7},{7,8},{8,9},{9,10},{10,1... | collective-permute-start | bytes 86024 | tf_op jit(solution)/shard_map/particles_in/ppermute | solution.py:554
  18.1 4.2 %collective-permute-start.2 = (f32[56,128]{1,0:T(8,128)}, f32[56,128]{1,0:T(8,128)S(1)}, u32[]{:S(2)}, u32[]{:S(2)}) collective-permute-start(f32[56,128]{1,0:T(8,128)} %pack.1.p4.own_ref), channel_id=1, source_target_pairs={{0,2},{1,3},{2,4},{3,5},{4,6},{5,7},{6,8},{7,9},{8,10},{9,11},{10,... | collective-permute-start | bytes 86024 | tf_op jit(solution)/shard_map/particles_in/ppermute | solution.py:554
  19.4 10.5 %copy-start.15 = (f32[56,128]{1,0:T(8,128)}, f32[56,128]{1,0:T(8,128)S(1)}, u32[]{:S(2)}) copy-start(f32[56,128]{1,0:T(8,128)S(1)} %collective-permute-done.6.p7) | copy-start | bytes 86020
  19.4 9.1 %collective-permute-start.1 = (f32[56,128]{1,0:T(8,128)}, f32[56,128]{1,0:T(8,128)S(1)}, u32[]{:S(2)}, u32[]{:S(2)}) collective-permute-start(f32[56,128]{1,0:T(8,128)} %pack.1.p4.own_ref), channel_id=1, source_target_pairs={{0,3},{1,4},{2,5},{3,6},{4,7},{5,8},{6,9},{7,10},{8,11},{9,12},{10... | collective-permute-start | bytes 86024 | tf_op jit(solution)/shard_map/particles_in/ppermute | solution.py:554
  19.4 10.5 %copy-start.16 = (f32[56,128]{1,0:T(8,128)}, f32[56,128]{1,0:T(8,128)S(1)}, u32[]{:S(2)}) copy-start(f32[56,128]{1,0:T(8,128)S(1)} %collective-permute-done.5.p6) | copy-start | bytes 86020
  19.5 9.1 %collective-permute-start = (f32[56,128]{1,0:T(8,128)}, f32[56,128]{1,0:T(8,128)S(1)}, u32[]{:S(2)}, u32[]{:S(2)}) collective-permute-start(f32[56,128]{1,0:T(8,128)} %pack.1.p4.own_ref), channel_id=1, source_target_pairs={{0,4},{1,5},{2,6},{3,7},{4,8},{5,9},{6,10},{7,11},{8,12},{9,13},{1... | collective-permute-start | bytes 86024 | tf_op jit(solution)/shard_map/particles_in/ppermute | solution.py:554
  20.7 9.2 %copy-start.8 = (f32[56,128]{1,0:T(8,128)}, f32[56,128]{1,0:T(8,128)S(1)}, u32[]{:S(2)}) copy-start(f32[56,128]{1,0:T(8,128)S(1)} %collective-permute-done.4.p5.after_ref) | copy-start | bytes 86020
  22.3 7.6 %copy-start.10 = (f32[56,128]{1,0:T(8,128)}, f32[56,128]{1,0:T(8,128)S(1)}, u32[]{:S(2)}) copy-start(f32[56,128]{1,0:T(8,128)S(1)} %collective-permute-done.3.p3.before_ref) | copy-start | bytes 86020
  22.3 7.6 %copy-start.17 = (f32[56,128]{1,0:T(8,128)}, f32[56,128]{1,0:T(8,128)S(1)}, u32[]{:S(2)}) copy-start(f32[56,128]{1,0:T(8,128)S(1)} %collective-permute-done.2.p2) | copy-start | bytes 86020
  28.5 1.4 %copy-start.18 = (f32[56,128]{1,0:T(8,128)}, f32[56,128]{1,0:T(8,128)S(1)}, u32[]{:S(2)}) copy-start(f32[56,128]{1,0:T(8,128)S(1)} %collective-permute-done.1.p1) | copy-start | bytes 86020
  28.5 1.5 %copy-start.19 = (f32[56,128]{1,0:T(8,128)}, f32[56,128]{1,0:T(8,128)S(1)}, u32[]{:S(2)}) copy-start(f32[56,128]{1,0:T(8,128)S(1)} %collective-permute-done.p0) | copy-start | bytes 86020
  28.5 9.8 %collective-permute-start.7 = (bf16[128,4,256]{2,1,0:T(4,128)(2,1)S(1)}, bf16[128,4,256]{2,1,0:T(4,128)(2,1)S(1)}, u32[]{:S(2)}, u32[]{:S(2)}) collective-permute-start(bf16[128,4,256]{2,1,0:T(4,128)(2,1)S(1)} %dynamic-slice_convert_fusion), channel_id=1, source_target_pairs={{0,1},{1,0},{2,3},{3,2},{4,5},{5,4},{6,7},{7,6},{8,9},{9,8},{10,11... | collective-permute-start | bytes 786440 | tf_op jit(solution)/shard_map/influence_swap/ppermute | solution.py:590
  38.4 26.4 %all-to-all-start = ((bf16[256,8,128]{2,1,0:T(8,128)(2,1)}), bf16[256,8,128]{2,1,0:T(8,128)(2,1)S(1)}, u32[]{:S(2)}, u32[]{:S(2)}) async-start(bf16[256,8,128]{2,1,0:T(8,128)(2,1)} %bitcast.18), calls=%async_computation | async-start | bytes 1048576 | tf_op jit(solution)/shard_map/to_columns/all_to_all | solution.py:638
  68.7 26.4 %all-to-all-start.1 = ((bf16[256,8,128]{2,1,0:T(8,128)(2,1)}), bf16[256,8,128]{2,1,0:T(8,128)(2,1)S(1)}, u32[]{:S(2)}, u32[]{:S(2)}) async-start(bf16[256,8,128]{2,1,0:T(8,128)(2,1)} %bitcast.10), calls=%async_computation.1 | async-start | bytes 1048576 | tf_op jit(solution)/shard_map/to_planes/all_to_all | solution.py:679
  74.8 20.2 %copy-start.1 = (bf16[2,512,512]{2,1,0:T(8,128)(2,1)S(1)}, bf16[2,512,512]{2,1,0:T(8,128)(2,1)}, u32[]{:S(2)}) copy-start(bf16[2,512,512]{2,1,0:T(8,128)(2,1)} %constant.16.clone.table_at) | copy-start | bytes 3145732
  74.9 20.2 %copy-start.6 = (f32[6,24,128]{2,1,0:T(8,128)S(1)}, f32[6,24,128]{2,1,0:T(8,128)}, u32[]{:S(2)}) copy-start(f32[6,24,128]{2,1,0:T(8,128)} %get-tuple-element.39.refs_0_.part_ref) | copy-start | bytes 221188
  89.0 32.7 %copy-start.2 = (f32[240,384]{1,0:T(8,128)S(1)}, f32[240,384]{1,0:T(8,128)}, u32[]{:S(2)}) copy-start(f32[240,384]{1,0:T(8,128)} %get-tuple-element.48.h1_ref) | copy-start | bytes 1105924
  89.0 32.7 %copy-start.3 = (f32[240,384]{1,0:T(8,128)S(1)}, f32[240,384]{1,0:T(8,128)}, u32[]{:S(2)}) copy-start(f32[240,384]{1,0:T(8,128)} %get-tuple-element.49.t2_ref) | copy-start | bytes 1105924
  89.0 32.7 %copy-start.4 = (bf16[240,240]{1,0:T(8,128)(2,1)S(1)}, bf16[240,240]{1,0:T(8,128)(2,1)}, u32[]{:S(2)}) copy-start(bf16[240,240]{1,0:T(8,128)(2,1)} %w2_ref.1) | copy-start | bytes 345604
  89.0 32.7 %copy-start.5 = (f32[56,128]{1,0:T(8,128)S(1)}, f32[56,128]{1,0:T(8,128)}, u32[]{:S(2)}) copy-start(f32[56,128]{1,0:T(8,128)} %pack.1.p4.own_ref) | copy-start | bytes 86020
  89.0 32.7 %copy-start.7 = (bf16[128,240]{0,1:T(8,128)(2,1)S(1)}, bf16[128,240]{0,1:T(8,128)(2,1)}, u32[]{:S(2)}) copy-start(bf16[128,240]{0,1:T(8,128)(2,1)} %param.22) | copy-start | bytes 184324
  89.0 32.7 %copy-start.9 = (f32[56,128]{1,0:T(8,128)S(1)}, f32[56,128]{1,0:T(8,128)}, u32[]{:S(2)}) copy-start(f32[56,128]{1,0:T(8,128)} %copy-done.8) | copy-start | bytes 86020
  89.0 32.7 %copy-start.11 = (f32[56,128]{1,0:T(8,128)S(1)}, f32[56,128]{1,0:T(8,128)}, u32[]{:S(2)}) copy-start(f32[56,128]{1,0:T(8,128)} %copy-done.10) | copy-start | bytes 86020
  89.0 32.7 %copy-start.12 = (f32[3,384]{1,0:T(4,128)S(1)}, f32[3,384]{1,0:T(4,128)}, u32[]{:S(2)}) copy-start(f32[3,384]{1,0:T(4,128)} %get-tuple-element.50.to_ref) | copy-start | bytes 13828
  89.1 32.7 %copy-start.13 = (bf16[240,3]{0,1:T(4,128)(2,1)S(1)}, bf16[240,3]{0,1:T(4,128)(2,1)}, u32[]{:S(2)}) copy-start(bf16[240,3]{0,1:T(4,128)(2,1)} %param.26) | copy-start | bytes 4324
  104.9 7.4 %collective-permute-start.8 = (f32[24,128]{1,0:T(8,128)S(1)}, f32[24,128]{1,0:T(8,128)S(1)}, u32[]{:S(2)}, u32[]{:S(2)}) collective-permute-start(f32[24,128]{1,0:T(8,128)S(1)} %get-tuple-element.40), channel_id=1, source_target_pairs={{0,252},{1,253},{2,254},{3,255},{4,0},{5,1},{6,2},{7,3},{8,4},{9,5... | collective-permute-start | bytes 36872 | tf_op jit(solution)/shard_map/pushes_out/ppermute | solution.py:554
  106.6 7.1 %collective-permute-start.9 = (f32[24,128]{1,0:T(8,128)S(1)}, f32[24,128]{1,0:T(8,128)S(1)}, u32[]{:S(2)}, u32[]{:S(2)}) collective-permute-start(f32[24,128]{1,0:T(8,128)S(1)} %get-tuple-element.41), channel_id=1, source_target_pairs={{0,253},{1,254},{2,255},{3,0},{4,1},{5,2},{6,3},{7,4},{8,5},{9,6},... | collective-permute-start | bytes 36872 | tf_op jit(solution)/shard_map/pushes_out/ppermute | solution.py:554
  108.4 5.6 %collective-permute-start.10 = (f32[24,128]{1,0:T(8,128)S(1)}, f32[24,128]{1,0:T(8,128)S(1)}, u32[]{:S(2)}, u32[]{:S(2)}) collective-permute-start(f32[24,128]{1,0:T(8,128)S(1)} %get-tuple-element.42), channel_id=1, source_target_pairs={{0,254},{1,255},{2,0},{3,1},{4,2},{5,3},{6,4},{7,5},{8,6},{9,7},{1... | collective-permute-start | bytes 36872 | tf_op jit(solution)/shard_map/pushes_out/ppermute | solution.py:554
  109.3 4.7 %collective-permute-start.11 = (f32[24,128]{1,0:T(8,128)S(1)}, f32[24,128]{1,0:T(8,128)S(1)}, u32[]{:S(2)}, u32[]{:S(2)}) collective-permute-start(f32[24,128]{1,0:T(8,128)S(1)} %get-tuple-element.43), channel_id=1, source_target_pairs={{0,255},{1,0},{2,1},{3,2},{4,3},{5,4},{6,5},{7,6},{8,7},{9,8},{10,... | collective-permute-start | bytes 36872 | tf_op jit(solution)/shard_map/pushes_out/ppermute | solution.py:554
  111.9 4.6 %collective-permute-start.12 = (f32[24,128]{1,0:T(8,128)S(1)}, f32[24,128]{1,0:T(8,128)S(1)}, u32[]{:S(2)}, u32[]{:S(2)}) collective-permute-start(f32[24,128]{1,0:T(8,128)S(1)} %get-tuple-element.45), channel_id=1, source_target_pairs={{0,1},{1,2},{2,3},{3,4},{4,5},{5,6},{6,7},{7,8},{8,9},{9,10},{10,1... | collective-permute-start | bytes 36872 | tf_op jit(solution)/shard_map/pushes_out/ppermute | solution.py:554
  112.3 4.2 %collective-permute-start.13 = (f32[24,128]{1,0:T(8,128)S(1)}, f32[24,128]{1,0:T(8,128)S(1)}, u32[]{:S(2)}, u32[]{:S(2)}) collective-permute-start(f32[24,128]{1,0:T(8,128)S(1)} %get-tuple-element.46), channel_id=1, source_target_pairs={{0,2},{1,3},{2,4},{3,5},{4,6},{5,7},{6,8},{7,9},{8,10},{9,11},{10,... | collective-permute-start | bytes 36872 | tf_op jit(solution)/shard_map/pushes_out/ppermute | solution.py:554
  113.7 8.0 %collective-permute-start.14 = (f32[24,128]{1,0:T(8,128)S(1)}, f32[24,128]{1,0:T(8,128)S(1)}, u32[]{:S(2)}, u32[]{:S(2)}) collective-permute-start(f32[24,128]{1,0:T(8,128)S(1)} %get-tuple-element.47), channel_id=1, source_target_pairs={{0,3},{1,4},{2,5},{3,6},{4,7},{5,8},{6,9},{7,10},{8,11},{9,12},{10... | collective-permute-start | bytes 36872 | tf_op jit(solution)/shard_map/pushes_out/ppermute | solution.py:554

commit v3 on v2

--- a/solution.py
+++ b/solution.py
@@ -7,6 +7,7 @@
 from jax import lax
 from jax.experimental import pallas as pl
 from jax.experimental.pallas import tpu as pltpu
+from jax.sharding import Mesh
 from jax.sharding import PartitionSpec as P
 
 NX = 512
@@ -65,6 +66,39 @@
     high = values.astype(BF)
     low = (values - high.astype(F32)).astype(BF)
     return high, low
+
+
+def chip_of(device):
+    device = device % 256
+    place = device % 8
+    return device // 8 * 4 + place // 4 * 2 + place % 2, place // 2 % 2
+
+
+def device_of(chip, core):
+    chip = chip % 128
+    return chip // 4 * 8 + chip % 4 // 2 * 4 + core * 2 + chip % 2
+
+
+def chip_steps(kind):
+    pairs = []
+    for chip in range(128):
+        if kind < 2:
+            pairs.append((device_of(chip - kind - 1, 0), device_of(chip, 0)))
+            pairs.append((device_of(chip + kind + 1, 1), device_of(chip, 1)))
+        else:
+            other = chip - 3 if chip % 2 else chip + 3
+            pairs.append((device_of(other, 0), device_of(chip, 0)))
+    return pairs
+
+
+def row_index(place, step):
+    there = place + step
+    inner = there & 7
+    chip = (there >> 3) * 4 + ((inner >> 2) & 1) * 2 + (inner & 1)
+    away = chip - (((place >> 2) & 1) * 2 + (place & 1))
+    first = jnp.where(away == 1, 6, jnp.where(away == 2, 8, 4))
+    first = jnp.where(away == -1, 0, jnp.where(away == -2, 2, first))
+    return jnp.where(away == 0, 12, first) + ((inner >> 1) & 1)
 
 
 def fetch(pairs, sems, first=0):
@@ -187,11 +221,11 @@
 
 
 def spread_kernel(
-    p0, p1, p2, p3, p4, p5, p6, p7,
-    w1_at, b1_at, w2_at, b2_at, wo_at, bo_at, table_at,
-    out_ref, part_ref, h1_ref, t2_ref, to_ref,
-    code_s, feat_s, in_s, xin_s, cell_s, wgt_s, sxa_s, wya_s, sxb_s, wyb_s, total_s,
-    table_ref, w1_ref, b1_ref, w2_ref, b2_ref, wo_ref, bo_ref, sems,
+    place_ref, far_ref, pair_ref,
+    w1_at, b1_at, w2_at, b2_at, wo_at, bo_at, table_at, infl_at,
+    out_ref, part_ref, h1_ref, t2_ref, to_ref, beside_ref, given_ref,
+    rows_s, code_s, feat_s, in_s, xin_s, cell_s, wgt_s, sxa_s, wya_s, sxb_s, wyb_s, total_s,
+    table_ref, w1_ref, b1_ref, w2_ref, b2_ref, wo_ref, bo_ref, half_s, sems,
 ):
     copies = fetch(
         (
@@ -200,11 +234,19 @@
         ),
         sems,
     )
-    (table_copy,) = fetch(((table_at, table_ref),), sems, 6)
-    pays = (p0, p1, p2, p3, p4, p5, p6, p7)
+    away = pl.multiple_of(256 - (place_ref[0] & 1) * 256, 256)
+    table_copy, half_copy = fetch(
+        ((table_at, table_ref), (infl_at.at[:, :, pl.ds(away, 256)], half_s)), sems, 6
+    )
+    index = [row_index(place_ref[0], step) for step in NEAR]
+    rows_s[0:12] = far_ref[...]
+    rows_s[12:14] = pair_ref[...]
 
     def pay(i, start, stop):
-        return pays[i][start:stop, :]
+        return rows_s[index[i], start:stop, :]
+
+    beside_ref[0] = pay(3, 0, 56)
+    beside_ref[1] = pay(5, 0, 56)
 
     rim = [
         jnp.concatenate([pay(i, r, r + 1) for i in range(8)], axis=0) for r in (0, 4, 8, 12, 16)
@@ -270,12 +312,13 @@
     part_ref[:, 22:24, :] = jnp.zeros((6, 2, 128), F32)
     tables = ((sxa_s, wya_s), (sxb_s, wyb_s))
     density = densities(part_ref, cell_s, wgt_s, tables, total_s)
+    half_copy.wait()
+    given_ref[...] = half_s[...].astype(BF)
     table_copy.wait()
-    hh, hl = table_ref[0], table_ref[1]
+    hh = table_ref[...]
     high, low = split(density)
-    inner = dot(high, hh) + dot(low, hh) + dot(high, hl)
-    inner = inner.astype(BF)
-    spectrum = dot(hh, inner) + dot(hl, inner)
+    inner = (dot(high, hh) + dot(low, hh)).astype(BF)
+    spectrum = dot(hh, inner)
     lower = lax.broadcasted_iota(jnp.int32, (64, 8, 128), 1) < 4
     for g in range(2):
         tile0 = spectrum[:, 256 * g : 256 * g + 128].reshape(64, 8, 128)
@@ -287,7 +330,7 @@
 
 
 def influence_kernel(group_ref, kept_ref, taken_ref, out_ref):
-    mine = pl.multiple_of(group_ref[0] * 128, 128)
+    mine = pl.multiple_of((group_ref[0] & 1) * 128, 128)
     other = pl.multiple_of(128 - mine, 128)
     for r in range(8):
         lanes = slice(128 * r, 128 * r + 128)
@@ -297,22 +340,20 @@
 
 
 def depth_kernel(
-    x_ref, infl_ref, table_at, out_ref, wide_s, xb_s, back_s, table_ref, sems
+    x_ref, infl_ref, table_ref, out_ref, wide_s, xb_s, back_s
 ):
-    (table_copy,) = fetch(((table_at, table_ref),), sems)
     wide_s[...] = x_ref[...].astype(F32)
     for r in range(8):
         lanes = slice(128 * r, 128 * r + 128)
         xb_s[0:128, lanes] = wide_s[:, r, :].astype(BF)
         xb_s[128:256, lanes] = wide_s[:, 8 + r, :].astype(BF)
-    table_copy.wait()
     fh, fl, ih, il = (table_ref[n] for n in range(4))
     for r in range(0, 8, 2):
         lanes = slice(128 * r, 128 * r + 256)
         xb = xb_s[:, lanes]
         spectrum = dot(fh, xb) + dot(fl, xb)
-        high, low = split(spectrum * infl_ref[:, lanes])
-        back = dot(ih, high) + dot(il, high) + dot(ih, low)
+        weighted = (spectrum * infl_ref[:, lanes]).astype(BF)
+        back = dot(ih, weighted) + dot(il, weighted)
         for t in range(2):
             column = back[:, 128 * t : 128 * t + 128]
             back_s[:, r + t, :] = column[0:128]
@@ -377,10 +418,10 @@
         r_s[:, 256 * g : 256 * g + 128] = tile0.reshape(512, 128).astype(BF)
         r_s[:, 256 * g + 128 : 256 * g + 256] = tile1.reshape(512, 128).astype(BF)
     table_copy.wait()
-    hh, hl = table_ref[0], table_ref[1]
-    inner = dot(hh, r_s[...]) + dot(hl, r_s[...])
+    hh = table_ref[...]
+    inner = dot(hh, r_s[...])
     inner = inner.astype(BF)
-    potential = (dot(inner, hh) + dot(inner, hl)) * (1.0 / 67108864.0)
+    potential = dot(inner, hh) * (1.0 / 67108864.0)
     pot_s[...] = potential
     pot_copy = pltpu.make_async_copy(pot_s, pot_at.at[0], sems.at[3])
     pot_copy.start()
@@ -440,7 +481,7 @@
 
 
 def force_kernel(
-    s0, s1, s2, s3, s4, s5, s6, s7, before_ref, own_ref, after_ref,
+    s0, s1, s2, s3, s4, s5, s6, s7, beside_ref, own_ref,
     h1_ref, t2_ref, to_ref, w1_ref, w2_ref, wo_ref, out_ref, gin_s,
 ):
     total = s0[...] + s1[...] + s2[...] + s3[...] + s4[...] + s5[...] + s6[...] + s7[...]
@@ -455,7 +496,7 @@
     g_pre = g_two * (1.0 - t2 * t2)
     g_one = dot(w2_ref[...], g_pre.astype(BF)) + g_two
     gin_s[...] = dot_first(w1_ref[...], (g_one * (1.0 - h1 * h1)).astype(BF))
-    pays = (before_ref, own_ref, after_ref)
+    pays = (beside_ref.at[0], own_ref, beside_ref.at[1])
     turn = lax.broadcasted_iota(jnp.int32, (8, 128), 0).astype(F32)
 
     def rims(ref):
@@ -545,15 +586,14 @@
     layer_out,
     bias_out,
 ):
-    both = ("slab", "grp")
+    both = ("row", "core", "grp")
     devices = 256
-    group = lax.axis_index("grp")
 
     def from_device(value, step):
         pairs = [(source, (source - step) % devices) for source in range(devices)]
         return lax.ppermute(value, both, pairs)
 
-    planes = jnp.asarray(np.stack(cas_pair(np.arange(NX), np.arange(NX), NX)))
+    planes = jnp.asarray(cas_pair(np.arange(NX), np.arange(NX), NX)[0])
     split_z = np.concatenate([np.arange(0, NZ, 2), np.arange(1, NZ, 2)])
     fore = cas_pair(np.arange(NZ), split_z, NZ)
     back = cas_pair(split_z, np.arange(NZ), NZ)
@@ -582,17 +622,18 @@
             limit=59,
         )
     with jax.named_scope("particles_in"):
-        pays = [payload if step == 0 else from_device(payload, step) for step in NEAR]
-    where = group.astype(jnp.int32).reshape(1)
-    with jax.named_scope("influence_swap"):
-        given = lax.dynamic_slice_in_dim(influence, (1 - group) * 256, 256, axis=2).astype(BF)
-        given, *pays = lax.optimization_barrier((given, *pays))
-        taken = lax.ppermute(given, "grp", [(0, 1), (1, 0)])
+        pair = lax.all_gather(payload, "core")
+        far = [lax.ppermute(pair, both, chip_steps(kind)) for kind in range(3)]
+        far = lax.all_gather(jnp.concatenate(far, axis=0), "core").reshape(12, 56, 128)
+    place = (lax.axis_index("row") & 1) * 4 + lax.axis_index("core") * 2 + lax.axis_index("grp")
+    where = place.astype(jnp.int32).reshape(1)
     with jax.named_scope("spread"):
-        columns, part, h1, t2, to = call(
+        columns, part, h1, t2, to, beside, given = call(
             spread_kernel,
             (
-                *pays,
+                where,
+                far,
+                pair,
                 layer_one.T,
                 bias_one.reshape(1, -1),
                 layer_two,
@@ -600,6 +641,7 @@
                 layer_out.T,
                 bias_out.reshape(1, -1),
                 planes,
+                influence,
             ),
             (
                 shape(64, 2, 16, 128, dtype=BF),
@@ -607,8 +649,11 @@
                 shape(HID, 384),
                 shape(HID, 384),
                 shape(3, 384),
+                shape(2, 56, 128),
+                shape(128, 4, 256, dtype=BF),
             ),
             (
+                pltpu.VMEM((14, 56, 128), F32),
                 pltpu.VMEM((NEIGH, 8, 128), F32),
                 pltpu.VMEM((24, 4, 8, 128), F32),
                 pltpu.VMEM((128, 8, 128), F32),
@@ -620,20 +665,22 @@
                 pltpu.VMEM((NX, 512), BF),
                 pltpu.VMEM((NY, 512), BF),
                 pltpu.VMEM((NX, NY), F32),
-                pltpu.VMEM((2, NX, NX), BF),
+                pltpu.VMEM((NX, NX), BF),
                 pltpu.VMEM((HID, 128), BF),
                 pltpu.VMEM((1, HID), F32),
                 pltpu.VMEM((HID, HID), BF),
                 pltpu.VMEM((1, HID), F32),
                 pltpu.VMEM((3, HID), BF),
                 pltpu.VMEM((1, 3), F32),
-                pltpu.SemaphoreType.DMA((7,)),
+                pltpu.VMEM((128, 4, 256), F32),
+                pltpu.SemaphoreType.DMA((8,)),
             ),
             limit=58,
-            spaces={n: HB for n in range(8, 15)},
+            spaces={0: SM, **{n: HB for n in range(3, 11)}},
             flops=4_000_000_000,
         )
-    columns, taken = lax.optimization_barrier((columns, taken))
+    with jax.named_scope("influence_swap"):
+        taken = lax.ppermute(given, "grp", [(0, 1), (1, 0)])
     with jax.named_scope("to_columns"):
         columns = lax.all_to_all(columns.reshape(256, 8, 128), both, 0, 0, tiled=True)
     def lookup(axis, kind):
@@ -668,10 +715,7 @@
                 pltpu.VMEM((128, 16, 128), F32),
                 pltpu.VMEM((NZ, 1024), BF),
                 pltpu.VMEM((128, 16, 128), F32),
-                pltpu.VMEM((4, NZ, NZ), BF),
-                pltpu.SemaphoreType.DMA((1,)),
             ),
-            spaces={2: HB},
             limit=50,
             flops=800_000_000,
         )
@@ -693,7 +737,7 @@
                 pltpu.VMEM((NX, NY), F32),
                 pltpu.VMEM((22, NX, 256), BF),
                 pltpu.VMEM((22, NY, 256), F32),
-                pltpu.VMEM((2, NX, NX), BF),
+                pltpu.VMEM((NX, NX), BF),
                 pltpu.SemaphoreType.DMA((5,)),
             ),
             first=HB,
@@ -708,7 +752,7 @@
     with jax.named_scope("force"):
         force = call(
             force_kernel,
-            (*sums, pays[3], payload, pays[5], h1, t2, to, layer_one.T, layer_two, layer_out.T),
+            (*sums, beside, payload, h1, t2, to, layer_one.T, layer_two, layer_out.T),
             shape(3, 512),
             (pltpu.VMEM((128, 384), F32),),
             limit=16,
@@ -717,17 +761,18 @@
 
 
 def solution(mesh):
+    fine = Mesh(mesh.devices.reshape(64, 2, 2), ("row", "core", "grp"))
     return jax.shard_map(
         body,
-        mesh=mesh,
+        mesh=fine,
         in_specs=(
-            P(None, ("slab", "grp")),
-            P(None, ("slab", "grp")),
-            P(("slab", "grp")),
-            P(("slab", "grp")),
-            P(("slab", "grp")),
-            P(None, ("slab", "grp")),
-            P("grp", "slab", None),
+            P(None, ("row", "core", "grp")),
+            P(None, ("row", "core", "grp")),
+            P(("row", "core", "grp")),
+            P(("row", "core", "grp")),
+            P(("row", "core", "grp")),
+            P(None, ("row", "core", "grp")),
+            P("grp", ("row", "core"), None),
             P(),
             P(),
             P(),
@@ -735,6 +780,6 @@
             P(),
             P(),
         ),
-        out_specs=(P(None, ("slab", "grp")), P(("slab", "grp"), None, None)),
+        out_specs=(P(None, ("row", "core", "grp")), P(("row", "core", "grp"), None, None)),
         check_vma=False,
     )

time: 124 us -> 122 us (0.984)
  blocking collectives: 0 us -> 13.7 us
  waiting for transfers between devices: 41.1 us -> 33 us
  starting transfers between devices: 39.2 us -> 34.5 us
  Pallas kernels: 40 us -> 38.6 us
    ppermute x14 -> x7, starting transfers between devices: 25.6 us -> 9.13 us  [from_device(): return lax.ppermute(value, both, pairs)]
    all_gather x0 -> x2, blocking collectives: none -> 13.7 us  [the longest x1 8.77 us: body(): lax.all_gather(jnp.concatenate(far, axis=0), 'core').reshape(12, 56, 128)]
    all_to_all x1, waiting for transfers between devices: 19.6 us -> 7.32 us  [body(): lax.all_to_all(columns.reshape(256, 8, 128), both, 0, 0, tiled=True)]
    ppermute x0 -> x3, starting transfers between devices: none -> 9.76 us  [body(): far = [lax.ppermute(pair, both, chip_steps(kind)) for kind in range(3)]]
    ppermute x1, waiting for transfers between devices: 0.01 us -> 9.32 us  [body(): taken = lax.ppermute(given, 'grp', [(0, 1), (1, 0)])]
    ppermute x14 -> x7, waiting for transfers between devices: 15.5 us -> 7.68 us  [from_device(): return lax.ppermute(value, both, pairs)]
    ppermute x0 -> x3, waiting for transfers between devices: none -> 2.72 us  [body(): far = [lax.ppermute(pair, both, chip_steps(kind)) for kind in range(3)]]
    ppermute x1, starting transfers between devices: 1.41 us -> 3 us  [body(): taken = lax.ppermute(given, 'grp', [(0, 1), (1, 0)])]
  transfers between devices with their start and end apart: 17 -> 13, of which waited for: 6 -> 6; matrix products, arithmetic and copies ran while one was open for 1% -> 0% of each run, Pallas kernels for 19% -> 12%
where the time goes in v3:
time: 122 us
  Pallas kernels  38.6 us (32%)
  starting transfers between devices  34.5 us (28%)
  waiting for transfers between devices  33 us (27%)
  blocking collectives  13.7 us (11%)
  between operations  1.59 us (1%)
    pallas_call x8, Pallas kernels, call(): pl.pallas_call(kernel, out_shape=outs, in_specs=[spaces.get(n, VM) for n...  38.6 us
    ppermute x3, starting transfers between devices, body(): far = [lax.ppermute(pair, both, chip_steps(kind)) for kind in range(3)]  9.76 us
    ppermute x1, waiting for transfers between devices, body(): taken = lax.ppermute(given, 'grp', [(0, 1), (1, 0)])  9.32 us
    ppermute x7, starting transfers between devices, from_device(): return lax.ppermute(value, both, pairs)  9.13 us
    all_gather x1, blocking collectives, body(): lax.all_gather(jnp.concatenate(far, axis=0), 'core').reshape(12, 56, 128)  8.77 us
    ppermute x7, waiting for transfers between devices, from_device(): return lax.ppermute(value, both, pairs)  7.68 us
    all_to_all x1, waiting for transfers between devices, body(): lax.all_to_all(columns.reshape(256, 8, 128), both, 0, 0, tiled=True)  7.32 us
    all_to_all x1, starting transfers between devices, body(): rows = lax.all_to_all(rows.reshape(256, 8, 128), both, 0, 0, tiled=True)  7.17 us
  transfers between devices with their start and end apart: 13, of which 6 were waited for; matrix products, arithmetic and copies ran while one was open for 0% of the time, Pallas kernels for 12%

profile of v3, /device:TPU:1, one launch (start us, length us, event | category | flops | bytes accessed | tf_op | source)
XLA Modules:
  0.0 121.6 jit_solution(6177504777690707862)
XLA Ops:
  0.6 0.0 copy-start.10
  0.6 0.0 copy-start
  1.4 1.6 %pack.1.own_ref = f32[56,128]{1,0:T(8,128)} custom-call(s32[1]{0:T(128)S(6)} %copy.17.count_ref, s32[3,512]{1,0:T(4,128)} %base_at.1, f32[3,512]{1,0:T(4,128)} %frac_at.1, f32[4,128]{1,0:T(4,128)} %bitcast.24, s32[1,128]{1,0:T(1,128)} %bitcast.25, s32[32,128]{1,0:T(8,128)} %near_at.1), custom_call_target="tpu_custom_call" | custom-call | bytes 4194304 | tf_op jit(solution)/shard_map/pack/pallas_call | solution.py:559
  3.0 5.0 %all-gather = f32[112,128]{1,0:T(8,128)S(1)} all-gather(f32[56,128]{1,0:T(8,128)} %pack.1.own_ref), channel_id=2, replica_groups=mesh['row'=64,'core'=2,'grp'=2] {'core'}, dimensions={0}, use_global_device_ids=true | all-gather | bytes 86016 | tf_op jit(solution)/shard_map/particles_in/all_gather | solution.py:625
  8.0 0.0 copy-start.12
  8.0 0.7 collective-permute-start.2
  8.6 7.3 %collective-permute-start.1 = (f32[2,56,128]{2,1,0:T(8,128)S(1)}, f32[2,56,128]{2,1,0:T(8,128)S(1)}, u32[]{:S(2)}, u32[]{:S(2)}) collective-permute-start(f32[2,56,128]{2,1,0:T(8,128)S(1)} %bitcast.21), channel_id=1, source_target_pairs={{252,0},{6,2},{253,1},{7,3},{0,4},{10,6},{1,5},{11,7},{4,8},{14,10... | collective-permute-start | bytes 172040 | tf_op jit(solution)/shard_map/particles_in/ppermute | solution.py:626
  15.9 1.8 %collective-permute-start = (f32[2,56,128]{2,1,0:T(8,128)S(1)}, f32[2,56,128]{2,1,0:T(8,128)S(1)}, u32[]{:S(2)}, u32[]{:S(2)}) collective-permute-start(f32[2,56,128]{2,1,0:T(8,128)S(1)} %bitcast.22), channel_id=1, source_target_pairs={{253,0},{3,2},{0,1},{6,3},{1,4},{7,6},{4,5},{10,7},{5,8},{11,10},{... | collective-permute-start | bytes 172040 | tf_op jit(solution)/shard_map/particles_in/ppermute | solution.py:626
  17.7 0.0 collective-permute-done.2
  17.8 0.0 collective-permute-done.1
  17.8 2.7 %collective-permute-done = f32[2,56,128]{2,1,0:T(8,128)S(1)} collective-permute-done((f32[2,56,128]{2,1,0:T(8,128)S(1)}, f32[2,56,128]{2,1,0:T(8,128)S(1)}, u32[]{:S(2)}, u32[]{:S(2)}) %collective-permute-start) | collective-permute-done | bytes 57376 | tf_op jit(solution)/shard_map/particles_in/ppermute | solution.py:626
  20.5 8.8 %all-gather.1.far_ref = f32[12,56,128]{2,1,0:T(8,128)} all-gather(f32[6,56,128]{2,1,0:T(8,128)S(1)} %pad_maximum_fusion), channel_id=3, replica_groups=mesh['row'=64,'core'=2,'grp'=2] {'core'}, dimensions={0}, use_global_device_ids=true | all-gather | bytes 516096 | tf_op jit(solution)/shard_map/particles_in/all_gather | solution.py:627
  29.3 0.0 copy-done.12
  29.3 8.1 %spread.1 = (bf16[64,2,16,128]{3,2,1,0:T(8,128)(2,1)}, f32[6,24,128]{2,1,0:T(8,128)}, f32[240,384]{1,0:T(8,128)}, f32[240,384]{1,0:T(8,128)}, f32[3,384]{1,0:T(4...) custom-call(s32[1]{0:T(128)} %bitcast.place_ref.group_ref, f32[12,56,128]{2,1,0:T(8,128)} %all-gather.1.far_ref, ...), custom_call_target="tpu_custom_call" | custom-call | flops 4000000000 | bytes 4194304 | tf_op jit(solution)/shard_map/spread/pallas_call | solution.py:559
  37.4 5.4 %all-to-all-start = ((bf16[256,8,128]{2,1,0:T(8,128)(2,1)}), bf16[256,8,128]{2,1,0:T(8,128)(2,1)S(1)}, u32[]{:S(2)}, u32[]{:S(2)}) async-start(bf16[256,8,128]{2,1,0:T(8,128)(2,1)} %bitcast.19), calls=%async_computation | async-start | bytes 1048576 | tf_op jit(solution)/shard_map/to_columns/all_to_all | solution.py:685
  42.8 3.0 %collective-permute-start.3 = (bf16[128,4,256]{2,1,0:T(4,128)(2,1)}, bf16[128,4,256]{2,1,0:T(4,128)(2,1)S(1)}, u32[]{:S(2)}, u32[]{:S(2)}) collective-permute-start(bf16[128,4,256]{2,1,0:T(4,128)(2,1)} %get-tuple-element.19), channel_id=1, source_target_pairs={{0,1},{1,0},{2,3},{3,2},{4,5},{5,4},{6,7},{7,6},{8,9},{9,8},{10,11... | collective-permute-start | bytes 786440 | tf_op jit(solution)/shard_map/influence_swap/ppermute | solution.py:683
  45.8 9.3 %collective-permute-done.3 = bf16[128,4,256]{2,1,0:T(4,128)(2,1)S(1)} collective-permute-done((bf16[128,4,256]{2,1,0:T(4,128)(2,1)}, bf16[128,4,256]{2,1,0:T(4,128)(2,1)S(1)}, u32[]{:S(2)}, u32[]{:S(2)}) %collective-permute-start.3) | collective-permute-done | bytes 262176 | tf_op jit(solution)/shard_map/influence_swap/ppermute | solution.py:683
  55.1 0.1 convert_element_type.3.taken_ref
  55.2 0.0 copy-done
  55.2 0.7 influence.1.infl_ref
  55.9 7.3 %all-to-all-done = bf16[256,8,128]{2,1,0:T(8,128)(2,1)S(1)} async-done(((bf16[256,8,128]{2,1,0:T(8,128)(2,1)}), bf16[256,8,128]{2,1,0:T(8,128)(2,1)S(1)}, u32[]{:S(2)}, u32[]{:S(2)}) %all-to-all-start) | async-done | bytes 524320 | tf_op jit(solution)/shard_map/to_columns/all_to_all | solution.py:685
  63.2 0.0 copy-done.10
  63.2 2.8 %depth.1 = bf16[128,16,128]{2,1,0:T(8,128)(2,1)} custom-call(bf16[128,16,128]{2,1,0:T(8,128)(2,1)S(1)} %bitcast.13, f32[256,1024]{1,0:T(8,128)S(1)} %influence.1.infl_ref, bf16[4,256,256]{2,1,0:T(8,128)(2,1)S(1)} %copy-done.10), custom_call_target="tpu_custom_call" | custom-call | flops 800000000 | bytes 4194304 | tf_op jit(solution)/shard_map/depth/pallas_call | solution.py:559
  66.0 7.2 %all-to-all-start.1 = ((bf16[256,8,128]{2,1,0:T(8,128)(2,1)}), bf16[256,8,128]{2,1,0:T(8,128)(2,1)S(1)}, u32[]{:S(2)}, u32[]{:S(2)}) async-start(bf16[256,8,128]{2,1,0:T(8,128)(2,1)} %bitcast.11), calls=%async_computation.1 | async-start | bytes 1048576 | tf_op jit(solution)/shard_map/to_planes/all_to_all | solution.py:723
  73.2 0.0 copy-start.9
  73.2 0.0 copy-start.11
  73.2 6.4 %lookup_x.1.wx_at = bf16[22,512,256]{2,1,0:T(8,128)(2,1)} custom-call(f32[6,24,128]{2,1,0:T(8,128)} %get-tuple-element.20.refs_0_.part_ref), custom_call_target="tpu_custom_call" | custom-call | flops 4000000000 | bytes 4194304 | tf_op jit(solution)/shard_map/lookup_x/pallas_call | solution.py:559
  79.6 7.8 %lookup_y.1.wy_at = f32[22,512,256]{2,1,0:T(8,128)} custom-call(f32[6,24,128]{2,1,0:T(8,128)} %get-tuple-element.20.refs_0_.part_ref), custom_call_target="tpu_custom_call" | custom-call | flops 4000000000 | bytes 4194304 | tf_op jit(solution)/shard_map/lookup_y/pallas_call | solution.py:559
  87.4 0.0 copy-start.1
  87.4 0.0 copy-start.2
  87.4 0.0 copy-start.3
  87.4 0.0 copy-start.4
  87.4 0.0 copy-start.5
  87.4 0.0 copy-start.6
  87.4 0.0 copy-start.7
  87.4 0.0 copy-start.8
  87.5 6.0 %all-to-all-done.1 = bf16[256,8,128]{2,1,0:T(8,128)(2,1)S(1)} async-done(((bf16[256,8,128]{2,1,0:T(8,128)(2,1)}), bf16[256,8,128]{2,1,0:T(8,128)(2,1)S(1)}, u32[]{:S(2)}, u32[]{:S(2)}) %all-to-all-start.1) | async-done | bytes 524320 | tf_op jit(solution)/shard_map/to_planes/all_to_all | solution.py:723
  93.4 0.0 copy-done.9
  93.4 0.0 copy-done.11
  93.4 9.8 %probe.1 = (f32[1,512,512]{2,1,0:T(8,128)}, f32[24,128]{1,0:T(8,128)S(1)}, f32[24,128]{1,0:T(8,128)S(1)}, f32[24,128]{1,0:T(8,128)S(1)}, f32[24,128]{1,0:T(8,128...) custom-call(bf16[64,2,16,128]{3,2,1,0:T(8,128)(2,1)S(1)} %bitcast.14, ...), custom_call_target="tpu_custom_call" | custom-call | flops 5000000000 | bytes 4194304 | tf_op jit(solution)/shard_map/probe/pallas_call | solution.py:559
  103.2 1.7 %collective-permute-start.4 = (f32[24,128]{1,0:T(8,128)S(1)}, f32[24,128]{1,0:T(8,128)S(1)}, u32[]{:S(2)}, u32[]{:S(2)}) collective-permute-start(f32[24,128]{1,0:T(8,128)S(1)} %get-tuple-element.21), channel_id=1, source_target_pairs={{0,252},{1,253},{2,254},{3,255},{4,0},{5,1},{6,2},{7,3},{8,4},{9,5... | collective-permute-start | bytes 36872 | tf_op jit(solution)/shard_map/pushes_out/ppermute | solution.py:594
  104.9 1.8 %collective-permute-start.5 = (f32[24,128]{1,0:T(8,128)S(1)}, f32[24,128]{1,0:T(8,128)S(1)}, u32[]{:S(2)}, u32[]{:S(2)}) collective-permute-start(f32[24,128]{1,0:T(8,128)S(1)} %get-tuple-element.22), channel_id=1, source_target_pairs={{0,253},{1,254},{2,255},{3,0},{4,1},{5,2},{6,3},{7,4},{8,5},{9,6},... | collective-permute-start | bytes 36872 | tf_op jit(solution)/shard_map/pushes_out/ppermute | solution.py:594
  106.8 0.9 collective-permute-start.6
  107.7 2.6 %collective-permute-start.7 = (f32[24,128]{1,0:T(8,128)S(1)}, f32[24,128]{1,0:T(8,128)S(1)}, u32[]{:S(2)}, u32[]{:S(2)}) collective-permute-start(f32[24,128]{1,0:T(8,128)S(1)} %get-tuple-element.24), channel_id=1, source_target_pairs={{0,255},{1,0},{2,1},{3,2},{4,3},{5,4},{6,5},{7,6},{8,7},{9,8},{10,... | collective-permute-start | bytes 36872 | tf_op jit(solution)/shard_map/pushes_out/ppermute | solution.py:594
  110.3 0.4 collective-permute-start.8
  110.6 0.0 collective-permute-done.4.s0
  110.6 1.4 %collective-permute-start.9 = (f32[24,128]{1,0:T(8,128)S(1)}, f32[24,128]{1,0:T(8,128)S(1)}, u32[]{:S(2)}, u32[]{:S(2)}) collective-permute-start(f32[24,128]{1,0:T(8,128)S(1)} %get-tuple-element.27), channel_id=1, source_target_pairs={{0,2},{1,3},{2,4},{3,5},{4,6},{5,7},{6,8},{7,9},{8,10},{9,11},{10,... | collective-permute-start | bytes 36872 | tf_op jit(solution)/shard_map/pushes_out/ppermute | solution.py:594
  112.0 0.0 collective-permute-done.5.s1
  112.0 0.3 collective-permute-start.10
  112.4 0.0 collective-permute-done.6.s2
  112.4 0.0 collective-permute-done.7.s3
  112.4 2.5 %collective-permute-done.8.s5 = f32[24,128]{1,0:T(8,128)S(1)} collective-permute-done((f32[24,128]{1,0:T(8,128)S(1)}, f32[24,128]{1,0:T(8,128)S(1)}, u32[]{:S(2)}, u32[]{:S(2)}) %collective-permute-start.8) | collective-permute-done | bytes 12320 | tf_op jit(solution)/shard_map/pushes_out/ppermute | solution.py:594
  114.9 0.0 collective-permute-done.9.s6
  114.9 5.2 %collective-permute-done.10.s7 = f32[24,128]{1,0:T(8,128)S(1)} collective-permute-done((f32[24,128]{1,0:T(8,128)S(1)}, f32[24,128]{1,0:T(8,128)S(1)}, u32[]{:S(2)}, u32[]{:S(2)}) %collective-permute-start.10) | collective-permute-done | bytes 12320 | tf_op jit(solution)/shard_map/pushes_out/ppermute | solution.py:594
  120.0 0.0 copy-done.1
  120.0 0.0 copy-done.2
  120.0 0.0 copy-done.3
  120.0 0.0 copy-done.4
  120.1 0.0 copy-done.5
  120.1 0.0 copy-done.6
  120.1 0.0 copy-done.7
  120.1 0.0 copy-done.8
  120.1 1.5 %force.1 = f32[3,512]{1,0:T(4,128)} custom-call(f32[24,128]{1,0:T(8,128)S(1)} %collective-permute-done.4.s0, f32[24,128]{1,0:T(8,128)S(1)} %collective-permute-done.5.s1, f32[24,128]{1,0:T(8,128)S(1)} %collective-permute-done.6.s2, f32[24,128]{1,0:T(8,128)S(1)} %collective-permute-done.7.s3, f32[24,128]{1,0:T(8,128)S(1)} %get-tuple-element.25.s4, ...), custom_call_target="tpu_custom_call" | custom-call | bytes 4194304 | tf_op jit(solution)/shard_map/force/pallas_call | solution.py:559
  (1 shorter events, 0.0 us)
Async XLA Ops:
  0.6 62.5 %copy-start.10 = (bf16[4,256,256]{2,1,0:T(8,128)(2,1)S(1)}, bf16[4,256,256]{2,1,0:T(8,128)(2,1)}, u32[]{:S(2)}) copy-start(bf16[4,256,256]{2,1,0:T(8,128)(2,1)} %constant.23.clone.table_ref) | copy-start | bytes 1572868
  0.6 54.5 %copy-start = (f32[128,4,512]{2,1,0:T(4,128)S(1)}, f32[128,4,512]{2,1,0:T(4,128)}, u32[]{:S(2)}) copy-start(f32[128,4,512]{2,1,0:T(4,128)} %kept_ref.1) | copy-start | bytes 3145732
  8.0 21.3 %copy-start.12 = (f32[112,128]{1,0:T(8,128)}, f32[112,128]{1,0:T(8,128)S(1)}, u32[]{:S(2)}) copy-start(f32[112,128]{1,0:T(8,128)S(1)} %all-gather) | copy-start | bytes 172036
  8.0 9.8 %collective-permute-start.2 = (f32[2,56,128]{2,1,0:T(8,128)S(1)}, f32[2,56,128]{2,1,0:T(8,128)S(1)}, u32[]{:S(2)}, u32[]{:S(2)}) collective-permute-start(f32[2,56,128]{2,1,0:T(8,128)S(1)} %bitcast.20), channel_id=1, source_target_pairs={{5,0},{252,1},{9,4},{0,5},{13,8},{4,9},{17,12},{8,13},{21,16},{12,... | collective-permute-start | bytes 172040 | tf_op jit(solution)/shard_map/particles_in/ppermute | solution.py:626
  8.6 9.1 %collective-permute-start.1 = (f32[2,56,128]{2,1,0:T(8,128)S(1)}, f32[2,56,128]{2,1,0:T(8,128)S(1)}, u32[]{:S(2)}, u32[]{:S(2)}) collective-permute-start(f32[2,56,128]{2,1,0:T(8,128)S(1)} %bitcast.21), channel_id=1, source_target_pairs={{252,0},{6,2},{253,1},{7,3},{0,4},{10,6},{1,5},{11,7},{4,8},{14,10... | collective-permute-start | bytes 172040 | tf_op jit(solution)/shard_map/particles_in/ppermute | solution.py:626
  15.9 4.5 %collective-permute-start = (f32[2,56,128]{2,1,0:T(8,128)S(1)}, f32[2,56,128]{2,1,0:T(8,128)S(1)}, u32[]{:S(2)}, u32[]{:S(2)}) collective-permute-start(f32[2,56,128]{2,1,0:T(8,128)S(1)} %bitcast.22), channel_id=1, source_target_pairs={{253,0},{3,2},{0,1},{6,3},{1,4},{7,6},{4,5},{10,7},{5,8},{11,10},{... | collective-permute-start | bytes 172040 | tf_op jit(solution)/shard_map/particles_in/ppermute | solution.py:626
  37.4 25.8 %all-to-all-start = ((bf16[256,8,128]{2,1,0:T(8,128)(2,1)}), bf16[256,8,128]{2,1,0:T(8,128)(2,1)S(1)}, u32[]{:S(2)}, u32[]{:S(2)}) async-start(bf16[256,8,128]{2,1,0:T(8,128)(2,1)} %bitcast.19), calls=%async_computation | async-start | bytes 1048576 | tf_op jit(solution)/shard_map/to_columns/all_to_all | solution.py:685
  42.8 12.3 %collective-permute-start.3 = (bf16[128,4,256]{2,1,0:T(4,128)(2,1)}, bf16[128,4,256]{2,1,0:T(4,128)(2,1)S(1)}, u32[]{:S(2)}, u32[]{:S(2)}) collective-permute-start(bf16[128,4,256]{2,1,0:T(4,128)(2,1)} %get-tuple-element.19), channel_id=1, source_target_pairs={{0,1},{1,0},{2,3},{3,2},{4,5},{5,4},{6,7},{7,6},{8,9},{9,8},{10,11... | collective-permute-start | bytes 786440 | tf_op jit(solution)/shard_map/influence_swap/ppermute | solution.py:683
  66.0 27.4 %all-to-all-start.1 = ((bf16[256,8,128]{2,1,0:T(8,128)(2,1)}), bf16[256,8,128]{2,1,0:T(8,128)(2,1)S(1)}, u32[]{:S(2)}, u32[]{:S(2)}) async-start(bf16[256,8,128]{2,1,0:T(8,128)(2,1)} %bitcast.11), calls=%async_computation.1 | async-start | bytes 1048576 | tf_op jit(solution)/shard_map/to_planes/all_to_all | solution.py:723
  73.2 20.2 %copy-start.9 = (bf16[512,512]{1,0:T(8,128)(2,1)S(1)}, bf16[512,512]{1,0:T(8,128)(2,1)}, u32[]{:S(2)}) copy-start(bf16[512,512]{1,0:T(8,128)(2,1)} %constant.22.clone.table_at) | copy-start | bytes 1572868
  73.2 20.2 %copy-start.11 = (f32[6,24,128]{2,1,0:T(8,128)S(1)}, f32[6,24,128]{2,1,0:T(8,128)}, u32[]{:S(2)}) copy-start(f32[6,24,128]{2,1,0:T(8,128)} %get-tuple-element.20.refs_0_.part_ref) | copy-start | bytes 221188
  87.4 32.6 %copy-start.1 = (f32[240,384]{1,0:T(8,128)S(1)}, f32[240,384]{1,0:T(8,128)}, u32[]{:S(2)}) copy-start(f32[240,384]{1,0:T(8,128)} %get-tuple-element.30.h1_ref) | copy-start | bytes 1105924
  87.4 32.6 %copy-start.2 = (f32[240,384]{1,0:T(8,128)S(1)}, f32[240,384]{1,0:T(8,128)}, u32[]{:S(2)}) copy-start(f32[240,384]{1,0:T(8,128)} %get-tuple-element.31.t2_ref) | copy-start | bytes 1105924
  87.4 32.6 %copy-start.3 = (f32[56,128]{1,0:T(8,128)S(1)}, f32[56,128]{1,0:T(8,128)}, u32[]{:S(2)}) copy-start(f32[56,128]{1,0:T(8,128)} %pack.1.own_ref) | copy-start | bytes 86020
  87.4 32.6 %copy-start.4 = (bf16[240,240]{1,0:T(8,128)(2,1)S(1)}, bf16[240,240]{1,0:T(8,128)(2,1)}, u32[]{:S(2)}) copy-start(bf16[240,240]{1,0:T(8,128)(2,1)} %w2_ref.1) | copy-start | bytes 345604
  87.4 32.6 %copy-start.5 = (bf16[128,240]{0,1:T(8,128)(2,1)S(1)}, bf16[128,240]{0,1:T(8,128)(2,1)}, u32[]{:S(2)}) copy-start(bf16[128,240]{0,1:T(8,128)(2,1)} %param.22) | copy-start | bytes 184324
  87.4 32.6 %copy-start.6 = (f32[2,56,128]{2,1,0:T(8,128)S(1)}, f32[2,56,128]{2,1,0:T(8,128)}, u32[]{:S(2)}) copy-start(f32[2,56,128]{2,1,0:T(8,128)} %get-tuple-element.29.beside_ref) | copy-start | bytes 172036
  87.4 32.6 %copy-start.7 = (f32[3,384]{1,0:T(4,128)S(1)}, f32[3,384]{1,0:T(4,128)}, u32[]{:S(2)}) copy-start(f32[3,384]{1,0:T(4,128)} %get-tuple-element.32.to_ref) | copy-start | bytes 13828
  87.4 32.6 %copy-start.8 = (bf16[240,3]{0,1:T(4,128)(2,1)S(1)}, bf16[240,3]{0,1:T(4,128)(2,1)}, u32[]{:S(2)}) copy-start(bf16[240,3]{0,1:T(4,128)(2,1)} %param.26) | copy-start | bytes 4324
  103.2 7.4 %collective-permute-start.4 = (f32[24,128]{1,0:T(8,128)S(1)}, f32[24,128]{1,0:T(8,128)S(1)}, u32[]{:S(2)}, u32[]{:S(2)}) collective-permute-start(f32[24,128]{1,0:T(8,128)S(1)} %get-tuple-element.21), channel_id=1, source_target_pairs={{0,252},{1,253},{2,254},{3,255},{4,0},{5,1},{6,2},{7,3},{8,4},{9,5... | collective-permute-start | bytes 36872 | tf_op jit(solution)/shard_map/pushes_out/ppermute | solution.py:594
  104.9 7.1 %collective-permute-start.5 = (f32[24,128]{1,0:T(8,128)S(1)}, f32[24,128]{1,0:T(8,128)S(1)}, u32[]{:S(2)}, u32[]{:S(2)}) collective-permute-start(f32[24,128]{1,0:T(8,128)S(1)} %get-tuple-element.22), channel_id=1, source_target_pairs={{0,253},{1,254},{2,255},{3,0},{4,1},{5,2},{6,3},{7,4},{8,5},{9,6},... | collective-permute-start | bytes 36872 | tf_op jit(solution)/shard_map/pushes_out/ppermute | solution.py:594
  106.8 5.6 %collective-permute-start.6 = (f32[24,128]{1,0:T(8,128)S(1)}, f32[24,128]{1,0:T(8,128)S(1)}, u32[]{:S(2)}, u32[]{:S(2)}) collective-permute-start(f32[24,128]{1,0:T(8,128)S(1)} %get-tuple-element.23), channel_id=1, source_target_pairs={{0,254},{1,255},{2,0},{3,1},{4,2},{5,3},{6,4},{7,5},{8,6},{9,7},{1... | collective-permute-start | bytes 36872 | tf_op jit(solution)/shard_map/pushes_out/ppermute | solution.py:594
  107.7 4.7 %collective-permute-start.7 = (f32[24,128]{1,0:T(8,128)S(1)}, f32[24,128]{1,0:T(8,128)S(1)}, u32[]{:S(2)}, u32[]{:S(2)}) collective-permute-start(f32[24,128]{1,0:T(8,128)S(1)} %get-tuple-element.24), channel_id=1, source_target_pairs={{0,255},{1,0},{2,1},{3,2},{4,3},{5,4},{6,5},{7,6},{8,7},{9,8},{10,... | collective-permute-start | bytes 36872 | tf_op jit(solution)/shard_map/pushes_out/ppermute | solution.py:594
  110.3 4.6 %collective-permute-start.8 = (f32[24,128]{1,0:T(8,128)S(1)}, f32[24,128]{1,0:T(8,128)S(1)}, u32[]{:S(2)}, u32[]{:S(2)}) collective-permute-start(f32[24,128]{1,0:T(8,128)S(1)} %get-tuple-element.26), channel_id=1, source_target_pairs={{0,1},{1,2},{2,3},{3,4},{4,5},{5,6},{6,7},{7,8},{8,9},{9,10},{10,1... | collective-permute-start | bytes 36872 | tf_op jit(solution)/shard_map/pushes_out/ppermute | solution.py:594
  110.6 4.2 %collective-permute-start.9 = (f32[24,128]{1,0:T(8,128)S(1)}, f32[24,128]{1,0:T(8,128)S(1)}, u32[]{:S(2)}, u32[]{:S(2)}) collective-permute-start(f32[24,128]{1,0:T(8,128)S(1)} %get-tuple-element.27), channel_id=1, source_target_pairs={{0,2},{1,3},{2,4},{3,5},{4,6},{5,7},{6,8},{7,9},{8,10},{9,11},{10,... | collective-permute-start | bytes 36872 | tf_op jit(solution)/shard_map/pushes_out/ppermute | solution.py:594
  112.0 8.0 %collective-permute-start.10 = (f32[24,128]{1,0:T(8,128)S(1)}, f32[24,128]{1,0:T(8,128)S(1)}, u32[]{:S(2)}, u32[]{:S(2)}) collective-permute-start(f32[24,128]{1,0:T(8,128)S(1)} %get-tuple-element.28), channel_id=1, source_target_pairs={{0,3},{1,4},{2,5},{3,6},{4,7},{5,8},{6,9},{7,10},{8,11},{9,12},{10... | collective-permute-start | bytes 36872 | tf_op jit(solution)/shard_map/pushes_out/ppermute | solution.py:594

commit v4 on v3

--- a/solution.py
+++ b/solution.py
@@ -399,16 +399,7 @@
     r_s, field_s, va_s, vb_s, push_s, pot_s, wx_ref, wy_ref, table_ref, sems,
 ):
     outs = (o0, o1, o2, o3, o4, o5, o6, o7)
-    half = pl.ds(0, 10), pl.ds(10, 12)
-    (table_copy,) = fetch(((table_at, table_ref),), sems, 4)
-    copies = fetch(
-        (
-            (wx_at, wx_ref),
-            (wy_at.at[half[0]], wy_ref.at[half[0]]),
-            (wy_at.at[half[1]], wy_ref.at[half[1]]),
-        ),
-        sems,
-    )
+    table_copy, wx_copy = fetch(((table_at, table_ref), (wx_at, wx_ref)), sems)
     lower = lax.broadcasted_iota(jnp.int32, (64, 8, 128), 1) < 4
     for g in range(2):
         even = y_ref[:, 0, 8 * g : 8 * g + 8, :].astype(F32)
@@ -417,13 +408,16 @@
         tile1 = jnp.where(lower, pltpu.roll(even, 4, 1), odd)
         r_s[:, 256 * g : 256 * g + 128] = tile0.reshape(512, 128).astype(BF)
         r_s[:, 256 * g + 128 : 256 * g + 256] = tile1.reshape(512, 128).astype(BF)
+    spans = ((0, 4), (4, 10), (10, 16), (16, 22))
+    pieces = [pl.ds(first, last - first) for first, last in spans]
+    wy_copies = fetch(tuple((wy_at.at[piece], wy_ref.at[piece]) for piece in pieces), sems, 3)
     table_copy.wait()
     hh = table_ref[...]
     inner = dot(hh, r_s[...])
     inner = inner.astype(BF)
     potential = dot(inner, hh) * (1.0 / 67108864.0)
     pot_s[...] = potential
-    pot_copy = pltpu.make_async_copy(pot_s, pot_at.at[0], sems.at[3])
+    pot_copy = pltpu.make_async_copy(pot_s, pot_at.at[0], sems.at[2])
     pot_copy.start()
     field_s[...] = potential.T.astype(BF)
 
@@ -452,12 +446,11 @@
         gather(row + 1, vb_s)
         return carry
 
-    copies[0].wait()
+    wx_copy.wait()
     va_s[...] = dot(field_s[...], wx_ref[0])
-    copies[1].wait()
-    lax.fori_loop(0, 5, probe, 0)
-    copies[2].wait()
-    lax.fori_loop(5, 11, probe, 0)
+    for (first, last), copy in zip(spans, wy_copies):
+        copy.wait()
+        lax.fori_loop(first // 2, last // 2, probe, 0)
     pot_copy.wait()
     charge = part_ref[5]
     charge_z = charge * spline(part_ref[4])
@@ -738,7 +731,7 @@
                 pltpu.VMEM((22, NX, 256), BF),
                 pltpu.VMEM((22, NY, 256), F32),
                 pltpu.VMEM((NX, NX), BF),
-                pltpu.SemaphoreType.DMA((5,)),
+                pltpu.SemaphoreType.DMA((7,)),
             ),
             first=HB,
             limit=52,

time: 122 us -> 121 us (level)
  no operation moved by 1% of the time
where the time goes in v4:
time: 121 us
  Pallas kernels  37.8 us (31%)
  starting transfers between devices  34.5 us (29%)
  waiting for transfers between devices  33 us (27%)
  blocking collectives  13.7 us (11%)
  between operations  1.59 us (1%)
    pallas_call x8, Pallas kernels, call(): pl.pallas_call(kernel, out_shape=outs, in_specs=[spaces.get(n, VM) for n...  37.8 us
    ppermute x3, starting transfers between devices, body(): far = [lax.ppermute(pair, both, chip_steps(kind)) for kind in range(3)]  9.76 us
    ppermute x1, waiting for transfers between devices, body(): taken = lax.ppermute(given, 'grp', [(0, 1), (1, 0)])  9.32 us
    ppermute x7, starting transfers between devices, from_device(): return lax.ppermute(value, both, pairs)  9.14 us
    all_gather x1, blocking collectives, body(): lax.all_gather(jnp.concatenate(far, axis=0), 'core').reshape(12, 56, 128)  8.77 us
    ppermute x7, waiting for transfers between devices, from_device(): return lax.ppermute(value, both, pairs)  7.68 us
    all_to_all x1, waiting for transfers between devices, body(): lax.all_to_all(columns.reshape(256, 8, 128), both, 0, 0, tiled=True)  7.32 us
    all_to_all x1, starting transfers between devices, body(): rows = lax.all_to_all(rows.reshape(256, 8, 128), both, 0, 0, tiled=True)  7.17 us
  transfers between devices with their start and end apart: 13, of which 6 were waited for; matrix products, arithmetic and copies ran while one was open for 0% of the time, Pallas kernels for 12%

profile of v4, /device:TPU:1, one launch (start us, length us, event | category | flops | bytes accessed | tf_op | source)
XLA Modules:
  0.0 120.7 jit_solution(10371530700975748249)
XLA Ops:
  0.6 0.0 copy-start.10
  0.6 0.0 copy-start
  1.4 1.6 %pack.1.own_ref = f32[56,128]{1,0:T(8,128)} custom-call(s32[1]{0:T(128)S(6)} %copy.17.count_ref, s32[3,512]{1,0:T(4,128)} %base_at.1, f32[3,512]{1,0:T(4,128)} %frac_at.1, f32[4,128]{1,0:T(4,128)} %bitcast.24, s32[1,128]{1,0:T(1,128)} %bitcast.25, s32[32,128]{1,0:T(8,128)} %near_at.1), custom_call_target="tpu_custom_call" | custom-call | bytes 4194304 | tf_op jit(solution)/shard_map/pack/pallas_call | solution.py:552
  3.0 5.0 %all-gather = f32[112,128]{1,0:T(8,128)S(1)} all-gather(f32[56,128]{1,0:T(8,128)} %pack.1.own_ref), channel_id=2, replica_groups=mesh['row'=64,'core'=2,'grp'=2] {'core'}, dimensions={0}, use_global_device_ids=true | all-gather | bytes 86016 | tf_op jit(solution)/shard_map/particles_in/all_gather | solution.py:618
  8.0 0.0 copy-start.12
  8.0 0.7 collective-permute-start.2
  8.6 7.3 %collective-permute-start.1 = (f32[2,56,128]{2,1,0:T(8,128)S(1)}, f32[2,56,128]{2,1,0:T(8,128)S(1)}, u32[]{:S(2)}, u32[]{:S(2)}) collective-permute-start(f32[2,56,128]{2,1,0:T(8,128)S(1)} %bitcast.21), channel_id=1, source_target_pairs={{252,0},{6,2},{253,1},{7,3},{0,4},{10,6},{1,5},{11,7},{4,8},{14,10... | collective-permute-start | bytes 172040 | tf_op jit(solution)/shard_map/particles_in/ppermute | solution.py:619
  15.9 1.8 %collective-permute-start = (f32[2,56,128]{2,1,0:T(8,128)S(1)}, f32[2,56,128]{2,1,0:T(8,128)S(1)}, u32[]{:S(2)}, u32[]{:S(2)}) collective-permute-start(f32[2,56,128]{2,1,0:T(8,128)S(1)} %bitcast.22), channel_id=1, source_target_pairs={{253,0},{3,2},{0,1},{6,3},{1,4},{7,6},{4,5},{10,7},{5,8},{11,10},{... | collective-permute-start | bytes 172040 | tf_op jit(solution)/shard_map/particles_in/ppermute | solution.py:619
  17.7 0.0 collective-permute-done.2
  17.8 0.0 collective-permute-done.1
  17.8 2.7 %collective-permute-done = f32[2,56,128]{2,1,0:T(8,128)S(1)} collective-permute-done((f32[2,56,128]{2,1,0:T(8,128)S(1)}, f32[2,56,128]{2,1,0:T(8,128)S(1)}, u32[]{:S(2)}, u32[]{:S(2)}) %collective-permute-start) | collective-permute-done | bytes 57376 | tf_op jit(solution)/shard_map/particles_in/ppermute | solution.py:619
  20.5 8.8 %all-gather.1.far_ref = f32[12,56,128]{2,1,0:T(8,128)} all-gather(f32[6,56,128]{2,1,0:T(8,128)S(1)} %pad_maximum_fusion), channel_id=3, replica_groups=mesh['row'=64,'core'=2,'grp'=2] {'core'}, dimensions={0}, use_global_device_ids=true | all-gather | bytes 516096 | tf_op jit(solution)/shard_map/particles_in/all_gather | solution.py:620
  29.3 0.0 copy-done.12
  29.3 8.1 %spread.1 = (bf16[64,2,16,128]{3,2,1,0:T(8,128)(2,1)}, f32[6,24,128]{2,1,0:T(8,128)}, f32[240,384]{1,0:T(8,128)}, f32[240,384]{1,0:T(8,128)}, f32[3,384]{1,0:T(4...) custom-call(s32[1]{0:T(128)} %bitcast.place_ref.group_ref, f32[12,56,128]{2,1,0:T(8,128)} %all-gather.1.far_ref, ...), custom_call_target="tpu_custom_call" | custom-call | flops 4000000000 | bytes 4194304 | tf_op jit(solution)/shard_map/spread/pallas_call | solution.py:552
  37.4 5.4 %all-to-all-start = ((bf16[256,8,128]{2,1,0:T(8,128)(2,1)}), bf16[256,8,128]{2,1,0:T(8,128)(2,1)S(1)}, u32[]{:S(2)}, u32[]{:S(2)}) async-start(bf16[256,8,128]{2,1,0:T(8,128)(2,1)} %bitcast.19), calls=%async_computation | async-start | bytes 1048576 | tf_op jit(solution)/shard_map/to_columns/all_to_all | solution.py:678
  42.8 3.0 %collective-permute-start.3 = (bf16[128,4,256]{2,1,0:T(4,128)(2,1)}, bf16[128,4,256]{2,1,0:T(4,128)(2,1)S(1)}, u32[]{:S(2)}, u32[]{:S(2)}) collective-permute-start(bf16[128,4,256]{2,1,0:T(4,128)(2,1)} %get-tuple-element.19), channel_id=1, source_target_pairs={{0,1},{1,0},{2,3},{3,2},{4,5},{5,4},{6,7},{7,6},{8,9},{9,8},{10,11... | collective-permute-start | bytes 786440 | tf_op jit(solution)/shard_map/influence_swap/ppermute | solution.py:676
  45.8 9.3 %collective-permute-done.3 = bf16[128,4,256]{2,1,0:T(4,128)(2,1)S(1)} collective-permute-done((bf16[128,4,256]{2,1,0:T(4,128)(2,1)}, bf16[128,4,256]{2,1,0:T(4,128)(2,1)S(1)}, u32[]{:S(2)}, u32[]{:S(2)}) %collective-permute-start.3) | collective-permute-done | bytes 262176 | tf_op jit(solution)/shard_map/influence_swap/ppermute | solution.py:676
  55.1 0.1 convert_element_type.3.taken_ref
  55.2 0.0 copy-done
  55.2 0.7 influence.1.infl_ref
  55.9 7.3 %all-to-all-done = bf16[256,8,128]{2,1,0:T(8,128)(2,1)S(1)} async-done(((bf16[256,8,128]{2,1,0:T(8,128)(2,1)}), bf16[256,8,128]{2,1,0:T(8,128)(2,1)S(1)}, u32[]{:S(2)}, u32[]{:S(2)}) %all-to-all-start) | async-done | bytes 524320 | tf_op jit(solution)/shard_map/to_columns/all_to_all | solution.py:678
  63.2 0.0 copy-done.10
  63.2 2.8 %depth.1 = bf16[128,16,128]{2,1,0:T(8,128)(2,1)} custom-call(bf16[128,16,128]{2,1,0:T(8,128)(2,1)S(1)} %bitcast.13, f32[256,1024]{1,0:T(8,128)S(1)} %influence.1.infl_ref, bf16[4,256,256]{2,1,0:T(8,128)(2,1)S(1)} %copy-done.10), custom_call_target="tpu_custom_call" | custom-call | flops 800000000 | bytes 4194304 | tf_op jit(solution)/shard_map/depth/pallas_call | solution.py:552
  66.0 7.2 %all-to-all-start.1 = ((bf16[256,8,128]{2,1,0:T(8,128)(2,1)}), bf16[256,8,128]{2,1,0:T(8,128)(2,1)S(1)}, u32[]{:S(2)}, u32[]{:S(2)}) async-start(bf16[256,8,128]{2,1,0:T(8,128)(2,1)} %bitcast.11), calls=%async_computation.1 | async-start | bytes 1048576 | tf_op jit(solution)/shard_map/to_planes/all_to_all | solution.py:716
  73.2 0.0 copy-start.9
  73.2 0.0 copy-start.11
  73.2 6.4 %lookup_x.1.wx_at = bf16[22,512,256]{2,1,0:T(8,128)(2,1)} custom-call(f32[6,24,128]{2,1,0:T(8,128)} %get-tuple-element.20.refs_0_.part_ref), custom_call_target="tpu_custom_call" | custom-call | flops 4000000000 | bytes 4194304 | tf_op jit(solution)/shard_map/lookup_x/pallas_call | solution.py:552
  79.6 7.8 %lookup_y.1.wy_at = f32[22,512,256]{2,1,0:T(8,128)} custom-call(f32[6,24,128]{2,1,0:T(8,128)} %get-tuple-element.20.refs_0_.part_ref), custom_call_target="tpu_custom_call" | custom-call | flops 4000000000 | bytes 4194304 | tf_op jit(solution)/shard_map/lookup_y/pallas_call | solution.py:552
  87.4 0.0 copy-start.1
  87.4 0.0 copy-start.2
  87.4 0.0 copy-start.3
  87.4 0.0 copy-start.4
  87.4 0.0 copy-start.5
  87.4 0.0 copy-start.6
  87.4 0.0 copy-start.7
  87.4 0.0 copy-start.8
  87.5 6.0 %all-to-all-done.1 = bf16[256,8,128]{2,1,0:T(8,128)(2,1)S(1)} async-done(((bf16[256,8,128]{2,1,0:T(8,128)(2,1)}), bf16[256,8,128]{2,1,0:T(8,128)(2,1)S(1)}, u32[]{:S(2)}, u32[]{:S(2)}) %all-to-all-start.1) | async-done | bytes 524320 | tf_op jit(solution)/shard_map/to_planes/all_to_all | solution.py:716
  93.4 0.0 copy-done.9
  93.4 0.0 copy-done.11
  93.4 8.9 %probe.1 = (f32[1,512,512]{2,1,0:T(8,128)}, f32[24,128]{1,0:T(8,128)S(1)}, f32[24,128]{1,0:T(8,128)S(1)}, f32[24,128]{1,0:T(8,128)S(1)}, f32[24,128]{1,0:T(8,128...) custom-call(bf16[64,2,16,128]{3,2,1,0:T(8,128)(2,1)S(1)} %bitcast.14, ...), custom_call_target="tpu_custom_call" | custom-call | flops 5000000000 | bytes 4194304 | tf_op jit(solution)/shard_map/probe/pallas_call | solution.py:552
  102.3 1.7 %collective-permute-start.4 = (f32[24,128]{1,0:T(8,128)S(1)}, f32[24,128]{1,0:T(8,128)S(1)}, u32[]{:S(2)}, u32[]{:S(2)}) collective-permute-start(f32[24,128]{1,0:T(8,128)S(1)} %get-tuple-element.21), channel_id=1, source_target_pairs={{0,252},{1,253},{2,254},{3,255},{4,0},{5,1},{6,2},{7,3},{8,4},{9,5... | collective-permute-start | bytes 36872 | tf_op jit(solution)/shard_map/pushes_out/ppermute | solution.py:587
  104.1 1.8 %collective-permute-start.5 = (f32[24,128]{1,0:T(8,128)S(1)}, f32[24,128]{1,0:T(8,128)S(1)}, u32[]{:S(2)}, u32[]{:S(2)}) collective-permute-start(f32[24,128]{1,0:T(8,128)S(1)} %get-tuple-element.22), channel_id=1, source_target_pairs={{0,253},{1,254},{2,255},{3,0},{4,1},{5,2},{6,3},{7,4},{8,5},{9,6},... | collective-permute-start | bytes 36872 | tf_op jit(solution)/shard_map/pushes_out/ppermute | solution.py:587
  105.9 0.9 collective-permute-start.6
  106.8 2.6 %collective-permute-start.7 = (f32[24,128]{1,0:T(8,128)S(1)}, f32[24,128]{1,0:T(8,128)S(1)}, u32[]{:S(2)}, u32[]{:S(2)}) collective-permute-start(f32[24,128]{1,0:T(8,128)S(1)} %get-tuple-element.24), channel_id=1, source_target_pairs={{0,255},{1,0},{2,1},{3,2},{4,3},{5,4},{6,5},{7,6},{8,7},{9,8},{10,... | collective-permute-start | bytes 36872 | tf_op jit(solution)/shard_map/pushes_out/ppermute | solution.py:587
  109.4 0.4 collective-permute-start.8
  109.8 0.0 collective-permute-done.4.s0
  109.8 1.4 %collective-permute-start.9 = (f32[24,128]{1,0:T(8,128)S(1)}, f32[24,128]{1,0:T(8,128)S(1)}, u32[]{:S(2)}, u32[]{:S(2)}) collective-permute-start(f32[24,128]{1,0:T(8,128)S(1)} %get-tuple-element.27), channel_id=1, source_target_pairs={{0,2},{1,3},{2,4},{3,5},{4,6},{5,7},{6,8},{7,9},{8,10},{9,11},{10,... | collective-permute-start | bytes 36872 | tf_op jit(solution)/shard_map/pushes_out/ppermute | solution.py:587
  111.2 0.0 collective-permute-done.5.s1
  111.2 0.3 collective-permute-start.10
  111.5 0.0 collective-permute-done.6.s2
  111.5 0.0 collective-permute-done.7.s3
  111.5 2.5 %collective-permute-done.8.s5 = f32[24,128]{1,0:T(8,128)S(1)} collective-permute-done((f32[24,128]{1,0:T(8,128)S(1)}, f32[24,128]{1,0:T(8,128)S(1)}, u32[]{:S(2)}, u32[]{:S(2)}) %collective-permute-start.8) | collective-permute-done | bytes 12320 | tf_op jit(solution)/shard_map/pushes_out/ppermute | solution.py:587
  114.0 0.0 collective-permute-done.9.s6
  114.0 5.2 %collective-permute-done.10.s7 = f32[24,128]{1,0:T(8,128)S(1)} collective-permute-done((f32[24,128]{1,0:T(8,128)S(1)}, f32[24,128]{1,0:T(8,128)S(1)}, u32[]{:S(2)}, u32[]{:S(2)}) %collective-permute-start.10) | collective-permute-done | bytes 12320 | tf_op jit(solution)/shard_map/pushes_out/ppermute | solution.py:587
  119.2 0.0 copy-done.1
  119.2 0.0 copy-done.2
  119.2 0.0 copy-done.3
  119.2 0.0 copy-done.4
  119.2 0.0 copy-done.5
  119.2 0.0 copy-done.6
  119.2 0.0 copy-done.7
  119.2 0.0 copy-done.8
  119.2 1.5 %force.1 = f32[3,512]{1,0:T(4,128)} custom-call(f32[24,128]{1,0:T(8,128)S(1)} %collective-permute-done.4.s0, f32[24,128]{1,0:T(8,128)S(1)} %collective-permute-done.5.s1, f32[24,128]{1,0:T(8,128)S(1)} %collective-permute-done.6.s2, f32[24,128]{1,0:T(8,128)S(1)} %collective-permute-done.7.s3, f32[24,128]{1,0:T(8,128)S(1)} %get-tuple-element.25.s4, ...), custom_call_target="tpu_custom_call" | custom-call | bytes 4194304 | tf_op jit(solution)/shard_map/force/pallas_call | solution.py:552
  (1 shorter events, 0.0 us)
Async XLA Ops:
  0.6 62.5 %copy-start.10 = (bf16[4,256,256]{2,1,0:T(8,128)(2,1)S(1)}, bf16[4,256,256]{2,1,0:T(8,128)(2,1)}, u32[]{:S(2)}) copy-start(bf16[4,256,256]{2,1,0:T(8,128)(2,1)} %constant.23.clone.table_ref) | copy-start | bytes 1572868
  0.6 54.5 %copy-start = (f32[128,4,512]{2,1,0:T(4,128)S(1)}, f32[128,4,512]{2,1,0:T(4,128)}, u32[]{:S(2)}) copy-start(f32[128,4,512]{2,1,0:T(4,128)} %kept_ref.1) | copy-start | bytes 3145732
  8.0 21.3 %copy-start.12 = (f32[112,128]{1,0:T(8,128)}, f32[112,128]{1,0:T(8,128)S(1)}, u32[]{:S(2)}) copy-start(f32[112,128]{1,0:T(8,128)S(1)} %all-gather) | copy-start | bytes 172036
  8.0 9.8 %collective-permute-start.2 = (f32[2,56,128]{2,1,0:T(8,128)S(1)}, f32[2,56,128]{2,1,0:T(8,128)S(1)}, u32[]{:S(2)}, u32[]{:S(2)}) collective-permute-start(f32[2,56,128]{2,1,0:T(8,128)S(1)} %bitcast.20), channel_id=1, source_target_pairs={{5,0},{252,1},{9,4},{0,5},{13,8},{4,9},{17,12},{8,13},{21,16},{12,... | collective-permute-start | bytes 172040 | tf_op jit(solution)/shard_map/particles_in/ppermute | solution.py:619
  8.6 9.1 %collective-permute-start.1 = (f32[2,56,128]{2,1,0:T(8,128)S(1)}, f32[2,56,128]{2,1,0:T(8,128)S(1)}, u32[]{:S(2)}, u32[]{:S(2)}) collective-permute-start(f32[2,56,128]{2,1,0:T(8,128)S(1)} %bitcast.21), channel_id=1, source_target_pairs={{252,0},{6,2},{253,1},{7,3},{0,4},{10,6},{1,5},{11,7},{4,8},{14,10... | collective-permute-start | bytes 172040 | tf_op jit(solution)/shard_map/particles_in/ppermute | solution.py:619
  15.9 4.5 %collective-permute-start = (f32[2,56,128]{2,1,0:T(8,128)S(1)}, f32[2,56,128]{2,1,0:T(8,128)S(1)}, u32[]{:S(2)}, u32[]{:S(2)}) collective-permute-start(f32[2,56,128]{2,1,0:T(8,128)S(1)} %bitcast.22), channel_id=1, source_target_pairs={{253,0},{3,2},{0,1},{6,3},{1,4},{7,6},{4,5},{10,7},{5,8},{11,10},{... | collective-permute-start | bytes 172040 | tf_op jit(solution)/shard_map/particles_in/ppermute | solution.py:619
  37.4 25.8 %all-to-all-start = ((bf16[256,8,128]{2,1,0:T(8,128)(2,1)}), bf16[256,8,128]{2,1,0:T(8,128)(2,1)S(1)}, u32[]{:S(2)}, u32[]{:S(2)}) async-start(bf16[256,8,128]{2,1,0:T(8,128)(2,1)} %bitcast.19), calls=%async_computation | async-start | bytes 1048576 | tf_op jit(solution)/shard_map/to_columns/all_to_all | solution.py:678
  42.8 12.3 %collective-permute-start.3 = (bf16[128,4,256]{2,1,0:T(4,128)(2,1)}, bf16[128,4,256]{2,1,0:T(4,128)(2,1)S(1)}, u32[]{:S(2)}, u32[]{:S(2)}) collective-permute-start(bf16[128,4,256]{2,1,0:T(4,128)(2,1)} %get-tuple-element.19), channel_id=1, source_target_pairs={{0,1},{1,0},{2,3},{3,2},{4,5},{5,4},{6,7},{7,6},{8,9},{9,8},{10,11... | collective-permute-start | bytes 786440 | tf_op jit(solution)/shard_map/influence_swap/ppermute | solution.py:676
  66.0 27.4 %all-to-all-start.1 = ((bf16[256,8,128]{2,1,0:T(8,128)(2,1)}), bf16[256,8,128]{2,1,0:T(8,128)(2,1)S(1)}, u32[]{:S(2)}, u32[]{:S(2)}) async-start(bf16[256,8,128]{2,1,0:T(8,128)(2,1)} %bitcast.11), calls=%async_computation.1 | async-start | bytes 1048576 | tf_op jit(solution)/shard_map/to_planes/all_to_all | solution.py:716
  73.2 20.2 %copy-start.9 = (bf16[512,512]{1,0:T(8,128)(2,1)S(1)}, bf16[512,512]{1,0:T(8,128)(2,1)}, u32[]{:S(2)}) copy-start(bf16[512,512]{1,0:T(8,128)(2,1)} %constant.22.clone.table_at) | copy-start | bytes 1572868
  73.2 20.2 %copy-start.11 = (f32[6,24,128]{2,1,0:T(8,128)S(1)}, f32[6,24,128]{2,1,0:T(8,128)}, u32[]{:S(2)}) copy-start(f32[6,24,128]{2,1,0:T(8,128)} %get-tuple-element.20.refs_0_.part_ref) | copy-start | bytes 221188
  87.4 31.8 %copy-start.1 = (f32[240,384]{1,0:T(8,128)S(1)}, f32[240,384]{1,0:T(8,128)}, u32[]{:S(2)}) copy-start(f32[240,384]{1,0:T(8,128)} %get-tuple-element.30.h1_ref) | copy-start | bytes 1105924
  87.4 31.8 %copy-start.2 = (f32[240,384]{1,0:T(8,128)S(1)}, f32[240,384]{1,0:T(8,128)}, u32[]{:S(2)}) copy-start(f32[240,384]{1,0:T(8,128)} %get-tuple-element.31.t2_ref) | copy-start | bytes 1105924
  87.4 31.8 %copy-start.3 = (f32[56,128]{1,0:T(8,128)S(1)}, f32[56,128]{1,0:T(8,128)}, u32[]{:S(2)}) copy-start(f32[56,128]{1,0:T(8,128)} %pack.1.own_ref) | copy-start | bytes 86020
  87.4 31.8 %copy-start.4 = (bf16[240,240]{1,0:T(8,128)(2,1)S(1)}, bf16[240,240]{1,0:T(8,128)(2,1)}, u32[]{:S(2)}) copy-start(bf16[240,240]{1,0:T(8,128)(2,1)} %w2_ref.1) | copy-start | bytes 345604
  87.4 31.8 %copy-start.5 = (bf16[128,240]{0,1:T(8,128)(2,1)S(1)}, bf16[128,240]{0,1:T(8,128)(2,1)}, u32[]{:S(2)}) copy-start(bf16[128,240]{0,1:T(8,128)(2,1)} %param.22) | copy-start | bytes 184324
  87.4 31.8 %copy-start.6 = (f32[2,56,128]{2,1,0:T(8,128)S(1)}, f32[2,56,128]{2,1,0:T(8,128)}, u32[]{:S(2)}) copy-start(f32[2,56,128]{2,1,0:T(8,128)} %get-tuple-element.29.beside_ref) | copy-start | bytes 172036
  87.4 31.8 %copy-start.7 = (f32[3,384]{1,0:T(4,128)S(1)}, f32[3,384]{1,0:T(4,128)}, u32[]{:S(2)}) copy-start(f32[3,384]{1,0:T(4,128)} %get-tuple-element.32.to_ref) | copy-start | bytes 13828
  87.4 31.8 %copy-start.8 = (bf16[240,3]{0,1:T(4,128)(2,1)S(1)}, bf16[240,3]{0,1:T(4,128)(2,1)}, u32[]{:S(2)}) copy-start(bf16[240,3]{0,1:T(4,128)(2,1)} %param.26) | copy-start | bytes 4324
  102.3 7.4 %collective-permute-start.4 = (f32[24,128]{1,0:T(8,128)S(1)}, f32[24,128]{1,0:T(8,128)S(1)}, u32[]{:S(2)}, u32[]{:S(2)}) collective-permute-start(f32[24,128]{1,0:T(8,128)S(1)} %get-tuple-element.21), channel_id=1, source_target_pairs={{0,252},{1,253},{2,254},{3,255},{4,0},{5,1},{6,2},{7,3},{8,4},{9,5... | collective-permute-start | bytes 36872 | tf_op jit(solution)/shard_map/pushes_out/ppermute | solution.py:587
  104.1 7.1 %collective-permute-start.5 = (f32[24,128]{1,0:T(8,128)S(1)}, f32[24,128]{1,0:T(8,128)S(1)}, u32[]{:S(2)}, u32[]{:S(2)}) collective-permute-start(f32[24,128]{1,0:T(8,128)S(1)} %get-tuple-element.22), channel_id=1, source_target_pairs={{0,253},{1,254},{2,255},{3,0},{4,1},{5,2},{6,3},{7,4},{8,5},{9,6},... | collective-permute-start | bytes 36872 | tf_op jit(solution)/shard_map/pushes_out/ppermute | solution.py:587
  105.9 5.6 %collective-permute-start.6 = (f32[24,128]{1,0:T(8,128)S(1)}, f32[24,128]{1,0:T(8,128)S(1)}, u32[]{:S(2)}, u32[]{:S(2)}) collective-permute-start(f32[24,128]{1,0:T(8,128)S(1)} %get-tuple-element.23), channel_id=1, source_target_pairs={{0,254},{1,255},{2,0},{3,1},{4,2},{5,3},{6,4},{7,5},{8,6},{9,7},{1... | collective-permute-start | bytes 36872 | tf_op jit(solution)/shard_map/pushes_out/ppermute | solution.py:587
  106.8 4.7 %collective-permute-start.7 = (f32[24,128]{1,0:T(8,128)S(1)}, f32[24,128]{1,0:T(8,128)S(1)}, u32[]{:S(2)}, u32[]{:S(2)}) collective-permute-start(f32[24,128]{1,0:T(8,128)S(1)} %get-tuple-element.24), channel_id=1, source_target_pairs={{0,255},{1,0},{2,1},{3,2},{4,3},{5,4},{6,5},{7,6},{8,7},{9,8},{10,... | collective-permute-start | bytes 36872 | tf_op jit(solution)/shard_map/pushes_out/ppermute | solution.py:587
  109.4 4.6 %collective-permute-start.8 = (f32[24,128]{1,0:T(8,128)S(1)}, f32[24,128]{1,0:T(8,128)S(1)}, u32[]{:S(2)}, u32[]{:S(2)}) collective-permute-start(f32[24,128]{1,0:T(8,128)S(1)} %get-tuple-element.26), channel_id=1, source_target_pairs={{0,1},{1,2},{2,3},{3,4},{4,5},{5,6},{6,7},{7,8},{8,9},{9,10},{10,1... | collective-permute-start | bytes 36872 | tf_op jit(solution)/shard_map/pushes_out/ppermute | solution.py:587
  109.8 4.2 %collective-permute-start.9 = (f32[24,128]{1,0:T(8,128)S(1)}, f32[24,128]{1,0:T(8,128)S(1)}, u32[]{:S(2)}, u32[]{:S(2)}) collective-permute-start(f32[24,128]{1,0:T(8,128)S(1)} %get-tuple-element.27), channel_id=1, source_target_pairs={{0,2},{1,3},{2,4},{3,5},{4,6},{5,7},{6,8},{7,9},{8,10},{9,11},{10,... | collective-permute-start | bytes 36872 | tf_op jit(solution)/shard_map/pushes_out/ppermute | solution.py:587
  111.2 8.0 %collective-permute-start.10 = (f32[24,128]{1,0:T(8,128)S(1)}, f32[24,128]{1,0:T(8,128)S(1)}, u32[]{:S(2)}, u32[]{:S(2)}) collective-permute-start(f32[24,128]{1,0:T(8,128)S(1)} %get-tuple-element.28), channel_id=1, source_target_pairs={{0,3},{1,4},{2,5},{3,6},{4,7},{5,8},{6,9},{7,10},{8,11},{9,12},{10... | collective-permute-start | bytes 36872 | tf_op jit(solution)/shard_map/pushes_out/ppermute | solution.py:587

commit v5 on v4

--- a/solution.py
+++ b/solution.py
@@ -112,12 +112,12 @@
 
 
 def pack_kernel(
-    count_ref, base_at, frac_at, charge_at, owner_at, near_at,
-    out_ref, base_ref, frac_ref, charge_ref, owner_ref, near_ref, sems,
+    count_at, base_at, frac_at, charge_at, owner_at, near_at,
+    out_ref, count_ref, base_ref, frac_ref, charge_ref, owner_ref, near_ref, sems,
 ):
     arrays = (
         (base_at, base_ref), (frac_at, frac_ref), (charge_at, charge_ref),
-        (owner_at, owner_ref), (near_at, near_ref),
+        (owner_at, owner_ref), (near_at, near_ref), (count_at, count_ref),
     )
     copies = [pltpu.make_async_copy(a, b, sems.at[n]) for n, (a, b) in enumerate(arrays)]
     for copy in copies:
@@ -132,7 +132,7 @@
             out_ref[8 + 4 * c + k : 9 + 4 * c + k, :] = frac_ref[c : c + 1, lanes]
         slot = lax.broadcasted_iota(jnp.int32, (1, 128), 1) + 128 * k
         out_ref[20 + k : 21 + k, :] = jnp.where(
-            slot < count_ref[0], charge_ref[k : k + 1, :], 0.0
+            slot < count_ref[...], charge_ref[k : k + 1, :], 0.0
         )
     owner = owner_ref[...]
     near = near_ref[...]
@@ -595,7 +595,7 @@
         payload = call(
             pack_kernel,
             (
-                atom_count,
+                atom_count.reshape(1, 1),
                 base_index,
                 fraction,
                 charge.reshape(4, 128),
@@ -604,14 +604,15 @@
             ),
             shape(56, 128),
             (
+                pltpu.VMEM((1, 1), jnp.int32),
                 pltpu.VMEM((3, 512), jnp.int32),
                 pltpu.VMEM((3, 512), F32),
                 pltpu.VMEM((4, 128), F32),
                 pltpu.VMEM((1, 128), jnp.int32),
                 pltpu.VMEM((NEIGH, 128), jnp.int32),
-                pltpu.SemaphoreType.DMA((5,)),
+                pltpu.SemaphoreType.DMA((6,)),
             ),
-            spaces={0: SM, 1: HB, 2: HB, 3: HB, 4: HB, 5: HB},
+            spaces={n: HB for n in range(6)},
             limit=59,
         )
     with jax.named_scope("particles_in"):

time: 121 us -> 121 us (level)
  no operation moved by 1% of the time
where the time goes in v5:
time: 121 us
  Pallas kernels  37.8 us (31%)
  starting transfers between devices  34.5 us (29%)
  waiting for transfers between devices  33 us (27%)
  blocking collectives  13.7 us (11%)
  between operations  1.59 us (1%)
    pallas_call x8, Pallas kernels, call(): pl.pallas_call(kernel, out_shape=outs, in_specs=[spaces.get(n, VM) for n...  37.8 us
    ppermute x3, starting transfers between devices, body(): far = [lax.ppermute(pair, both, chip_steps(kind)) for kind in range(3)]  9.76 us
    ppermute x1, waiting for transfers between devices, body(): taken = lax.ppermute(given, 'grp', [(0, 1), (1, 0)])  9.32 us
    ppermute x7, starting transfers between devices, from_device(): return lax.ppermute(value, both, pairs)  9.13 us
    all_gather x1, blocking collectives, body(): lax.all_gather(jnp.concatenate(far, axis=0), 'core').reshape(12, 56, 128)  8.77 us
    ppermute x7, waiting for transfers between devices, from_device(): return lax.ppermute(value, both, pairs)  7.68 us
    all_to_all x1, waiting for transfers between devices, body(): lax.all_to_all(columns.reshape(256, 8, 128), both, 0, 0, tiled=True)  7.32 us
    all_to_all x1, starting transfers between devices, body(): rows = lax.all_to_all(rows.reshape(256, 8, 128), both, 0, 0, tiled=True)  7.18 us
  transfers between devices with their start and end apart: 13, of which 6 were waited for; matrix products, arithmetic and copies ran while one was open for 0% of the time, Pallas kernels for 12%

profile of v5, /device:TPU:1, one launch (start us, length us, event | category | flops | bytes accessed | tf_op | source)
XLA Modules:
  0.0 120.7 jit_solution(15257664430351183837)
XLA Ops:
  0.6 0.0 copy-start.10
  0.6 0.0 copy-start
  1.4 1.6 %pack.1.own_ref = f32[56,128]{1,0:T(8,128)} custom-call(s32[1,1]{1,0:T(1,128)} %bitcast.14.count_at, s32[3,512]{1,0:T(4,128)} %base_at.1, f32[3,512]{1,0:T(4,128)} %frac_at.1, f32[4,128]{1,0:T(4,128)} %bitcast.26, s32[1,128]{1,0:T(1,128)} %bitcast.27, s32[32,128]{1,0:T(8,128)} %near_at.1), custom_call_target="tpu_custom_call" | custom-call | bytes 4194304 | tf_op jit(solution)/shard_map/pack/pallas_call | solution.py:552
  3.0 5.0 %all-gather = f32[112,128]{1,0:T(8,128)S(1)} all-gather(f32[56,128]{1,0:T(8,128)} %pack.1.own_ref), channel_id=2, replica_groups=mesh['row'=64,'core'=2,'grp'=2] {'core'}, dimensions={0}, use_global_device_ids=true | all-gather | bytes 86016 | tf_op jit(solution)/shard_map/particles_in/all_gather | solution.py:619
  8.0 0.0 copy-start.12
  8.0 0.7 collective-permute-start.2
  8.6 7.3 %collective-permute-start.1 = (f32[2,56,128]{2,1,0:T(8,128)S(1)}, f32[2,56,128]{2,1,0:T(8,128)S(1)}, u32[]{:S(2)}, u32[]{:S(2)}) collective-permute-start(f32[2,56,128]{2,1,0:T(8,128)S(1)} %bitcast.23), channel_id=1, source_target_pairs={{252,0},{6,2},{253,1},{7,3},{0,4},{10,6},{1,5},{11,7},{4,8},{14,10... | collective-permute-start | bytes 172040 | tf_op jit(solution)/shard_map/particles_in/ppermute | solution.py:620
  15.9 1.8 %collective-permute-start = (f32[2,56,128]{2,1,0:T(8,128)S(1)}, f32[2,56,128]{2,1,0:T(8,128)S(1)}, u32[]{:S(2)}, u32[]{:S(2)}) collective-permute-start(f32[2,56,128]{2,1,0:T(8,128)S(1)} %bitcast.24), channel_id=1, source_target_pairs={{253,0},{3,2},{0,1},{6,3},{1,4},{7,6},{4,5},{10,7},{5,8},{11,10},{... | collective-permute-start | bytes 172040 | tf_op jit(solution)/shard_map/particles_in/ppermute | solution.py:620
  17.8 0.0 collective-permute-done.2
  17.8 0.0 collective-permute-done.1
  17.8 2.7 %collective-permute-done = f32[2,56,128]{2,1,0:T(8,128)S(1)} collective-permute-done((f32[2,56,128]{2,1,0:T(8,128)S(1)}, f32[2,56,128]{2,1,0:T(8,128)S(1)}, u32[]{:S(2)}, u32[]{:S(2)}) %collective-permute-start) | collective-permute-done | bytes 57376 | tf_op jit(solution)/shard_map/particles_in/ppermute | solution.py:620
  20.5 8.8 %all-gather.1.far_ref = f32[12,56,128]{2,1,0:T(8,128)} all-gather(f32[6,56,128]{2,1,0:T(8,128)S(1)} %pad_maximum_fusion), channel_id=3, replica_groups=mesh['row'=64,'core'=2,'grp'=2] {'core'}, dimensions={0}, use_global_device_ids=true | all-gather | bytes 516096 | tf_op jit(solution)/shard_map/particles_in/all_gather | solution.py:621
  29.3 0.0 copy-done.12
  29.3 8.1 %spread.1 = (bf16[64,2,16,128]{3,2,1,0:T(8,128)(2,1)}, f32[6,24,128]{2,1,0:T(8,128)}, f32[240,384]{1,0:T(8,128)}, f32[240,384]{1,0:T(8,128)}, f32[3,384]{1,0:T(4...) custom-call(s32[1]{0:T(128)} %bitcast.place_ref.group_ref, f32[12,56,128]{2,1,0:T(8,128)} %all-gather.1.far_ref, ...), custom_call_target="tpu_custom_call" | custom-call | flops 4000000000 | bytes 4194304 | tf_op jit(solution)/shard_map/spread/pallas_call | solution.py:552
  37.4 5.4 %all-to-all-start = ((bf16[256,8,128]{2,1,0:T(8,128)(2,1)}), bf16[256,8,128]{2,1,0:T(8,128)(2,1)S(1)}, u32[]{:S(2)}, u32[]{:S(2)}) async-start(bf16[256,8,128]{2,1,0:T(8,128)(2,1)} %bitcast.21), calls=%async_computation | async-start | bytes 1048576 | tf_op jit(solution)/shard_map/to_columns/all_to_all | solution.py:679
  42.8 3.0 %collective-permute-start.3 = (bf16[128,4,256]{2,1,0:T(4,128)(2,1)}, bf16[128,4,256]{2,1,0:T(4,128)(2,1)S(1)}, u32[]{:S(2)}, u32[]{:S(2)}) collective-permute-start(bf16[128,4,256]{2,1,0:T(4,128)(2,1)} %get-tuple-element.19), channel_id=1, source_target_pairs={{0,1},{1,0},{2,3},{3,2},{4,5},{5,4},{6,7},{7,6},{8,9},{9,8},{10,11... | collective-permute-start | bytes 786440 | tf_op jit(solution)/shard_map/influence_swap/ppermute | solution.py:677
  45.8 9.3 %collective-permute-done.3 = bf16[128,4,256]{2,1,0:T(4,128)(2,1)S(1)} collective-permute-done((bf16[128,4,256]{2,1,0:T(4,128)(2,1)}, bf16[128,4,256]{2,1,0:T(4,128)(2,1)S(1)}, u32[]{:S(2)}, u32[]{:S(2)}) %collective-permute-start.3) | collective-permute-done | bytes 262176 | tf_op jit(solution)/shard_map/influence_swap/ppermute | solution.py:677
  55.1 0.1 convert_element_type.3.taken_ref
  55.2 0.0 copy-done
  55.2 0.7 influence.1.infl_ref
  55.9 7.3 %all-to-all-done = bf16[256,8,128]{2,1,0:T(8,128)(2,1)S(1)} async-done(((bf16[256,8,128]{2,1,0:T(8,128)(2,1)}), bf16[256,8,128]{2,1,0:T(8,128)(2,1)S(1)}, u32[]{:S(2)}, u32[]{:S(2)}) %all-to-all-start) | async-done | bytes 524320 | tf_op jit(solution)/shard_map/to_columns/all_to_all | solution.py:679
  63.2 0.0 copy-done.10
  63.2 2.8 %depth.1 = bf16[128,16,128]{2,1,0:T(8,128)(2,1)} custom-call(bf16[128,16,128]{2,1,0:T(8,128)(2,1)S(1)} %bitcast.15, f32[256,1024]{1,0:T(8,128)S(1)} %influence.1.infl_ref, bf16[4,256,256]{2,1,0:T(8,128)(2,1)S(1)} %copy-done.10), custom_call_target="tpu_custom_call" | custom-call | flops 800000000 | bytes 4194304 | tf_op jit(solution)/shard_map/depth/pallas_call | solution.py:552
  66.0 7.2 %all-to-all-start.1 = ((bf16[256,8,128]{2,1,0:T(8,128)(2,1)}), bf16[256,8,128]{2,1,0:T(8,128)(2,1)S(1)}, u32[]{:S(2)}, u32[]{:S(2)}) async-start(bf16[256,8,128]{2,1,0:T(8,128)(2,1)} %bitcast.12), calls=%async_computation.1 | async-start | bytes 1048576 | tf_op jit(solution)/shard_map/to_planes/all_to_all | solution.py:717
  73.2 0.0 copy-start.9
  73.2 0.0 copy-start.11
  73.2 6.4 %lookup_x.1.wx_at = bf16[22,512,256]{2,1,0:T(8,128)(2,1)} custom-call(f32[6,24,128]{2,1,0:T(8,128)} %get-tuple-element.20.refs_0_.part_ref), custom_call_target="tpu_custom_call" | custom-call | flops 4000000000 | bytes 4194304 | tf_op jit(solution)/shard_map/lookup_x/pallas_call | solution.py:552
  79.7 7.8 %lookup_y.1.wy_at = f32[22,512,256]{2,1,0:T(8,128)} custom-call(f32[6,24,128]{2,1,0:T(8,128)} %get-tuple-element.20.refs_0_.part_ref), custom_call_target="tpu_custom_call" | custom-call | flops 4000000000 | bytes 4194304 | tf_op jit(solution)/shard_map/lookup_y/pallas_call | solution.py:552
  87.4 0.0 copy-start.1
  87.4 0.0 copy-start.2
  87.4 0.0 copy-start.3
  87.4 0.0 copy-start.4
  87.4 0.0 copy-start.5
  87.4 0.0 copy-start.6
  87.5 0.0 copy-start.7
  87.5 0.0 copy-start.8
  87.5 6.0 %all-to-all-done.1 = bf16[256,8,128]{2,1,0:T(8,128)(2,1)S(1)} async-done(((bf16[256,8,128]{2,1,0:T(8,128)(2,1)}), bf16[256,8,128]{2,1,0:T(8,128)(2,1)S(1)}, u32[]{:S(2)}, u32[]{:S(2)}) %all-to-all-start.1) | async-done | bytes 524320 | tf_op jit(solution)/shard_map/to_planes/all_to_all | solution.py:717
  93.5 0.0 copy-done.9
  93.5 0.0 copy-done.11
  93.5 8.9 %probe.1 = (f32[1,512,512]{2,1,0:T(8,128)}, f32[24,128]{1,0:T(8,128)S(1)}, f32[24,128]{1,0:T(8,128)S(1)}, f32[24,128]{1,0:T(8,128)S(1)}, f32[24,128]{1,0:T(8,128...) custom-call(bf16[64,2,16,128]{3,2,1,0:T(8,128)(2,1)S(1)} %bitcast.16, ...), custom_call_target="tpu_custom_call" | custom-call | flops 5000000000 | bytes 4194304 | tf_op jit(solution)/shard_map/probe/pallas_call | solution.py:552
  102.4 1.7 %collective-permute-start.4 = (f32[24,128]{1,0:T(8,128)S(1)}, f32[24,128]{1,0:T(8,128)S(1)}, u32[]{:S(2)}, u32[]{:S(2)}) collective-permute-start(f32[24,128]{1,0:T(8,128)S(1)} %get-tuple-element.21), channel_id=1, source_target_pairs={{0,252},{1,253},{2,254},{3,255},{4,0},{5,1},{6,2},{7,3},{8,4},{9,5... | collective-permute-start | bytes 36872 | tf_op jit(solution)/shard_map/pushes_out/ppermute | solution.py:587
  104.1 1.8 %collective-permute-start.5 = (f32[24,128]{1,0:T(8,128)S(1)}, f32[24,128]{1,0:T(8,128)S(1)}, u32[]{:S(2)}, u32[]{:S(2)}) collective-permute-start(f32[24,128]{1,0:T(8,128)S(1)} %get-tuple-element.22), channel_id=1, source_target_pairs={{0,253},{1,254},{2,255},{3,0},{4,1},{5,2},{6,3},{7,4},{8,5},{9,6},... | collective-permute-start | bytes 36872 | tf_op jit(solution)/shard_map/pushes_out/ppermute | solution.py:587
  105.9 0.9 collective-permute-start.6
  106.8 2.6 %collective-permute-start.7 = (f32[24,128]{1,0:T(8,128)S(1)}, f32[24,128]{1,0:T(8,128)S(1)}, u32[]{:S(2)}, u32[]{:S(2)}) collective-permute-start(f32[24,128]{1,0:T(8,128)S(1)} %get-tuple-element.24), channel_id=1, source_target_pairs={{0,255},{1,0},{2,1},{3,2},{4,3},{5,4},{6,5},{7,6},{8,7},{9,8},{10,... | collective-permute-start | bytes 36872 | tf_op jit(solution)/shard_map/pushes_out/ppermute | solution.py:587
  109.4 0.4 collective-permute-start.8
  109.8 0.0 collective-permute-done.4.s0
  109.8 1.4 %collective-permute-start.9 = (f32[24,128]{1,0:T(8,128)S(1)}, f32[24,128]{1,0:T(8,128)S(1)}, u32[]{:S(2)}, u32[]{:S(2)}) collective-permute-start(f32[24,128]{1,0:T(8,128)S(1)} %get-tuple-element.27), channel_id=1, source_target_pairs={{0,2},{1,3},{2,4},{3,5},{4,6},{5,7},{6,8},{7,9},{8,10},{9,11},{10,... | collective-permute-start | bytes 36872 | tf_op jit(solution)/shard_map/pushes_out/ppermute | solution.py:587
  111.2 0.0 collective-permute-done.5.s1
  111.2 0.3 collective-permute-start.10
  111.5 0.0 collective-permute-done.6.s2
  111.5 0.0 collective-permute-done.7.s3
  111.5 2.5 %collective-permute-done.8.s5 = f32[24,128]{1,0:T(8,128)S(1)} collective-permute-done((f32[24,128]{1,0:T(8,128)S(1)}, f32[24,128]{1,0:T(8,128)S(1)}, u32[]{:S(2)}, u32[]{:S(2)}) %collective-permute-start.8) | collective-permute-done | bytes 12320 | tf_op jit(solution)/shard_map/pushes_out/ppermute | solution.py:587
  114.0 0.0 collective-permute-done.9.s6
  114.0 5.2 %collective-permute-done.10.s7 = f32[24,128]{1,0:T(8,128)S(1)} collective-permute-done((f32[24,128]{1,0:T(8,128)S(1)}, f32[24,128]{1,0:T(8,128)S(1)}, u32[]{:S(2)}, u32[]{:S(2)}) %collective-permute-start.10) | collective-permute-done | bytes 12320 | tf_op jit(solution)/shard_map/pushes_out/ppermute | solution.py:587
  119.2 0.0 copy-done.1
  119.2 0.0 copy-done.2
  119.2 0.0 copy-done.3
  119.2 0.0 copy-done.4
  119.2 0.0 copy-done.5
  119.2 0.0 copy-done.6
  119.2 0.0 copy-done.7
  119.2 0.0 copy-done.8
  119.2 1.5 %force.1 = f32[3,512]{1,0:T(4,128)} custom-call(f32[24,128]{1,0:T(8,128)S(1)} %collective-permute-done.4.s0, f32[24,128]{1,0:T(8,128)S(1)} %collective-permute-done.5.s1, f32[24,128]{1,0:T(8,128)S(1)} %collective-permute-done.6.s2, f32[24,128]{1,0:T(8,128)S(1)} %collective-permute-done.7.s3, f32[24,128]{1,0:T(8,128)S(1)} %get-tuple-element.25.s4, ...), custom_call_target="tpu_custom_call" | custom-call | bytes 4194304 | tf_op jit(solution)/shard_map/force/pallas_call | solution.py:552
  (1 shorter events, 0.0 us)
Async XLA Ops:
  0.6 62.6 %copy-start.10 = (bf16[4,256,256]{2,1,0:T(8,128)(2,1)S(1)}, bf16[4,256,256]{2,1,0:T(8,128)(2,1)}, u32[]{:S(2)}) copy-start(bf16[4,256,256]{2,1,0:T(8,128)(2,1)} %constant.23.clone.table_ref) | copy-start | bytes 1572868
  0.6 54.6 %copy-start = (f32[128,4,512]{2,1,0:T(4,128)S(1)}, f32[128,4,512]{2,1,0:T(4,128)}, u32[]{:S(2)}) copy-start(f32[128,4,512]{2,1,0:T(4,128)} %kept_ref.1) | copy-start | bytes 3145732
  8.0 21.3 %copy-start.12 = (f32[112,128]{1,0:T(8,128)}, f32[112,128]{1,0:T(8,128)S(1)}, u32[]{:S(2)}) copy-start(f32[112,128]{1,0:T(8,128)S(1)} %all-gather) | copy-start | bytes 172036
  8.0 9.8 %collective-permute-start.2 = (f32[2,56,128]{2,1,0:T(8,128)S(1)}, f32[2,56,128]{2,1,0:T(8,128)S(1)}, u32[]{:S(2)}, u32[]{:S(2)}) collective-permute-start(f32[2,56,128]{2,1,0:T(8,128)S(1)} %bitcast.22), channel_id=1, source_target_pairs={{5,0},{252,1},{9,4},{0,5},{13,8},{4,9},{17,12},{8,13},{21,16},{12,... | collective-permute-start | bytes 172040 | tf_op jit(solution)/shard_map/particles_in/ppermute | solution.py:620
  8.6 9.1 %collective-permute-start.1 = (f32[2,56,128]{2,1,0:T(8,128)S(1)}, f32[2,56,128]{2,1,0:T(8,128)S(1)}, u32[]{:S(2)}, u32[]{:S(2)}) collective-permute-start(f32[2,56,128]{2,1,0:T(8,128)S(1)} %bitcast.23), channel_id=1, source_target_pairs={{252,0},{6,2},{253,1},{7,3},{0,4},{10,6},{1,5},{11,7},{4,8},{14,10... | collective-permute-start | bytes 172040 | tf_op jit(solution)/shard_map/particles_in/ppermute | solution.py:620
  15.9 4.5 %collective-permute-start = (f32[2,56,128]{2,1,0:T(8,128)S(1)}, f32[2,56,128]{2,1,0:T(8,128)S(1)}, u32[]{:S(2)}, u32[]{:S(2)}) collective-permute-start(f32[2,56,128]{2,1,0:T(8,128)S(1)} %bitcast.24), channel_id=1, source_target_pairs={{253,0},{3,2},{0,1},{6,3},{1,4},{7,6},{4,5},{10,7},{5,8},{11,10},{... | collective-permute-start | bytes 172040 | tf_op jit(solution)/shard_map/particles_in/ppermute | solution.py:620
  37.4 25.8 %all-to-all-start = ((bf16[256,8,128]{2,1,0:T(8,128)(2,1)}), bf16[256,8,128]{2,1,0:T(8,128)(2,1)S(1)}, u32[]{:S(2)}, u32[]{:S(2)}) async-start(bf16[256,8,128]{2,1,0:T(8,128)(2,1)} %bitcast.21), calls=%async_computation | async-start | bytes 1048576 | tf_op jit(solution)/shard_map/to_columns/all_to_all | solution.py:679
  42.8 12.3 %collective-permute-start.3 = (bf16[128,4,256]{2,1,0:T(4,128)(2,1)}, bf16[128,4,256]{2,1,0:T(4,128)(2,1)S(1)}, u32[]{:S(2)}, u32[]{:S(2)}) collective-permute-start(bf16[128,4,256]{2,1,0:T(4,128)(2,1)} %get-tuple-element.19), channel_id=1, source_target_pairs={{0,1},{1,0},{2,3},{3,2},{4,5},{5,4},{6,7},{7,6},{8,9},{9,8},{10,11... | collective-permute-start | bytes 786440 | tf_op jit(solution)/shard_map/influence_swap/ppermute | solution.py:677
  66.0 27.4 %all-to-all-start.1 = ((bf16[256,8,128]{2,1,0:T(8,128)(2,1)}), bf16[256,8,128]{2,1,0:T(8,128)(2,1)S(1)}, u32[]{:S(2)}, u32[]{:S(2)}) async-start(bf16[256,8,128]{2,1,0:T(8,128)(2,1)} %bitcast.12), calls=%async_computation.1 | async-start | bytes 1048576 | tf_op jit(solution)/shard_map/to_planes/all_to_all | solution.py:717
  73.2 20.2 %copy-start.9 = (bf16[512,512]{1,0:T(8,128)(2,1)S(1)}, bf16[512,512]{1,0:T(8,128)(2,1)}, u32[]{:S(2)}) copy-start(bf16[512,512]{1,0:T(8,128)(2,1)} %constant.22.clone.table_at) | copy-start | bytes 1572868
  73.2 20.2 %copy-start.11 = (f32[6,24,128]{2,1,0:T(8,128)S(1)}, f32[6,24,128]{2,1,0:T(8,128)}, u32[]{:S(2)}) copy-start(f32[6,24,128]{2,1,0:T(8,128)} %get-tuple-element.20.refs_0_.part_ref) | copy-start | bytes 221188
  87.4 31.8 %copy-start.1 = (f32[240,384]{1,0:T(8,128)S(1)}, f32[240,384]{1,0:T(8,128)}, u32[]{:S(2)}) copy-start(f32[240,384]{1,0:T(8,128)} %get-tuple-element.30.h1_ref) | copy-start | bytes 1105924
  87.4 31.8 %copy-start.2 = (f32[240,384]{1,0:T(8,128)S(1)}, f32[240,384]{1,0:T(8,128)}, u32[]{:S(2)}) copy-start(f32[240,384]{1,0:T(8,128)} %get-tuple-element.31.t2_ref) | copy-start | bytes 1105924
  87.4 31.8 %copy-start.3 = (f32[56,128]{1,0:T(8,128)S(1)}, f32[56,128]{1,0:T(8,128)}, u32[]{:S(2)}) copy-start(f32[56,128]{1,0:T(8,128)} %pack.1.own_ref) | copy-start | bytes 86020
  87.4 31.8 %copy-start.4 = (bf16[240,240]{1,0:T(8,128)(2,1)S(1)}, bf16[240,240]{1,0:T(8,128)(2,1)}, u32[]{:S(2)}) copy-start(bf16[240,240]{1,0:T(8,128)(2,1)} %w2_ref.1) | copy-start | bytes 345604
  87.4 31.8 %copy-start.5 = (bf16[128,240]{0,1:T(8,128)(2,1)S(1)}, bf16[128,240]{0,1:T(8,128)(2,1)}, u32[]{:S(2)}) copy-start(bf16[128,240]{0,1:T(8,128)(2,1)} %param.22) | copy-start | bytes 184324
  87.4 31.8 %copy-start.6 = (f32[2,56,128]{2,1,0:T(8,128)S(1)}, f32[2,56,128]{2,1,0:T(8,128)}, u32[]{:S(2)}) copy-start(f32[2,56,128]{2,1,0:T(8,128)} %get-tuple-element.29.beside_ref) | copy-start | bytes 172036
  87.5 31.8 %copy-start.7 = (f32[3,384]{1,0:T(4,128)S(1)}, f32[3,384]{1,0:T(4,128)}, u32[]{:S(2)}) copy-start(f32[3,384]{1,0:T(4,128)} %get-tuple-element.32.to_ref) | copy-start | bytes 13828
  87.5 31.8 %copy-start.8 = (bf16[240,3]{0,1:T(4,128)(2,1)S(1)}, bf16[240,3]{0,1:T(4,128)(2,1)}, u32[]{:S(2)}) copy-start(bf16[240,3]{0,1:T(4,128)(2,1)} %param.26) | copy-start | bytes 4324
  102.4 7.4 %collective-permute-start.4 = (f32[24,128]{1,0:T(8,128)S(1)}, f32[24,128]{1,0:T(8,128)S(1)}, u32[]{:S(2)}, u32[]{:S(2)}) collective-permute-start(f32[24,128]{1,0:T(8,128)S(1)} %get-tuple-element.21), channel_id=1, source_target_pairs={{0,252},{1,253},{2,254},{3,255},{4,0},{5,1},{6,2},{7,3},{8,4},{9,5... | collective-permute-start | bytes 36872 | tf_op jit(solution)/shard_map/pushes_out/ppermute | solution.py:587
  104.1 7.1 %collective-permute-start.5 = (f32[24,128]{1,0:T(8,128)S(1)}, f32[24,128]{1,0:T(8,128)S(1)}, u32[]{:S(2)}, u32[]{:S(2)}) collective-permute-start(f32[24,128]{1,0:T(8,128)S(1)} %get-tuple-element.22), channel_id=1, source_target_pairs={{0,253},{1,254},{2,255},{3,0},{4,1},{5,2},{6,3},{7,4},{8,5},{9,6},... | collective-permute-start | bytes 36872 | tf_op jit(solution)/shard_map/pushes_out/ppermute | solution.py:587
  105.9 5.6 %collective-permute-start.6 = (f32[24,128]{1,0:T(8,128)S(1)}, f32[24,128]{1,0:T(8,128)S(1)}, u32[]{:S(2)}, u32[]{:S(2)}) collective-permute-start(f32[24,128]{1,0:T(8,128)S(1)} %get-tuple-element.23), channel_id=1, source_target_pairs={{0,254},{1,255},{2,0},{3,1},{4,2},{5,3},{6,4},{7,5},{8,6},{9,7},{1... | collective-permute-start | bytes 36872 | tf_op jit(solution)/shard_map/pushes_out/ppermute | solution.py:587
  106.8 4.7 %collective-permute-start.7 = (f32[24,128]{1,0:T(8,128)S(1)}, f32[24,128]{1,0:T(8,128)S(1)}, u32[]{:S(2)}, u32[]{:S(2)}) collective-permute-start(f32[24,128]{1,0:T(8,128)S(1)} %get-tuple-element.24), channel_id=1, source_target_pairs={{0,255},{1,0},{2,1},{3,2},{4,3},{5,4},{6,5},{7,6},{8,7},{9,8},{10,... | collective-permute-start | bytes 36872 | tf_op jit(solution)/shard_map/pushes_out/ppermute | solution.py:587
  109.4 4.6 %collective-permute-start.8 = (f32[24,128]{1,0:T(8,128)S(1)}, f32[24,128]{1,0:T(8,128)S(1)}, u32[]{:S(2)}, u32[]{:S(2)}) collective-permute-start(f32[24,128]{1,0:T(8,128)S(1)} %get-tuple-element.26), channel_id=1, source_target_pairs={{0,1},{1,2},{2,3},{3,4},{4,5},{5,6},{6,7},{7,8},{8,9},{9,10},{10,1... | collective-permute-start | bytes 36872 | tf_op jit(solution)/shard_map/pushes_out/ppermute | solution.py:587
  109.8 4.2 %collective-permute-start.9 = (f32[24,128]{1,0:T(8,128)S(1)}, f32[24,128]{1,0:T(8,128)S(1)}, u32[]{:S(2)}, u32[]{:S(2)}) collective-permute-start(f32[24,128]{1,0:T(8,128)S(1)} %get-tuple-element.27), channel_id=1, source_target_pairs={{0,2},{1,3},{2,4},{3,5},{4,6},{5,7},{6,8},{7,9},{8,10},{9,11},{10,... | collective-permute-start | bytes 36872 | tf_op jit(solution)/shard_map/pushes_out/ppermute | solution.py:587
  111.2 8.0 %collective-permute-start.10 = (f32[24,128]{1,0:T(8,128)S(1)}, f32[24,128]{1,0:T(8,128)S(1)}, u32[]{:S(2)}, u32[]{:S(2)}) collective-permute-start(f32[24,128]{1,0:T(8,128)S(1)} %get-tuple-element.28), channel_id=1, source_target_pairs={{0,3},{1,4},{2,5},{3,6},{4,7},{5,8},{6,9},{7,10},{8,11},{9,12},{10... | collective-permute-start | bytes 36872 | tf_op jit(solution)/shard_map/pushes_out/ppermute | solution.py:587
